TPU v7x, 32 devices: a whole 2x2x4 slice. The times are simulated.
32 devices in a mesh: member: 2 (over x), gx: 16 (over z, y, core).
Axes of the slice: x: 2, y: 2, z: 4, core: 2. Of those that a mesh axis runs over, the one named last changes fastest.
Arguments:
- edge_tiles: bfloat16 [128, 832, 832], P('member', 'gx'), parts along dimension 0, may hold values from -0.036771775 to 0.036771775
- trial_panel: float32 [64, 48, 832], P(('member', 'gx')), parts along dimension 0, may hold values from -6 to 6
- col_blocks: int32 [32, 2], replicated, may hold values from 0 to 31, as said below
Outputs:
- filtered_low: float32 [64, 48, 832], P(('member', 'gx')), parts along dimension 0
- filtered_high: float32 [64, 48, 832], P(('member', 'gx')), parts along dimension 0
There are 2 independent parts, one for each index of `member`. A program takes and returns all parts, laid end to end along the dimension named above; an argument that names none is the same for every part. Nothing has to cross between parts.
Inputs may be any that keep to these rules, and one draw needn't show every extreme that they name: Row block b lies in domain b // 2; every col_blocks[b, s] lies in the same domain or in the next one, cyclically, the domain after the last being the first. When b is the first block of its domain, col_blocks[b, 0] lies in the next domain. Row block 30 couples to blocks 0 and 31. Entries may repeat.
All inputs are finite; a program needn't handle non-finite values.
Results may differ from a plain program's by a relative error of at most 0.0034.
Values may be sent and summed in bfloat16 or wider, within the bound.
No kernel may reach another device: no remote copies, remote signals or barrier semaphores. Data moves between devices by JAX's collectives and lax.ppermute only.
A program may use at most 64 MiB of HBM per device.

v0:
```python
import jax
import jax.numpy as jnp
from jax import lax
from jax.sharding import PartitionSpec as P

DEGREE = 4


def passed_along(value, axis, steps):
    count = lax.axis_size(axis)
    pairs = [(source, (source + steps) % count) for source in range(count)]
    return lax.ppermute(value, axis, pairs)


def per_device(edge_tiles, trial_panel, col_blocks):
    blk_dev, vec_count, orb_count = trial_panel.shape
    slot_count = col_blocks.shape[1]
    group = lax.axis_size("gx")
    block_total = blk_dev * group
    domain = lax.axis_index("gx")
    own_cols = lax.dynamic_slice_in_dim(col_blocks, domain * blk_dev, blk_dev, 0).reshape(-1)
    target = jnp.mod(own_cols - domain * blk_dev, block_total)
    start_bf = trial_panel.astype(jnp.bfloat16)
    laid_out = edge_tiles.reshape(block_total, slot_count, orb_count // group, orb_count)
    arrived = lax.all_to_all(laid_out, "gx", split_axis=0, concat_axis=2, tiled=True)
    turned = jnp.einsum("bkm,bsmn->bskn", start_bf, arrived, preferred_element_type=jnp.float32)
    first_turn = turned

    def direct_terms(source_rows):
        picked = jnp.take(source_rows, target, axis=0).reshape(
            blk_dev, slot_count, vec_count, orb_count
        )
        return jnp.einsum("bskn,bsmn->bkm", picked, arrived, preferred_element_type=jnp.float32)

    def scatter_terms(selector, turned):
        return jnp.einsum(
            "ec,ekn->ckn",
            selector,
            turned.reshape(-1, vec_count, orb_count),
            precision=lax.Precision.HIGHEST,
        )

    pair_select = (target[:, None] == jnp.arange(2 * blk_dev)[None, :]).astype(jnp.float32)

    def operate(rounded, turned):
        following = passed_along(rounded, "gx", -1)
        direct = direct_terms(jnp.concatenate([rounded, following], 0))
        spread = scatter_terms(pair_select, turned)
        arrive = passed_along(spread[blk_dev:], "gx", 1)
        return direct + spread[:blk_dev] + arrive

    previous = trial_panel
    current = operate(start_bf, first_turn)
    for degree_k in range(DEGREE - 1):
        rounded = current.astype(jnp.bfloat16)
        following_panel = (
            2.0
            * operate(
                rounded,
                jnp.einsum("bkm,bsmn->bskn", rounded, arrived, preferred_element_type=jnp.float32),
            )
            - previous
        )
        previous, current = (current, following_panel)
    return (previous, current)


def solution(mesh):
    return jax.shard_map(
        per_device,
        mesh=mesh,
        in_specs=(P("member", "gx", None), P(("member", "gx"), None, None), P()),
        out_specs=(P(("member", "gx"), None, None), P(("member", "gx"), None, None)),
        check_vma=False,
    )
```

profile of v0, /device:TPU:0, one launch (start us, length us, event | category | flops | bytes accessed | tf_op | source)
XLA Modules:
  0.0 236.0 jit_solution(2648077602503263297)
XLA Ops:
  0.6 12.6 %reshape.56 = bf16[32,2,52,832]{3,1,0,2:T(2,128)(2,1)} reshape(bf16[64,52,832]{2,0,1:T(8,128)(2,1)} %param.5) | data formatting | bytes 11075584 | tf_op jit(solution)/shard_map/reshape | solution.py:24
  13.2 6.7 %copy.19 = bf16[32,2,52,832]{3,1,2,0:T(2,128)(2,1)} copy(bf16[32,2,52,832]{3,1,0,2:T(2,128)(2,1)} %reshape.56) | data formatting | bytes 11075584 | tf_op jit(solution)/shard_map/reshape | solution.py:24
  19.9 7.6 %all-to-all-start = ((bf16[32,2,52,832]{3,1,2,0:T(2,128)(2,1)}), bf16[32,2,52,832]{3,1,2,0:T(2,128)(2,1)}, u32[]{:S(2)}, u32[]{:S(2)}) async-start(bf16[32,2,52,832]{3,1,2,0:T(2,128)(2,1)} %copy.19), calls=%async_computation | async-start | bytes 11927552 | tf_op jit(solution)/shard_map/all_to_all | solution.py:25
  27.6 4.4 %collective-permute-start = (bf16[2,48,832]{2,1,0:T(8,128)(2,1)S(1)}, bf16[2,48,832]{2,1,0:T(8,128)(2,1)S(1)}, u32[]{:S(2)}, u32[]{:S(2)}) collective-permute-start(bf16[2,48,832]{2,1,0:T(8,128)(2,1)S(1)} %convert_element_type.13), channel_id=1, source_target_pairs={{0,15},{1,0},{2,1},{3,2},{4,3},{5,4},{6,5},{7,6},{8,7},{9,8},{10,9... | collective-permute-start | bytes 479240 | tf_op jit(solution)/shard_map/ppermute | solution.py:12
  32.2 103.8 %all-to-all-done = bf16[32,2,52,832]{3,1,2,0:T(2,128)(2,1)} async-done(((bf16[32,2,52,832]{3,1,2,0:T(2,128)(2,1)}), bf16[32,2,52,832]{3,1,2,0:T(2,128)(2,1)}, u32[]{:S(2)}, u32[]{:S(2)}) %all-to-all-start) | async-done | bytes 5537824 | tf_op jit(solution)/shard_map/all_to_all | solution.py:25
  136.1 5.7 %copy.20 = bf16[2,2,16,52,832]{4,1,3,2,0:T(2,128)(2,1)S(1)} copy(bf16[2,2,16,52,832]{4,1,3,0,2:T(2,128)(2,1)} %bitcast.2) | data formatting | bytes 11075584 | tf_op jit(solution)/shard_map/all_to_all | solution.py:25
  141.8 2.6 %copy-done = bf16[2,2,16,52,832]{4,1,3,2,0:T(2,128)(2,1)} copy-done((bf16[2,2,16,52,832]{4,1,3,2,0:T(2,128)(2,1)}, bf16[2,2,16,52,832]{4,1,3,2,0:T(2,128)(2,1)S(1)}, u32[]{:S(2)}) %copy-start) | copy-done | bytes 5537816
  144.4 1.2 fusion.23
  145.5 0.9 fusion.32
  146.8 0.8 collective-permute-start.1
  147.6 0.6 gather_fusion
  148.4 30.4 %collective-permute-done.1 = f32[2,48,832]{2,1,0:T(8,128)S(1)} collective-permute-done((f32[2,48,832]{2,1,0:T(8,128)S(1)}, f32[2,48,832]{2,1,0:T(8,128)S(1)}, u32[]{:S(2)}, u32[]{:S(2)}) %collective-permute-start.1) | collective-permute-done | bytes 319520 | tf_op jit(solution)/shard_map/ppermute | solution.py:12
  178.8 4.4 %fusion.48 = (bf16[2,48,832]{2,1,0:T(8,128)(2,1)S(1)}, f32[2,48,832]{2,1,0:T(8,128)S(1)}) fusion(f32[2,48,832]{2,1,0:T(8,128)S(1)} %collective-permute-done.1, f32[2,48,832]{2,0,1:T(2,128)S(1)} %get-tuple-element.11, bf16[2,2,48,832]{3,2,1,0:T(8,128)(2,1)S(1)} %bitcast.109, bf16[2,2,832,832]{3,1,2,0:T(2,128)(2,1)} %bitcast.93), kind=kOutput, calls=%fused_computation.68 | convolution fusion | flops 266053632 | bytes 6975488 | tf_op jit(solution)/shard_map/bskn,bsmn->bkm/dot_general | solution.py:33
  183.3 1.2 fusion.20
  184.5 0.9 fusion.30
  185.6 0.8 copy.52
  187.4 0.6 gather_fusion.1
  188.2 7.9 %collective-permute-done.3 = f32[2,48,832]{2,1,0:T(8,128)} collective-permute-done((f32[2,48,832]{2,1,0:T(8,128)}, f32[2,48,832]{2,1,0:T(8,128)}, u32[]{:S(2)}, u32[]{:S(2)}) %collective-permute-start.3) | collective-permute-done | bytes 319520 | tf_op jit(solution)/shard_map/ppermute | solution.py:12
  196.1 4.6 %fusion.49 = (bf16[2,48,832]{2,1,0:T(8,128)(2,1)S(1)}, f32[2,48,832]{2,1,0:T(8,128)S(1)}) fusion(f32[2,48,832]{2,1,0:T(8,128)S(1)} %copy-done.2, f32[2,48,832]{2,1,0:T(8,128)} %collective-permute-done.3, f32[2,48,832]{2,0,1:T(2,128)S(1)} %get-tuple-element.9, bf16[2,2,48,832]{3,2,1,0:T(8,128)(2,1)S(1)} %bitcast.110, bf16[2,2,832,832]{3,1,2,0:T(2,128)(2,1)} %bitcast.94), kind=kOutput, calls=%fused_computation.69 | convolution fusion | flops 266213376 | bytes 7294976 | tf_op jit(solution)/shard_map/bskn,bsmn->bkm/dot_general | solution.py:33
  200.7 1.2 fusion.17
  202.1 0.9 fusion.28
  203.3 0.8 copy.54
  205.1 0.6 gather_fusion.2
  205.8 7.9 %collective-permute-done.5 = f32[2,48,832]{2,1,0:T(8,128)} collective-permute-done((f32[2,48,832]{2,1,0:T(8,128)}, f32[2,48,832]{2,1,0:T(8,128)}, u32[]{:S(2)}, u32[]{:S(2)}) %collective-permute-start.5) | collective-permute-done | bytes 319520 | tf_op jit(solution)/shard_map/ppermute | solution.py:12
  213.7 5.3 %fusion.50 = (bf16[2,48,832]{2,1,0:T(8,128)(2,1)S(1)}, f32[2,48,832]{2,1,0:T(8,128)}) fusion(f32[2,48,832]{2,1,0:T(8,128)S(1)} %get-tuple-element.14, f32[2,48,832]{2,1,0:T(8,128)} %collective-permute-done.5, f32[2,48,832]{2,0,1:T(2,128)S(1)} %get-tuple-element.7, bf16[2,2,48,832]{3,2,1,0:T(8,128)(2,1)S(1)} %bitcast.108, bf16[2,2,832,832]{3,1,2,0:T(2,128)(2,1)} %bitcast.95), kind=kOutput, calls=%fused_computation.70 | convolution fusion | flops 266213376 | bytes 7294976 | tf_op jit(solution)/shard_map/bskn,bsmn->bkm/dot_general | solution.py:33
  219.1 1.2 fusion.14
  220.3 0.9 fusion.26
  221.5 0.6 collective-permute-start.7
  222.0 1.2 collective-permute-done.6
  223.2 0.6 gather_fusion.3
  224.0 6.9 %collective-permute-done.7 = f32[2,48,832]{2,1,0:T(8,128)S(1)} collective-permute-done((f32[2,48,832]{2,1,0:T(8,128)S(1)}, f32[2,48,832]{2,1,0:T(8,128)S(1)}, u32[]{:S(2)}, u32[]{:S(2)}) %collective-permute-start.7) | collective-permute-done | bytes 319520 | tf_op jit(solution)/shard_map/ppermute | solution.py:12
  230.9 5.2 %fusion.3 = f32[2,48,832]{2,1,0:T(8,128)} fusion(f32[2,48,832]{2,1,0:T(8,128)S(1)} %get-tuple-element.16, f32[2,48,832]{2,1,0:T(8,128)S(1)} %collective-permute-done.7, bf16[2,2,48,832]{3,2,1,0:T(8,128)(2,1)S(1)} %bitcast.111, bf16[2,2,832,832]{3,1,2,0:T(2,128)(2,1)} %bitcast.96, f32[2,48,832]{2,0,1:T(2,128)S(1)} %get-tuple-element.5), kind=kOutput, calls=%fused_computation.8 | convolution fusion | flops 266133504 | bytes 7135232 | tf_op jit(solution)/shard_map/bskn,bsmn->bkm/dot_general | solution.py:33
  (46 shorter events, 4.3 us)
Async XLA Ops:
  19.9 7.6 %copy-start.2 = (f32[2,48,832]{2,1,0:T(8,128)S(1)}, f32[2,48,832]{2,1,0:T(8,128)}, u32[]{:S(2)}) copy-start(f32[2,48,832]{2,1,0:T(8,128)} %param.6) | copy-start | bytes 958468
  19.9 12.0 %copy-start.3 = (s32[32,2]{0,1:T(2,128)S(1)}, s32[32,2]{0,1:T(2,128)}, u32[]{:S(2)}) copy-start(s32[32,2]{0,1:T(2,128)} %param.7) | copy-start | bytes 772
  19.9 116.1 %all-to-all-start = ((bf16[32,2,52,832]{3,1,2,0:T(2,128)(2,1)}), bf16[32,2,52,832]{3,1,2,0:T(2,128)(2,1)}, u32[]{:S(2)}, u32[]{:S(2)}) async-start(bf16[32,2,52,832]{3,1,2,0:T(2,128)(2,1)} %copy.19), calls=%async_computation | async-start | bytes 11927552 | tf_op jit(solution)/shard_map/all_to_all | solution.py:25
  27.6 120.0 %collective-permute-start = (bf16[2,48,832]{2,1,0:T(8,128)(2,1)S(1)}, bf16[2,48,832]{2,1,0:T(8,128)(2,1)S(1)}, u32[]{:S(2)}, u32[]{:S(2)}) collective-permute-start(bf16[2,48,832]{2,1,0:T(8,128)(2,1)S(1)} %convert_element_type.13), channel_id=1, source_target_pairs={{0,15},{1,0},{2,1},{3,2},{4,3},{5,4},{6,5},{7,6},{8,7},{9,8},{10,9... | collective-permute-start | bytes 479240 | tf_op jit(solution)/shard_map/ppermute | solution.py:12
  141.8 2.6 %copy-start = (bf16[2,2,16,52,832]{4,1,3,2,0:T(2,128)(2,1)}, bf16[2,2,16,52,832]{4,1,3,2,0:T(2,128)(2,1)S(1)}, u32[]{:S(2)}) copy-start(bf16[2,2,16,52,832]{4,1,3,2,0:T(2,128)(2,1)S(1)} %copy.20) | copy-start | bytes 16613380
  146.8 32.1 %collective-permute-start.1 = (f32[2,48,832]{2,1,0:T(8,128)S(1)}, f32[2,48,832]{2,1,0:T(8,128)S(1)}, u32[]{:S(2)}, u32[]{:S(2)}) collective-permute-start(f32[2,48,832]{2,1,0:T(8,128)S(1)} %copy.50), channel_id=1, source_target_pairs={{0,1},{1,2},{2,3},{3,4},{4,5},{5,6},{6,7},{7,8},{8,9},{9,10},{10,1... | collective-permute-start | bytes 958472 | tf_op jit(solution)/shard_map/ppermute | solution.py:12
  148.2 35.0 %copy-start.1 = (bf16[2,2,16,52,832]{4,1,3,2,0:T(2,128)(2,1)S(1)}, bf16[2,2,16,52,832]{4,1,3,2,0:T(2,128)(2,1)}, u32[]{:S(2)}) copy-start(bf16[2,2,16,52,832]{4,1,3,2,0:T(2,128)(2,1)} %copy-done) | copy-start | bytes 16613380
  184.4 2.9 %collective-permute-start.2 = (bf16[2,48,832]{2,1,0:T(8,128)(2,1)S(1)}, bf16[2,48,832]{2,1,0:T(8,128)(2,1)S(1)}, u32[]{:S(2)}, u32[]{:S(2)}) collective-permute-start(bf16[2,48,832]{2,1,0:T(8,128)(2,1)S(1)} %get-tuple-element.13), channel_id=1, source_target_pairs={{0,15},{1,0},{2,1},{3,2},{4,3},{5,4},{6,5},{7,6},{8,7},{9,8},{10,9... | collective-permute-start | bytes 479240 | tf_op jit(solution)/shard_map/ppermute | solution.py:12
  185.4 15.3 %slice-start = ((s8[5963776]{0:T(1024)(128)(4,1)}), s8[1769472]{0:T(1024)(128)(4,1)S(1)}, s32[]{:S(2)}) async-start(s8[5963776]{0:T(1024)(128)(4,1)} %bitcast.98), calls=%async_computation.1 | async-start | bytes 3538944
  186.4 9.7 %collective-permute-start.3 = (f32[2,48,832]{2,1,0:T(8,128)}, f32[2,48,832]{2,1,0:T(8,128)}, u32[]{:S(2)}, u32[]{:S(2)}) collective-permute-start(f32[2,48,832]{2,1,0:T(8,128)} %copy.52), channel_id=1, source_target_pairs={{0,1},{1,2},{2,3},{3,4},{4,5},{5,6},{6,7},{7,8},{8,9},{9,10},{10,1... | collective-permute-start | bytes 958472 | tf_op jit(solution)/shard_map/ppermute | solution.py:12
  196.1 4.6 %slice-start.1 = ((s8[5963776]{0:T(1024)(128)(4,1)}), s8[4194304]{0:T(1024)(128)(4,1)S(1)}, s32[]{:S(2)}) async-start(s8[5963776]{0:T(1024)(128)(4,1)} %bitcast.98), calls=%async_computation.2 | async-start | bytes 8388608
  201.9 3.1 %collective-permute-start.4 = (bf16[2,48,832]{2,1,0:T(8,128)(2,1)S(1)}, bf16[2,48,832]{2,1,0:T(8,128)(2,1)S(1)}, u32[]{:S(2)}, u32[]{:S(2)}) collective-permute-start(bf16[2,48,832]{2,1,0:T(8,128)(2,1)S(1)} %get-tuple-element.15), channel_id=1, source_target_pairs={{0,15},{1,0},{2,1},{3,2},{4,3},{5,4},{6,5},{7,6},{8,7},{9,8},{10,9... | collective-permute-start | bytes 479240 | tf_op jit(solution)/shard_map/ppermute | solution.py:12
  203.0 16.1 %slice-start.2 = ((s8[5963776]{0:T(1024)(128)(4,1)}), s8[1769472]{0:T(1024)(128)(4,1)S(1)}, s32[]{:S(2)}) async-start(s8[5963776]{0:T(1024)(128)(4,1)} %bitcast.101), calls=%async_computation.3 | async-start | bytes 3538944
  204.0 9.7 %collective-permute-start.5 = (f32[2,48,832]{2,1,0:T(8,128)}, f32[2,48,832]{2,1,0:T(8,128)}, u32[]{:S(2)}, u32[]{:S(2)}) collective-permute-start(f32[2,48,832]{2,1,0:T(8,128)} %copy.54), channel_id=1, source_target_pairs={{0,1},{1,2},{2,3},{3,4},{4,5},{5,6},{6,7},{7,8},{8,9},{9,10},{10,1... | collective-permute-start | bytes 958472 | tf_op jit(solution)/shard_map/ppermute | solution.py:12
  213.7 5.3 %slice-start.3 = ((s8[5963776]{0:T(1024)(128)(4,1)}), s8[4194304]{0:T(1024)(128)(4,1)S(1)}, s32[]{:S(2)}) async-start(s8[5963776]{0:T(1024)(128)(4,1)} %bitcast.101), calls=%async_computation.4 | async-start | bytes 8388608
  220.2 2.9 %collective-permute-start.6 = (bf16[2,48,832]{2,1,0:T(8,128)(2,1)S(1)}, bf16[2,48,832]{2,1,0:T(8,128)(2,1)S(1)}, u32[]{:S(2)}, u32[]{:S(2)}) collective-permute-start(bf16[2,48,832]{2,1,0:T(8,128)(2,1)S(1)} %get-tuple-element.17), channel_id=1, source_target_pairs={{0,15},{1,0},{2,1},{3,2},{4,3},{5,4},{6,5},{7,6},{8,7},{9,8},{10,9... | collective-permute-start | bytes 479240 | tf_op jit(solution)/shard_map/ppermute | solution.py:12
  221.5 9.4 %collective-permute-start.7 = (f32[2,48,832]{2,1,0:T(8,128)S(1)}, f32[2,48,832]{2,1,0:T(8,128)S(1)}, u32[]{:S(2)}, u32[]{:S(2)}) collective-permute-start(f32[2,48,832]{2,1,0:T(8,128)S(1)} %copy.56), channel_id=1, source_target_pairs={{0,1},{1,2},{2,3},{3,4},{4,5},{5,6},{6,7},{7,8},{8,9},{9,10},{10,1... | collective-permute-start | bytes 958472 | tf_op jit(solution)/shard_map/ppermute | solution.py:12
where the time goes:
time: 237 us; the launch traced here: 236 us
  waiting for transfers between devices  159 us (67%)
  local copies, waits for them, and re-layouts  32.8 us (14%)
  matrix products  27.8 us (12%)
  starting transfers between devices  14.5 us (6%)
    all_to_all x1, waiting for transfers between devices, per_device(): lax.all_to_all(laid_out, 'gx', split_axis=0, concat_axis=2, tiled=True)  104 us
    ppermute x8, waiting for transfers between devices, passed_along(): return lax.ppermute(value, axis, pairs)  55.4 us
    dot_general x4, matrix products, direct_terms(): jnp.einsum('bskn,bsmn->bkm', picked, arrived, preferred_element_type=jnp....  19.6 us
    reshape x2, local copies, waits for them, and re-layouts, per_device(): edge_tiles.reshape(block_total, slot_count, orb_count // group, orb_count)  19.3 us
    all_to_all x1, starting transfers between devices, per_device(): lax.all_to_all(laid_out, 'gx', split_axis=0, concat_axis=2, tiled=True)  7.57 us
    ppermute x8, starting transfers between devices, passed_along(): return lax.ppermute(value, axis, pairs)  6.97 us
    all_to_all x1, local copies, waits for them, and re-layouts, per_device(): lax.all_to_all(laid_out, 'gx', split_axis=0, concat_axis=2, tiled=True)  5.74 us
  transfers between devices with their start and end apart: 9, of which 8 were waited for; matrix products, arithmetic and copies ran while one was open for 7% of the time, Pallas kernels for 0%

commit v1 on v0

v1 whole, which is shorter than its diff:
```python
import functools

import jax
import jax.numpy as jnp
from jax import lax
from jax.experimental import pallas as pl
from jax.experimental.pallas import tpu as pltpu
from jax.sharding import PartitionSpec as P

DEGREE = 4
LANES = 128
QUAD = 4
MIB = 2**20
VMEM_WHOLE = pl.BlockSpec(memory_space=pltpu.VMEM)
HBM_WHOLE = pl.BlockSpec(memory_space=pltpu.HBM)
SMEM_WHOLE = pl.BlockSpec(memory_space=pltpu.SMEM)


def passed_along(value, axis, steps):
    count = lax.axis_size(axis)
    pairs = [(source, (source + steps) % count) for source in range(count)]
    return lax.ppermute(value, axis, pairs)


def dot_nn(a, b):
    return lax.dot_general(a, b, (((1,), (0,)), ((), ())), preferred_element_type=jnp.float32)


def dot_nt(a, b):
    return lax.dot_general(a, b, (((1,), (1,)), ((), ())), preferred_element_type=jnp.float32)


def selector(rows, columns, source_of_row):
    row = lax.broadcasted_iota(jnp.int32, (rows, columns), 0)
    column = lax.broadcasted_iota(jnp.int32, (rows, columns), 1)
    return (column == source_of_row(row)).astype(jnp.bfloat16)


def pack_kernel(batch, x_ref, out_ref, x_buf, out_buf, tail_buf, in_sems, out_sems):
    rows, tiles, orbs = x_ref.shape
    group = tiles // QUAD
    unit = QUAD * QUAD
    steps = rows // QUAD
    full = orbs // LANES
    half = LANES // 2
    length = steps * unit
    arrivals = []
    for j in range(steps):
        part = pl.ds(j * QUAD, QUAD)
        arrivals.append(pltpu.make_async_copy(x_ref.at[part], x_buf.at[part], in_sems.at[j]))
        arrivals[-1].start()
    order = selector(QUAD * tiles, QUAD * tiles, lambda o: ((o % unit) // QUAD) * tiles + (o // unit) * QUAD + o % QUAD)
    leaving = []

    def leave(first, count):
        part = pl.ds(first, count)
        copy = pltpu.make_async_copy(out_buf.at[:, part, :], out_ref.at[:, part, :], out_sems.at[len(leaving)])
        copy.start()
        leaving.append(copy)

    begun = 0
    for j in range(steps):
        arrivals[j].wait()
        data = x_buf[j * QUAD : (j + 1) * QUAD].reshape(QUAD * tiles, orbs)
        for left in range(0, full * LANES, 2 * LANES):
            width = min(2 * LANES, full * LANES - left)
            part = dot_nn(order, data[:, left : left + width]).astype(jnp.bfloat16)
            for k in range(0, width, LANES):
                first = (left + k) // LANES * length + j * unit
                out_buf[:, first : first + unit, :] = part[:, k : k + LANES].reshape(group, unit, LANES)
        last = dot_nn(order, data[:, full * LANES :]).reshape(group, unit, half)
        both = jnp.concatenate([last[:, : unit // 2], last[:, unit // 2 :]], axis=2)
        tail_buf[:, j * unit // 2 : (j + 1) * unit // 2, :] = both
        if (j + 1) % batch == 0 or j == steps - 1:
            for k in range(full):
                leave(k * length + begun * unit, (j + 1 - begun) * unit)
            begun = j + 1
    out_buf[:, full * length :, :] = tail_buf[...].astype(jnp.bfloat16)
    leave(full * length, length // 2)
    for copy in leaving:
        copy.wait()


def pack(edge_tiles):
    tiles, rows, orbs = edge_tiles.shape
    group = tiles // QUAD
    turned = jnp.transpose(edge_tiles, (1, 0, 2))
    flat = rows * QUAD * orbs // LANES
    steps = rows // QUAD
    batch = 4
    copies = -(-steps // batch) * (orbs // LANES) + 1
    return pl.pallas_call(
        functools.partial(pack_kernel, batch),
        out_shape=jax.ShapeDtypeStruct((group, flat, LANES), jnp.bfloat16),
        in_specs=[HBM_WHOLE],
        out_specs=HBM_WHOLE,
        scratch_shapes=[
            pltpu.VMEM((rows, tiles, orbs), jnp.bfloat16),
            pltpu.VMEM((group, flat, LANES), jnp.bfloat16),
            pltpu.VMEM((group, rows * QUAD // 2, LANES), jnp.float32),
            pltpu.SemaphoreType.DMA((steps,)),
            pltpu.SemaphoreType.DMA((copies,)),
        ],
        compiler_params=pltpu.CompilerParams(vmem_limit_bytes=32 * MIB),
        name="pack",
    )(turned)


def unpack_kernel(orbs, in_ref, out_ref, body_ref, tail_ref, sems):
    group, rows, _ = body_ref.shape
    full = orbs // LANES
    half = LANES // 2
    unit = QUAD * QUAD
    copies = [
        pltpu.make_async_copy(
            in_ref.at[:, pl.ds(j * rows, rows), :], body_ref.at[:, :, pl.ds(j * LANES, LANES)], sems.at[j]
        )
        for j in range(full)
    ]
    copies.append(pltpu.make_async_copy(in_ref.at[:, pl.ds(full * rows, rows // 2), :], tail_ref, sems.at[full]))
    for copy in copies:
        copy.start()
    for copy in copies:
        copy.wait()
    block = 4 * QUAD
    size = block * unit
    span = block * QUAD
    order = selector(size, size, lambda o: (o % span) // QUAD * unit + (o % QUAD) * QUAD + o // span)
    order_tail = selector(
        size, size // 2, lambda o: (o % span) // QUAD * (unit // 2) + (o % QUAD) % 2 * QUAD + o // span
    )
    early = lax.broadcasted_iota(jnp.int32, (size, half), 0) % QUAD < 2
    body = body_ref.reshape(group * rows, full * LANES)
    tail = tail_ref.reshape(group * rows // 2, LANES)
    for i in range(orbs // span):
        clean = dot_nn(order, body[pl.ds(i * size, size), :]).astype(jnp.bfloat16)
        both = dot_nn(order_tail, tail[pl.ds(i * size // 2, size // 2), :])
        last = jnp.where(early, both[:, :half], both[:, half:]).astype(jnp.bfloat16)
        for e in range(QUAD):
            out_ref[e, pl.ds(i * span, span), : full * LANES] = clean[e * span : (e + 1) * span]
            out_ref[e, pl.ds(i * span, span), full * LANES :] = last[e * span : (e + 1) * span]


def unpack(arrived, rows, orbs):
    group = arrived.shape[0]
    full = orbs // LANES
    return pl.pallas_call(
        functools.partial(unpack_kernel, orbs),
        out_shape=jax.ShapeDtypeStruct((QUAD, orbs, orbs), jnp.bfloat16),
        in_specs=[HBM_WHOLE],
        out_specs=VMEM_WHOLE,
        scratch_shapes=[
            pltpu.VMEM((group, rows * QUAD, full * LANES), jnp.bfloat16),
            pltpu.VMEM((group, rows * QUAD // 2, LANES), jnp.bfloat16),
            pltpu.SemaphoreType.DMA((full + 1,)),
        ],
        compiler_params=pltpu.CompilerParams(vmem_limit_bytes=32 * MIB),
        name="unpack",
    )(arrived)


def turned_kernel(target_ref, rounded_ref, tiles_ref, own_ref, send_ref, acc_ref):
    blk_dev = rounded_ref.shape[0]
    edges = tiles_ref.shape[0]
    acc_ref[...] = jnp.zeros_like(acc_ref)
    for e in range(edges):
        acc_ref[target_ref[e]] += dot_nn(rounded_ref[e * blk_dev // edges], tiles_ref[e])
    own_ref[...] = acc_ref[:blk_dev]
    send_ref[...] = acc_ref[blk_dev:].astype(jnp.bfloat16)


def turned_terms(target, rounded, tiles):
    blk_dev, vecs, orbs = rounded.shape
    return pl.pallas_call(
        turned_kernel,
        out_shape=(
            jax.ShapeDtypeStruct(rounded.shape, jnp.float32),
            jax.ShapeDtypeStruct(rounded.shape, jnp.bfloat16),
        ),
        in_specs=[SMEM_WHOLE, VMEM_WHOLE, VMEM_WHOLE],
        out_specs=(VMEM_WHOLE, VMEM_WHOLE),
        scratch_shapes=[pltpu.VMEM((2 * blk_dev, vecs, orbs), jnp.float32)],
        compiler_params=pltpu.CompilerParams(vmem_limit_bytes=16 * MIB),
        cost_estimate=pl.CostEstimate(
            flops=2 * tiles.size * vecs * 4, bytes_accessed=2 * tiles.size, transcendentals=0
        ),
        name="turned",
    )(target, rounded, tiles)


def direct_kernel(target_ref, rounded_ref, following_ref, tiles_ref, own_ref, out_ref, picked_ref):
    blk_dev = rounded_ref.shape[0]
    edges = tiles_ref.shape[0]
    slots = edges // blk_dev
    picked_ref[:blk_dev] = rounded_ref[...]
    picked_ref[blk_dev:] = following_ref[...]
    for b in range(blk_dev):
        total = own_ref[b]
        for e in range(b * slots, (b + 1) * slots):
            total += dot_nt(picked_ref[target_ref[e]], tiles_ref[e])
        out_ref[b] = total


def direct_terms(target, rounded, following, tiles, own):
    blk_dev, vecs, orbs = rounded.shape
    return pl.pallas_call(
        direct_kernel,
        out_shape=jax.ShapeDtypeStruct(rounded.shape, jnp.float32),
        in_specs=[SMEM_WHOLE] + [VMEM_WHOLE] * 4,
        out_specs=VMEM_WHOLE,
        scratch_shapes=[pltpu.VMEM((2 * blk_dev, vecs, orbs), jnp.bfloat16)],
        compiler_params=pltpu.CompilerParams(vmem_limit_bytes=16 * MIB),
        cost_estimate=pl.CostEstimate(
            flops=2 * tiles.size * vecs * 4, bytes_accessed=2 * tiles.size, transcendentals=0
        ),
        name="direct",
    )(target, rounded, following, tiles, own)


def gathered_tiles(edge_tiles, block_total, slots):
    group = lax.axis_size("gx")
    tiles, rows, orbs = edge_tiles.shape
    per_owner = tiles // group
    if per_owner == QUAD and rows % QUAD == 0 and orbs % LANES == LANES // 2 and orbs % (4 * QUAD * QUAD) == 0:
        sent = lax.all_to_all(pack(edge_tiles), "gx", split_axis=0, concat_axis=0, tiled=True)
        return unpack(sent, rows, orbs)
    return lax.all_to_all(edge_tiles, "gx", split_axis=0, concat_axis=1, tiled=True)


def per_device(edge_tiles, trial_panel, col_blocks):
    blk_dev, _, _ = trial_panel.shape
    slots = col_blocks.shape[1]
    block_total = blk_dev * lax.axis_size("gx")
    domain = lax.axis_index("gx")
    own_cols = lax.dynamic_slice_in_dim(col_blocks, domain * blk_dev, blk_dev, 0).reshape(-1)
    target = jnp.mod(own_cols - domain * blk_dev, block_total)
    tiles = gathered_tiles(edge_tiles, block_total, slots)

    def operate(rounded):
        following = passed_along(rounded, "gx", -1)
        own, send = turned_terms(target, rounded, tiles)
        arrive = passed_along(send, "gx", 1)
        return direct_terms(target, rounded, following, tiles, own) + arrive.astype(jnp.float32)

    previous = trial_panel
    current = operate(trial_panel.astype(jnp.bfloat16))
    for _ in range(DEGREE - 1):
        following_panel = 2.0 * operate(current.astype(jnp.bfloat16)) - previous
        previous, current = current, following_panel
    return previous, current


def solution(mesh):
    return jax.shard_map(
        per_device,
        mesh=mesh,
        in_specs=(P("member", "gx", None), P(("member", "gx"), None, None), P()),
        out_specs=(P(("member", "gx"), None, None), P(("member", "gx"), None, None)),
        check_vma=False,
    )
```

time: 237 us -> 190 us (0.80)
  Pallas kernels: 0 us -> 29.5 us
  matrix products: 27.8 us -> 0 us
  local copies, waits for them, and re-layouts: 32.8 us -> 5.34 us
  waiting for transfers between devices: 159 us -> 137 us
    pallas_call x0 -> x10, Pallas kernels: none -> 29.5 us  [the longest x1 9.25 us: pack(): pl.pallas_call(functools.partial(pack_kernel, batch), out_shape=jax.Shape...]
    dot_general x12 -> x0, matrix products: 27.8 us -> none  [the longest x4 19.6 us: direct_terms(): jnp.einsum('bskn,bsmn->bkm', picked, arrived, preferred_element_type=jnp....]
    reshape x2 -> x0, local copies, waits for them, and re-layouts: 19.3 us -> none  [per_device(): edge_tiles.reshape(block_total, slot_count, orb_count // group, orb_count)]
    ppermute x8, waiting for transfers between devices: 55.4 us -> 40.6 us  [passed_along(): return lax.ppermute(value, axis, pairs)]
    all_to_all x1, waiting for transfers between devices: 104 us -> 96.4 us  [gathered_tiles(): lax.all_to_all(pack(edge_tiles), 'gx', split_axis=0, concat_axis=0, tiled...]
    all_to_all x1 -> x0, local copies, waits for them, and re-layouts: 5.74 us -> none  [per_device(): lax.all_to_all(laid_out, 'gx', split_axis=0, concat_axis=2, tiled=True)]
    gather x4 -> x0, local copies, waits for them, and re-layouts: 2.41 us -> none  [direct_terms(): jnp.take(source_rows, target, axis=0)]
    unnamed x20 -> x8, local copies, waits for them, and re-layouts: 4.14 us -> 5.16 us
  transfers between devices with their start and end apart: 9 -> 9, of which waited for: 8 -> 8; matrix products, arithmetic and copies ran while one was open for 7% -> 0% of each run, Pallas kernels for 0% -> 11%
where the time goes in v1:
time: 190 us; the launch traced here: 189 us
  waiting for transfers between devices  137 us (72%)
  Pallas kernels  29.5 us (16%)
  starting transfers between devices  14.9 us (8%)
  local copies, waits for them, and re-layouts  5.34 us (3%)
    all_to_all x1, waiting for transfers between devices, gathered_tiles(): lax.all_to_all(pack(edge_tiles), 'gx', split_axis=0, concat_axis=0, tiled...  96.4 us
    ppermute x8, waiting for transfers between devices, passed_along(): return lax.ppermute(value, axis, pairs)  40.6 us
    pallas_call x1, Pallas kernels, pack(): pl.pallas_call(functools.partial(pack_kernel, batch), out_shape=jax.Shape...  9.25 us
    pallas_call x4, Pallas kernels, direct_terms(): pl.pallas_call(direct_kernel, out_shape=jax.ShapeDtypeStruct(rounded.shap...  9.23 us
    all_to_all x1, starting transfers between devices, gathered_tiles(): lax.all_to_all(pack(edge_tiles), 'gx', split_axis=0, concat_axis=0, tiled...  7.56 us
    ppermute x8, starting transfers between devices, passed_along(): return lax.ppermute(value, axis, pairs)  7.31 us
    pallas_call x4, Pallas kernels, turned_terms(): pl.pallas_call(turned_kernel, out_shape=(jax.ShapeDtypeStruct(rounded.sha...  6.62 us
    unnamed x8, local copies, waits for them, and re-layouts  5.16 us
  transfers between devices with their start and end apart: 9, of which 8 were waited for; matrix products, arithmetic and copies ran while one was open for 0% of the time, Pallas kernels for 11%

profile of v1, /device:TPU:0, one launch (start us, length us, event | category | flops | bytes accessed | tf_op | source)
XLA Modules:
  0.0 189.4 jit_solution(11942105051938305924)
XLA Ops:
  0.6 2.7 %copy-done.1 = bf16[64,52,832]{2,0,1:T(8,128)(2,1)S(1)} copy-done((bf16[64,52,832]{2,0,1:T(8,128)(2,1)S(1)}, bf16[64,52,832]{2,0,1:T(8,128)(2,1)}, u32[]{:S(2)}) %copy-start.1) | copy-done | bytes 5537816
  3.3 9.3 %pack.1 = bf16[16,1352,128]{2,1,0:T(8,128)(2,1)S(1)} custom-call(bf16[52,64,832]{2,1,0:T(8,128)(2,1)S(1)} %bitcast.1), custom_call_target="tpu_custom_call" | custom-call | tf_op jit(solution)/shard_map/pack/pallas_call | solution.py:92
  12.6 2.5 %copy-done = bf16[16,1352,128]{2,1,0:T(8,128)(2,1)} copy-done((bf16[16,1352,128]{2,1,0:T(8,128)(2,1)}, bf16[16,1352,128]{2,1,0:T(8,128)(2,1)S(1)}, u32[]{:S(2)}) %copy-start) | copy-done | bytes 5537816
  15.1 7.6 %all-to-all-start = ((bf16[16,1352,128]{2,1,0:T(8,128)(2,1)}), bf16[16,1352,128]{2,1,0:T(8,128)(2,1)}, u32[]{:S(2)}, u32[]{:S(2)}) async-start(bf16[16,1352,128]{2,1,0:T(8,128)(2,1)} %copy-done), calls=%async_computation | async-start | bytes 11075584 | tf_op jit(solution)/shard_map/all_to_all | solution.py:225
  22.7 4.4 %collective-permute-start = (bf16[2,48,832]{2,1,0:T(8,128)(2,1)S(1)}, bf16[2,48,832]{2,1,0:T(8,128)(2,1)S(1)}, u32[]{:S(2)}, u32[]{:S(2)}) collective-permute-start(bf16[2,48,832]{2,1,0:T(8,128)(2,1)S(1)} %convert_element_type.24.rounded_ref), channel_id=1, source_target_pairs={{0,15},{1,0},{2,1},{3,2},{4,3},{5,4},{6,5},{7,6},{8,7},{9,8},{10,9... | collective-permute-start | bytes 479240 | tf_op jit(solution)/shard_map/ppermute | solution.py:22
  27.1 0.1 copy.5
  27.2 0.1 sub.20
  27.3 96.4 %all-to-all-done.in_ref = bf16[16,1352,128]{2,1,0:T(8,128)(2,1)} async-done(((bf16[16,1352,128]{2,1,0:T(8,128)(2,1)}), bf16[16,1352,128]{2,1,0:T(8,128)(2,1)}, u32[]{:S(2)}, u32[]{:S(2)}) %all-to-all-start) | async-done | bytes 5537824 | tf_op jit(solution)/shard_map/all_to_all | solution.py:225
  123.7 4.4 %unpack.1.tiles_ref = bf16[4,832,832]{2,1,0:T(8,128)(2,1)S(1)} custom-call(bf16[16,1352,128]{2,1,0:T(8,128)(2,1)} %all-to-all-done.in_ref), custom_call_target="tpu_custom_call" | custom-call | tf_op jit(solution)/shard_map/unpack/pallas_call | solution.py:147
  128.2 1.7 turned.4
  129.8 0.8 collective-permute-start.1
  130.7 2.3 %direct.4 = f32[2,48,832]{2,1,0:T(8,128)S(1)} custom-call(s32[4]{0:T(128)S(1)} %and_select_fusion.target_ref, bf16[2,48,832]{2,1,0:T(8,128)(2,1)S(1)} %convert_element_type.24.rounded_ref, bf16[2,48,832]{2,1,0:T(8,128)(2,1)S(1)} %collective-permute-done.following_ref, bf16[4,832,832]{2,1,0:T(8,128)(2,1)S(1)} %unpack.1.tiles_ref, ...), custom_call_target="tpu_custom_call" | custom-call | flops 1063256064 | bytes 5537792 | tf_op jit(solution)/shard_map/direct/pallas_call | solution.py:206
  133.0 25.4 %collective-permute-done.1 = bf16[2,48,832]{2,1,0:T(8,128)(2,1)S(1)} collective-permute-done((bf16[2,48,832]{2,1,0:T(8,128)(2,1)S(1)}, bf16[2,48,832]{2,1,0:T(8,128)(2,1)S(1)}, u32[]{:S(2)}, u32[]{:S(2)}) %collective-permute-start.1) | collective-permute-done | bytes 159776 | tf_op jit(solution)/shard_map/ppermute | solution.py:22
  158.4 1.7 turned.5
  160.1 0.5 collective-permute-start.3
  160.6 0.7 collective-permute-done.2.following_ref
  161.4 2.3 %direct.5 = f32[2,48,832]{2,1,0:T(8,128)S(1)} custom-call(s32[4]{0:T(128)S(1)} %and_select_fusion.target_ref, bf16[2,48,832]{2,1,0:T(8,128)(2,1)S(1)} %fusion.rounded_ref, bf16[2,48,832]{2,1,0:T(8,128)(2,1)S(1)} %collective-permute-done.2.following_ref, bf16[4,832,832]{2,1,0:T(8,128)(2,1)S(1)} %unpack.1.tiles_ref, f32[2,48,832]{2,1,0:T(8,128)S(1)} %get-tuple-element.12.own_ref), custom_call_target="tpu_custom_call" | custom-call | flops 1063256064 | bytes 5537792 | tf_op jit(solution)/shard_map/direct/pallas_call | solution.py:206
  163.7 4.1 %collective-permute-done.3 = bf16[2,48,832]{2,1,0:T(8,128)(2,1)S(1)} collective-permute-done((bf16[2,48,832]{2,1,0:T(8,128)(2,1)S(1)}, bf16[2,48,832]{2,1,0:T(8,128)(2,1)S(1)}, u32[]{:S(2)}, u32[]{:S(2)}) %collective-permute-start.3) | collective-permute-done | bytes 159776 | tf_op jit(solution)/shard_map/ppermute | solution.py:22
  167.8 0.7 collective-permute-start.4
  168.5 1.7 turned.6
  170.2 0.2 collective-permute-start.5
  170.4 1.0 collective-permute-done.4.following_ref
  171.4 2.3 %direct.6 = f32[2,48,832]{2,1,0:T(8,128)S(1)} custom-call(s32[4]{0:T(128)S(1)} %and_select_fusion.target_ref, bf16[2,48,832]{2,1,0:T(8,128)(2,1)S(1)} %fusion.1.rounded_ref, bf16[2,48,832]{2,1,0:T(8,128)(2,1)S(1)} %collective-permute-done.4.following_ref, bf16[4,832,832]{2,1,0:T(8,128)(2,1)S(1)} %unpack.1.tiles_ref, f32[2,48,832]{2,1,0:T(8,128)S(1)} %get-tuple-element.14.own_ref), custom_call_target="tpu_custom_call" | custom-call | flops 1063256064 | bytes 5537792 | tf_op jit(solution)/shard_map/direct/pallas_call | solution.py:206
  173.8 4.2 %collective-permute-done.5 = bf16[2,48,832]{2,1,0:T(8,128)(2,1)S(1)} collective-permute-done((bf16[2,48,832]{2,1,0:T(8,128)(2,1)S(1)}, bf16[2,48,832]{2,1,0:T(8,128)(2,1)S(1)}, u32[]{:S(2)}, u32[]{:S(2)}) %collective-permute-start.5) | collective-permute-done | bytes 159776 | tf_op jit(solution)/shard_map/ppermute | solution.py:22
  178.0 0.8 fusion.3
  178.8 0.5 collective-permute-start.6
  179.3 1.7 turned.7
  181.0 0.1 collective-permute-start.7
  181.0 1.2 collective-permute-done.6.following_ref
  182.2 2.3 %direct.7 = f32[2,48,832]{2,1,0:T(8,128)S(1)} custom-call(s32[4]{0:T(128)S(1)} %and_select_fusion.target_ref, bf16[2,48,832]{2,1,0:T(8,128)(2,1)S(1)} %get-tuple-element.18.rounded_ref, bf16[2,48,832]{2,1,0:T(8,128)(2,1)S(1)} %collective-permute-done.6.following_ref, bf16[4,832,832]{2,1,0:T(8,128)(2,1)S(1)} %unpack.1.tiles_ref, ...), custom_call_target="tpu_custom_call" | custom-call | flops 1063256064 | bytes 5537792 | tf_op jit(solution)/shard_map/direct/pallas_call | solution.py:206
  184.5 4.0 %collective-permute-done.7 = bf16[2,48,832]{2,1,0:T(8,128)(2,1)S(1)} collective-permute-done((bf16[2,48,832]{2,1,0:T(8,128)(2,1)S(1)}, bf16[2,48,832]{2,1,0:T(8,128)(2,1)S(1)}, u32[]{:S(2)}, u32[]{:S(2)}) %collective-permute-start.7) | collective-permute-done | bytes 159776 | tf_op jit(solution)/shard_map/ppermute | solution.py:22
  188.5 0.8 multiply_subtract_fusion
  (13 shorter events, 0.3 us)
Async XLA Ops:
  0.6 2.7 %copy-start.1 = (bf16[64,52,832]{2,0,1:T(8,128)(2,1)S(1)}, bf16[64,52,832]{2,0,1:T(8,128)(2,1)}, u32[]{:S(2)}) copy-start(bf16[64,52,832]{2,0,1:T(8,128)(2,1)} %param.3) | copy-start | bytes 16613380
  12.6 2.5 %copy-start = (bf16[16,1352,128]{2,1,0:T(8,128)(2,1)}, bf16[16,1352,128]{2,1,0:T(8,128)(2,1)S(1)}, u32[]{:S(2)}) copy-start(bf16[16,1352,128]{2,1,0:T(8,128)(2,1)S(1)} %pack.1) | copy-start | bytes 16613380
  15.1 7.6 %copy-start.2 = (f32[2,48,832]{2,1,0:T(8,128)S(1)}, f32[2,48,832]{2,1,0:T(8,128)}, u32[]{:S(2)}) copy-start(f32[2,48,832]{2,1,0:T(8,128)} %param.4) | copy-start | bytes 958468
  15.1 12.0 %copy-start.3 = (s32[32,2]{0,1:T(2,128)S(1)}, s32[32,2]{0,1:T(2,128)}, u32[]{:S(2)}) copy-start(s32[32,2]{0,1:T(2,128)} %param.5) | copy-start | bytes 772
  15.1 108.7 %all-to-all-start = ((bf16[16,1352,128]{2,1,0:T(8,128)(2,1)}), bf16[16,1352,128]{2,1,0:T(8,128)(2,1)}, u32[]{:S(2)}, u32[]{:S(2)}) async-start(bf16[16,1352,128]{2,1,0:T(8,128)(2,1)} %copy-done), calls=%async_computation | async-start | bytes 11075584 | tf_op jit(solution)/shard_map/all_to_all | solution.py:225
  22.7 108.0 %collective-permute-start = (bf16[2,48,832]{2,1,0:T(8,128)(2,1)S(1)}, bf16[2,48,832]{2,1,0:T(8,128)(2,1)S(1)}, u32[]{:S(2)}, u32[]{:S(2)}) collective-permute-start(bf16[2,48,832]{2,1,0:T(8,128)(2,1)S(1)} %convert_element_type.24.rounded_ref), channel_id=1, source_target_pairs={{0,15},{1,0},{2,1},{3,2},{4,3},{5,4},{6,5},{7,6},{8,7},{9,8},{10,9... | collective-permute-start | bytes 479240 | tf_op jit(solution)/shard_map/ppermute | solution.py:22
  129.8 28.5 %collective-permute-start.1 = (bf16[2,48,832]{2,1,0:T(8,128)(2,1)S(1)}, bf16[2,48,832]{2,1,0:T(8,128)(2,1)S(1)}, u32[]{:S(2)}, u32[]{:S(2)}) collective-permute-start(bf16[2,48,832]{2,1,0:T(8,128)(2,1)S(1)} %get-tuple-element.11), channel_id=1, source_target_pairs={{0,1},{1,2},{2,3},{3,4},{4,5},{5,6},{6,7},{7,8},{8,9},{9,10},{10,1... | collective-permute-start | bytes 479240 | tf_op jit(solution)/shard_map/ppermute | solution.py:22
  158.4 3.0 %collective-permute-start.2 = (bf16[2,48,832]{2,1,0:T(8,128)(2,1)S(1)}, bf16[2,48,832]{2,1,0:T(8,128)(2,1)S(1)}, u32[]{:S(2)}, u32[]{:S(2)}) collective-permute-start(bf16[2,48,832]{2,1,0:T(8,128)(2,1)S(1)} %fusion.rounded_ref), channel_id=1, source_target_pairs={{0,15},{1,0},{2,1},{3,2},{4,3},{5,4},{6,5},{7,6},{8,7},{9,8},{10,9... | collective-permute-start | bytes 479240 | tf_op jit(solution)/shard_map/ppermute | solution.py:22
  160.1 7.6 %collective-permute-start.3 = (bf16[2,48,832]{2,1,0:T(8,128)(2,1)S(1)}, bf16[2,48,832]{2,1,0:T(8,128)(2,1)S(1)}, u32[]{:S(2)}, u32[]{:S(2)}) collective-permute-start(bf16[2,48,832]{2,1,0:T(8,128)(2,1)S(1)} %get-tuple-element.13), channel_id=1, source_target_pairs={{0,1},{1,2},{2,3},{3,4},{4,5},{5,6},{6,7},{7,8},{8,9},{9,10},{10,1... | collective-permute-start | bytes 479240 | tf_op jit(solution)/shard_map/ppermute | solution.py:22
  167.8 3.6 %collective-permute-start.4 = (bf16[2,48,832]{2,1,0:T(8,128)(2,1)S(1)}, bf16[2,48,832]{2,1,0:T(8,128)(2,1)S(1)}, u32[]{:S(2)}, u32[]{:S(2)}) collective-permute-start(bf16[2,48,832]{2,1,0:T(8,128)(2,1)S(1)} %fusion.1.rounded_ref), channel_id=1, source_target_pairs={{0,15},{1,0},{2,1},{3,2},{4,3},{5,4},{6,5},{7,6},{8,7},{9,8},{10,9... | collective-permute-start | bytes 479240 | tf_op jit(solution)/shard_map/ppermute | solution.py:22
  170.2 7.8 %collective-permute-start.5 = (bf16[2,48,832]{2,1,0:T(8,128)(2,1)S(1)}, bf16[2,48,832]{2,1,0:T(8,128)(2,1)S(1)}, u32[]{:S(2)}, u32[]{:S(2)}) collective-permute-start(bf16[2,48,832]{2,1,0:T(8,128)(2,1)S(1)} %get-tuple-element.15), channel_id=1, source_target_pairs={{0,1},{1,2},{2,3},{3,4},{4,5},{5,6},{6,7},{7,8},{8,9},{9,10},{10,1... | collective-permute-start | bytes 479240 | tf_op jit(solution)/shard_map/ppermute | solution.py:22
  178.8 3.4 %collective-permute-start.6 = (bf16[2,48,832]{2,1,0:T(8,128)(2,1)S(1)}, bf16[2,48,832]{2,1,0:T(8,128)(2,1)S(1)}, u32[]{:S(2)}, u32[]{:S(2)}) collective-permute-start(bf16[2,48,832]{2,1,0:T(8,128)(2,1)S(1)} %get-tuple-element.18.rounded_ref), channel_id=1, source_target_pairs={{0,15},{1,0},{2,1},{3,2},{4,3},{5,4},{6,5},{7,6},{8,7},{9,8},{10,9... | collective-permute-start | bytes 479240 | tf_op jit(solution)/shard_map/ppermute | solution.py:22
  181.0 7.6 %collective-permute-start.7 = (bf16[2,48,832]{2,1,0:T(8,128)(2,1)S(1)}, bf16[2,48,832]{2,1,0:T(8,128)(2,1)S(1)}, u32[]{:S(2)}, u32[]{:S(2)}) collective-permute-start(bf16[2,48,832]{2,1,0:T(8,128)(2,1)S(1)} %get-tuple-element.17), channel_id=1, source_target_pairs={{0,1},{1,2},{2,3},{3,4},{4,5},{5,6},{6,7},{7,8},{8,9},{9,10},{10,1... | collective-permute-start | bytes 479240 | tf_op jit(solution)/shard_map/ppermute | solution.py:22

commit v2 on v1

--- a/solution.py
+++ b/solution.py
@@ -101,7 +101,7 @@
             pltpu.SemaphoreType.DMA((steps,)),
             pltpu.SemaphoreType.DMA((copies,)),
         ],
-        compiler_params=pltpu.CompilerParams(vmem_limit_bytes=32 * MIB),
+        compiler_params=pltpu.CompilerParams(vmem_limit_bytes=58 * MIB),
         name="pack",
     )(turned)
 
@@ -159,62 +159,61 @@
     )(arrived)
 
 
-def turned_kernel(target_ref, rounded_ref, tiles_ref, own_ref, send_ref, acc_ref):
+def edge_row(edge, edges, blk_dev):
+    return edge * blk_dev // edges
+
+
+def leaving_kernel(target_ref, rounded_ref, tiles_ref, out_ref, acc_ref):
     blk_dev = rounded_ref.shape[0]
     edges = tiles_ref.shape[0]
     acc_ref[...] = jnp.zeros_like(acc_ref)
     for e in range(edges):
-        acc_ref[target_ref[e]] += dot_nn(rounded_ref[e * blk_dev // edges], tiles_ref[e])
-    own_ref[...] = acc_ref[:blk_dev]
-    send_ref[...] = acc_ref[blk_dev:].astype(jnp.bfloat16)
-
-
-def turned_terms(target, rounded, tiles):
-    blk_dev, vecs, orbs = rounded.shape
+
+        @pl.when(target_ref[e] >= blk_dev)
+        def _(e=e):
+            acc_ref[target_ref[e] - blk_dev] += dot_nn(rounded_ref[edge_row(e, edges, blk_dev)], tiles_ref[e])
+
+    out_ref[...] = acc_ref[...].astype(jnp.bfloat16)
+
+
+def staying_kernel(target_ref, rounded_ref, tiles_ref, after_ref, out_ref):
+    blk_dev = rounded_ref.shape[0]
+    edges = tiles_ref.shape[0]
+    out_ref[...] = jnp.zeros_like(out_ref)
+    for e in range(edges):
+
+        @pl.when(target_ref[e] < blk_dev)
+        def _(e=e):
+            row = edge_row(e, edges, blk_dev)
+            out_ref[target_ref[e]] += dot_nn(rounded_ref[row], tiles_ref[e])
+            out_ref[row] += dot_nt(rounded_ref[target_ref[e]], tiles_ref[e])
+
+
+def entering_kernel(target_ref, following_ref, tiles_ref, start_ref, out_ref):
+    blk_dev = following_ref.shape[0]
+    edges = tiles_ref.shape[0]
+    out_ref[...] = start_ref[...]
+    for e in range(edges):
+
+        @pl.when(target_ref[e] >= blk_dev)
+        def _(e=e):
+            out_ref[edge_row(e, edges, blk_dev)] += dot_nt(following_ref[target_ref[e] - blk_dev], tiles_ref[e])
+
+
+def step_call(kernel, name, dtype, target, panel, tiles, rest=(), scratch=(), rest_specs=()):
+    vecs = panel.shape[1]
     return pl.pallas_call(
-        turned_kernel,
-        out_shape=(
-            jax.ShapeDtypeStruct(rounded.shape, jnp.float32),
-            jax.ShapeDtypeStruct(rounded.shape, jnp.bfloat16),
-        ),
-        in_specs=[SMEM_WHOLE, VMEM_WHOLE, VMEM_WHOLE],
-        out_specs=(VMEM_WHOLE, VMEM_WHOLE),
-        scratch_shapes=[pltpu.VMEM((2 * blk_dev, vecs, orbs), jnp.float32)],
+        kernel,
+        out_shape=jax.ShapeDtypeStruct(panel.shape, dtype),
+        in_specs=[SMEM_WHOLE, VMEM_WHOLE, VMEM_WHOLE, *rest_specs],
+        out_specs=VMEM_WHOLE,
+        scratch_shapes=scratch,
         compiler_params=pltpu.CompilerParams(vmem_limit_bytes=16 * MIB),
         cost_estimate=pl.CostEstimate(
             flops=2 * tiles.size * vecs * 4, bytes_accessed=2 * tiles.size, transcendentals=0
         ),
-        name="turned",
-    )(target, rounded, tiles)
-
-
-def direct_kernel(target_ref, rounded_ref, following_ref, tiles_ref, own_ref, out_ref, picked_ref):
-    blk_dev = rounded_ref.shape[0]
-    edges = tiles_ref.shape[0]
-    slots = edges // blk_dev
-    picked_ref[:blk_dev] = rounded_ref[...]
-    picked_ref[blk_dev:] = following_ref[...]
-    for b in range(blk_dev):
-        total = own_ref[b]
-        for e in range(b * slots, (b + 1) * slots):
-            total += dot_nt(picked_ref[target_ref[e]], tiles_ref[e])
-        out_ref[b] = total
-
-
-def direct_terms(target, rounded, following, tiles, own):
-    blk_dev, vecs, orbs = rounded.shape
-    return pl.pallas_call(
-        direct_kernel,
-        out_shape=jax.ShapeDtypeStruct(rounded.shape, jnp.float32),
-        in_specs=[SMEM_WHOLE] + [VMEM_WHOLE] * 4,
-        out_specs=VMEM_WHOLE,
-        scratch_shapes=[pltpu.VMEM((2 * blk_dev, vecs, orbs), jnp.bfloat16)],
-        compiler_params=pltpu.CompilerParams(vmem_limit_bytes=16 * MIB),
-        cost_estimate=pl.CostEstimate(
-            flops=2 * tiles.size * vecs * 4, bytes_accessed=2 * tiles.size, transcendentals=0
-        ),
-        name="direct",
-    )(target, rounded, following, tiles, own)
+        name=name,
+    )(target, panel, tiles, *rest)
 
 
 def gathered_tiles(edge_tiles, block_total, slots):
@@ -238,9 +237,21 @@
 
     def operate(rounded):
         following = passed_along(rounded, "gx", -1)
-        own, send = turned_terms(target, rounded, tiles)
+        send = step_call(
+            leaving_kernel,
+            "leaving",
+            jnp.bfloat16,
+            target,
+            rounded,
+            tiles,
+            scratch=[pltpu.VMEM(rounded.shape, jnp.float32)],
+        )
         arrive = passed_along(send, "gx", 1)
-        return direct_terms(target, rounded, following, tiles, own) + arrive.astype(jnp.float32)
+        home = step_call(
+            staying_kernel, "staying", jnp.float32, target, rounded, tiles, (send,), (), (pl.BlockSpec(memory_space=pl.ANY),)
+        )
+        direct = step_call(entering_kernel, "entering", jnp.float32, target, following, tiles, (home,), (), (VMEM_WHOLE,))
+        return direct + arrive.astype(jnp.float32)
 
     previous = trial_panel
     current = operate(trial_panel.astype(jnp.bfloat16))

time: 190 us -> 182 us (0.958)
  local copies, waits for them, and re-layouts: 5.34 us -> 0.19 us
  waiting for transfers between devices: 137 us -> 132 us
  Pallas kernels: 29.5 us -> 32.3 us
    ppermute x8, waiting for transfers between devices: 40.6 us -> 35.1 us  [passed_along(): return lax.ppermute(value, axis, pairs)]
    unnamed x8 -> x4, local copies, waits for them, and re-layouts: 5.16 us -> 0.01 us
    pallas_call x8 -> x12, Pallas kernels: 15.8 us -> 20.6 us  [step_call(): pl.pallas_call(kernel, out_shape=jax.ShapeDtypeStruct(panel.shape, dtype)...]
    pallas_call x1, Pallas kernels: 9.25 us -> 7.24 us  [pack(): pl.pallas_call(functools.partial(pack_kernel, batch), out_shape=jax.Shape...]
  transfers between devices with their start and end apart: 9 -> 9, of which waited for: 8 -> 5; matrix products, arithmetic and copies ran while one was open for 0% -> 0% of each run, Pallas kernels for 11% -> 14%
where the time goes in v2:
time: 182 us
  waiting for transfers between devices  132 us (73%)
  Pallas kernels  32.3 us (18%)
  starting transfers between devices  15.1 us (8%)
  other arithmetic  1.89 us (1%)
    all_to_all x1, waiting for transfers between devices, gathered_tiles(): lax.all_to_all(pack(edge_tiles), 'gx', split_axis=0, concat_axis=0, tiled...  96.4 us
    ppermute x8, waiting for transfers between devices, passed_along(): return lax.ppermute(value, axis, pairs)  35.1 us
    pallas_call x12, Pallas kernels, step_call(): pl.pallas_call(kernel, out_shape=jax.ShapeDtypeStruct(panel.shape, dtype)...  20.6 us
    all_to_all x1, starting transfers between devices, gathered_tiles(): lax.all_to_all(pack(edge_tiles), 'gx', split_axis=0, concat_axis=0, tiled...  7.57 us
    ppermute x8, starting transfers between devices, passed_along(): return lax.ppermute(value, axis, pairs)  7.52 us
    pallas_call x1, Pallas kernels, pack(): pl.pallas_call(functools.partial(pack_kernel, batch), out_shape=jax.Shape...  7.24 us
    pallas_call x1, Pallas kernels, unpack(): pl.pallas_call(functools.partial(unpack_kernel, orbs), out_shape=jax.Shap...  4.41 us
  transfers between devices with their start and end apart: 9, of which 5 were waited for; matrix products, arithmetic and copies ran while one was open for 0% of the time, Pallas kernels for 14%

profile of v2, /device:TPU:0, one launch (start us, length us, event | category | flops | bytes accessed | tf_op | source)
XLA Modules:
  0.0 181.8 jit_solution(10020334804505397295)
XLA Ops:
  0.6 7.2 %pack.1 = bf16[16,1352,128]{2,1,0:T(8,128)(2,1)} custom-call(bf16[52,64,832]{2,1,0:T(8,128)(2,1)} %bitcast.1), custom_call_target="tpu_custom_call" | custom-call | tf_op jit(solution)/shard_map/pack/pallas_call | solution.py:92
  7.9 7.6 %all-to-all-start = ((bf16[16,1352,128]{2,1,0:T(8,128)(2,1)}), bf16[16,1352,128]{2,1,0:T(8,128)(2,1)}, u32[]{:S(2)}, u32[]{:S(2)}) async-start(bf16[16,1352,128]{2,1,0:T(8,128)(2,1)} %pack.1), calls=%async_computation | async-start | bytes 11075584 | tf_op jit(solution)/shard_map/all_to_all | solution.py:224
  15.5 4.4 %collective-permute-start = (bf16[2,48,832]{2,1,0:T(8,128)(2,1)S(1)}, bf16[2,48,832]{2,1,0:T(8,128)(2,1)S(1)}, u32[]{:S(2)}, u32[]{:S(2)}) collective-permute-start(bf16[2,48,832]{2,1,0:T(8,128)(2,1)S(1)} %convert_element_type.24.rounded_ref), channel_id=1, source_target_pairs={{0,15},{1,0},{2,1},{3,2},{4,3},{5,4},{6,5},{7,6},{8,7},{9,8},{10,9... | collective-permute-start | bytes 479240 | tf_op jit(solution)/shard_map/ppermute | solution.py:22
  19.9 0.1 dynamic-slice_subtract_fusion
  20.0 0.1 copy.5
  20.1 0.1 sub.20
  20.2 96.4 %all-to-all-done.in_ref = bf16[16,1352,128]{2,1,0:T(8,128)(2,1)} async-done(((bf16[16,1352,128]{2,1,0:T(8,128)(2,1)}), bf16[16,1352,128]{2,1,0:T(8,128)(2,1)}, u32[]{:S(2)}, u32[]{:S(2)}) %all-to-all-start) | async-done | bytes 5537824 | tf_op jit(solution)/shard_map/all_to_all | solution.py:224
  116.6 4.4 %unpack.1.tiles_ref = bf16[4,832,832]{2,1,0:T(8,128)(2,1)S(1)} custom-call(bf16[16,1352,128]{2,1,0:T(8,128)(2,1)} %all-to-all-done.in_ref), custom_call_target="tpu_custom_call" | custom-call | tf_op jit(solution)/shard_map/unpack/pallas_call | solution.py:147
  121.0 1.3 leaving.4.after_ref
  122.3 0.5 collective-permute-start.1
  122.8 2.1 %staying.4.start_ref = f32[2,48,832]{2,1,0:T(8,128)S(1)} custom-call(s32[4]{0:T(128)S(1)} %and_select_fusion.target_ref, bf16[2,48,832]{2,1,0:T(8,128)(2,1)S(1)} %convert_element_type.24.rounded_ref, bf16[4,832,832]{2,1,0:T(8,128)(2,1)S(1)} %unpack.1.tiles_ref, bf16[2,48,832]{2,1,0:T(8,128)(2,1)S(1)} %leaving.4.after_ref), custom_call_target="tpu_custom_call" | custom-call | flops 1063256064 | bytes 5537792 | tf_op jit(solution)/shard_map/staying/pallas_call | solution.py:205
  124.9 1.7 entering.4
  126.6 24.2 %collective-permute-done.1 = bf16[2,48,832]{2,1,0:T(8,128)(2,1)S(1)} collective-permute-done((bf16[2,48,832]{2,1,0:T(8,128)(2,1)S(1)}, bf16[2,48,832]{2,1,0:T(8,128)(2,1)S(1)}, u32[]{:S(2)}, u32[]{:S(2)}) %collective-permute-start.1) | collective-permute-done | bytes 159776 | tf_op jit(solution)/shard_map/ppermute | solution.py:22
  150.9 0.8 collective-permute-start.2
  151.7 1.3 leaving.5.after_ref
  153.0 0.1 collective-permute-start.3
  153.1 2.3 %staying.5.start_ref = f32[2,48,832]{2,1,0:T(8,128)S(1)} custom-call(s32[4]{0:T(128)S(1)} %and_select_fusion.target_ref, bf16[2,48,832]{2,1,0:T(8,128)(2,1)S(1)} %fusion.rounded_ref, bf16[4,832,832]{2,1,0:T(8,128)(2,1)S(1)} %unpack.1.tiles_ref, bf16[2,48,832]{2,1,0:T(8,128)(2,1)S(1)} %leaving.5.after_ref), custom_call_target="tpu_custom_call" | custom-call | flops 1063256064 | bytes 5537792 | tf_op jit(solution)/shard_map/staying/pallas_call | solution.py:205
  155.4 1.7 entering.5
  157.1 3.6 %collective-permute-done.3 = bf16[2,48,832]{2,1,0:T(8,128)(2,1)S(1)} collective-permute-done((bf16[2,48,832]{2,1,0:T(8,128)(2,1)S(1)}, bf16[2,48,832]{2,1,0:T(8,128)(2,1)S(1)}, u32[]{:S(2)}, u32[]{:S(2)}) %collective-permute-start.3) | collective-permute-done | bytes 159776 | tf_op jit(solution)/shard_map/ppermute | solution.py:22
  160.6 0.1 fusion.1.rounded_ref
  160.7 0.9 collective-permute-start.4
  161.6 1.3 leaving.6.after_ref
  163.0 2.1 %staying.6.start_ref = f32[2,48,832]{2,1,0:T(8,128)S(1)} custom-call(s32[4]{0:T(128)S(1)} %and_select_fusion.target_ref, bf16[2,48,832]{2,1,0:T(8,128)(2,1)S(1)} %fusion.1.rounded_ref, bf16[4,832,832]{2,1,0:T(8,128)(2,1)S(1)} %unpack.1.tiles_ref, bf16[2,48,832]{2,1,0:T(8,128)(2,1)S(1)} %leaving.6.after_ref), custom_call_target="tpu_custom_call" | custom-call | flops 1063256064 | bytes 5537792 | tf_op jit(solution)/shard_map/staying/pallas_call | solution.py:205
  165.1 1.7 entering.6
  166.8 3.7 %collective-permute-done.5 = bf16[2,48,832]{2,1,0:T(8,128)(2,1)S(1)} collective-permute-done((bf16[2,48,832]{2,1,0:T(8,128)(2,1)S(1)}, bf16[2,48,832]{2,1,0:T(8,128)(2,1)S(1)}, u32[]{:S(2)}, u32[]{:S(2)}) %collective-permute-start.5) | collective-permute-done | bytes 159776 | tf_op jit(solution)/shard_map/ppermute | solution.py:22
  170.5 0.8 fusion.3
  171.4 0.7 collective-permute-start.6
  172.1 1.3 leaving.7.after_ref
  173.5 2.1 %staying.7.start_ref = f32[2,48,832]{2,1,0:T(8,128)S(1)} custom-call(s32[4]{0:T(128)S(1)} %and_select_fusion.target_ref, bf16[2,48,832]{2,1,0:T(8,128)(2,1)S(1)} %get-tuple-element.2.rounded_ref, bf16[4,832,832]{2,1,0:T(8,128)(2,1)S(1)} %unpack.1.tiles_ref, bf16[2,48,832]{2,1,0:T(8,128)(2,1)S(1)} %leaving.7.after_ref), custom_call_target="tpu_custom_call" | custom-call | flops 1063256064 | bytes 5537792 | tf_op jit(solution)/shard_map/staying/pallas_call | solution.py:205
  175.6 1.7 entering.7
  177.3 3.7 %collective-permute-done.7 = bf16[2,48,832]{2,1,0:T(8,128)(2,1)S(1)} collective-permute-done((bf16[2,48,832]{2,1,0:T(8,128)(2,1)S(1)}, bf16[2,48,832]{2,1,0:T(8,128)(2,1)S(1)}, u32[]{:S(2)}, u32[]{:S(2)}) %collective-permute-start.7) | collective-permute-done | bytes 159776 | tf_op jit(solution)/shard_map/ppermute | solution.py:22
  181.0 0.8 multiply_subtract_fusion
  (13 shorter events, 0.2 us)
Async XLA Ops:
  7.9 7.6 %copy-start = (f32[2,48,832]{2,1,0:T(8,128)S(1)}, f32[2,48,832]{2,1,0:T(8,128)}, u32[]{:S(2)}) copy-start(f32[2,48,832]{2,1,0:T(8,128)} %param.4) | copy-start | bytes 958468
  7.9 12.0 %copy-start.1 = (s32[32,2]{0,1:T(2,128)S(1)}, s32[32,2]{0,1:T(2,128)}, u32[]{:S(2)}) copy-start(s32[32,2]{0,1:T(2,128)} %param.5) | copy-start | bytes 772
  7.9 108.7 %all-to-all-start = ((bf16[16,1352,128]{2,1,0:T(8,128)(2,1)}), bf16[16,1352,128]{2,1,0:T(8,128)(2,1)}, u32[]{:S(2)}, u32[]{:S(2)}) async-start(bf16[16,1352,128]{2,1,0:T(8,128)(2,1)} %pack.1), calls=%async_computation | async-start | bytes 11075584 | tf_op jit(solution)/shard_map/all_to_all | solution.py:224
  15.5 109.4 %collective-permute-start = (bf16[2,48,832]{2,1,0:T(8,128)(2,1)S(1)}, bf16[2,48,832]{2,1,0:T(8,128)(2,1)S(1)}, u32[]{:S(2)}, u32[]{:S(2)}) collective-permute-start(bf16[2,48,832]{2,1,0:T(8,128)(2,1)S(1)} %convert_element_type.24.rounded_ref), channel_id=1, source_target_pairs={{0,15},{1,0},{2,1},{3,2},{4,3},{5,4},{6,5},{7,6},{8,7},{9,8},{10,9... | collective-permute-start | bytes 479240 | tf_op jit(solution)/shard_map/ppermute | solution.py:22
  122.3 28.5 %collective-permute-start.1 = (bf16[2,48,832]{2,1,0:T(8,128)(2,1)S(1)}, bf16[2,48,832]{2,1,0:T(8,128)(2,1)S(1)}, u32[]{:S(2)}, u32[]{:S(2)}) collective-permute-start(bf16[2,48,832]{2,1,0:T(8,128)(2,1)S(1)} %leaving.4.after_ref), channel_id=1, source_target_pairs={{0,1},{1,2},{2,3},{3,4},{4,5},{5,6},{6,7},{7,8},{8,9},{9,10},{10,1... | collective-permute-start | bytes 479240 | tf_op jit(solution)/shard_map/ppermute | solution.py:22
  150.9 4.5 %collective-permute-start.2 = (bf16[2,48,832]{2,1,0:T(8,128)(2,1)S(1)}, bf16[2,48,832]{2,1,0:T(8,128)(2,1)S(1)}, u32[]{:S(2)}, u32[]{:S(2)}) collective-permute-start(bf16[2,48,832]{2,1,0:T(8,128)(2,1)S(1)} %fusion.rounded_ref), channel_id=1, source_target_pairs={{0,15},{1,0},{2,1},{3,2},{4,3},{5,4},{6,5},{7,6},{8,7},{9,8},{10,9... | collective-permute-start | bytes 479240 | tf_op jit(solution)/shard_map/ppermute | solution.py:22
  153.0 7.6 %collective-permute-start.3 = (bf16[2,48,832]{2,1,0:T(8,128)(2,1)S(1)}, bf16[2,48,832]{2,1,0:T(8,128)(2,1)S(1)}, u32[]{:S(2)}, u32[]{:S(2)}) collective-permute-start(bf16[2,48,832]{2,1,0:T(8,128)(2,1)S(1)} %leaving.5.after_ref), channel_id=1, source_target_pairs={{0,1},{1,2},{2,3},{3,4},{4,5},{5,6},{6,7},{7,8},{8,9},{9,10},{10,1... | collective-permute-start | bytes 479240 | tf_op jit(solution)/shard_map/ppermute | solution.py:22
  160.7 4.4 %collective-permute-start.4 = (bf16[2,48,832]{2,1,0:T(8,128)(2,1)S(1)}, bf16[2,48,832]{2,1,0:T(8,128)(2,1)S(1)}, u32[]{:S(2)}, u32[]{:S(2)}) collective-permute-start(bf16[2,48,832]{2,1,0:T(8,128)(2,1)S(1)} %fusion.1.rounded_ref), channel_id=1, source_target_pairs={{0,15},{1,0},{2,1},{3,2},{4,3},{5,4},{6,5},{7,6},{8,7},{9,8},{10,9... | collective-permute-start | bytes 479240 | tf_op jit(solution)/shard_map/ppermute | solution.py:22
  162.9 7.6 %collective-permute-start.5 = (bf16[2,48,832]{2,1,0:T(8,128)(2,1)S(1)}, bf16[2,48,832]{2,1,0:T(8,128)(2,1)S(1)}, u32[]{:S(2)}, u32[]{:S(2)}) collective-permute-start(bf16[2,48,832]{2,1,0:T(8,128)(2,1)S(1)} %leaving.6.after_ref), channel_id=1, source_target_pairs={{0,1},{1,2},{2,3},{3,4},{4,5},{5,6},{6,7},{7,8},{8,9},{9,10},{10,1... | collective-permute-start | bytes 479240 | tf_op jit(solution)/shard_map/ppermute | solution.py:22
  171.4 4.2 %collective-permute-start.6 = (bf16[2,48,832]{2,1,0:T(8,128)(2,1)S(1)}, bf16[2,48,832]{2,1,0:T(8,128)(2,1)S(1)}, u32[]{:S(2)}, u32[]{:S(2)}) collective-permute-start(bf16[2,48,832]{2,1,0:T(8,128)(2,1)S(1)} %get-tuple-element.2.rounded_ref), channel_id=1, source_target_pairs={{0,15},{1,0},{2,1},{3,2},{4,3},{5,4},{6,5},{7,6},{8,7},{9,8},{10,9... | collective-permute-start | bytes 479240 | tf_op jit(solution)/shard_map/ppermute | solution.py:22
  173.4 7.6 %collective-permute-start.7 = (bf16[2,48,832]{2,1,0:T(8,128)(2,1)S(1)}, bf16[2,48,832]{2,1,0:T(8,128)(2,1)S(1)}, u32[]{:S(2)}, u32[]{:S(2)}) collective-permute-start(bf16[2,48,832]{2,1,0:T(8,128)(2,1)S(1)} %leaving.7.after_ref), channel_id=1, source_target_pairs={{0,1},{1,2},{2,3},{3,4},{4,5},{5,6},{6,7},{7,8},{8,9},{9,10},{10,1... | collective-permute-start | bytes 479240 | tf_op jit(solution)/shard_map/ppermute | solution.py:22

commit v3 on v1

--- a/solution.py
+++ b/solution.py
@@ -101,7 +101,7 @@
             pltpu.SemaphoreType.DMA((steps,)),
             pltpu.SemaphoreType.DMA((copies,)),
         ],
-        compiler_params=pltpu.CompilerParams(vmem_limit_bytes=32 * MIB),
+        compiler_params=pltpu.CompilerParams(vmem_limit_bytes=58 * MIB),
         name="pack",
     )(turned)
 
@@ -111,17 +111,24 @@
     full = orbs // LANES
     half = LANES // 2
     unit = QUAD * QUAD
-    copies = [
-        pltpu.make_async_copy(
-            in_ref.at[:, pl.ds(j * rows, rows), :], body_ref.at[:, :, pl.ds(j * LANES, LANES)], sems.at[j]
+    stages = sems.shape[0]
+    sources = group // stages
+    arrivals = []
+    for g in range(stages):
+        part = pl.ds(g * sources, sources)
+        copies = [
+            pltpu.make_async_copy(
+                in_ref.at[part, pl.ds(j * rows, rows), :], body_ref.at[part, :, pl.ds(j * LANES, LANES)], sems.at[g, j]
+            )
+            for j in range(full)
+        ]
+        copies.append(
+            pltpu.make_async_copy(in_ref.at[part, pl.ds(full * rows, rows // 2), :], tail_ref.at[part], sems.at[g, full])
         )
-        for j in range(full)
-    ]
-    copies.append(pltpu.make_async_copy(in_ref.at[:, pl.ds(full * rows, rows // 2), :], tail_ref, sems.at[full]))
-    for copy in copies:
-        copy.start()
-    for copy in copies:
-        copy.wait()
+        for copy in copies:
+            copy.start()
+        arrivals.append(copies)
+    here = 0
     block = 4 * QUAD
     size = block * unit
     span = block * QUAD
@@ -133,6 +140,10 @@
     body = body_ref.reshape(group * rows, full * LANES)
     tail = tail_ref.reshape(group * rows // 2, LANES)
     for i in range(orbs // span):
+        while here * sources * rows < (i + 1) * size:
+            for copy in arrivals[here]:
+                copy.wait()
+            here += 1
         clean = dot_nn(order, body[pl.ds(i * size, size), :]).astype(jnp.bfloat16)
         both = dot_nn(order_tail, tail[pl.ds(i * size // 2, size // 2), :])
         last = jnp.where(early, both[:, :half], both[:, half:]).astype(jnp.bfloat16)
@@ -152,7 +163,7 @@
         scratch_shapes=[
             pltpu.VMEM((group, rows * QUAD, full * LANES), jnp.bfloat16),
             pltpu.VMEM((group, rows * QUAD // 2, LANES), jnp.bfloat16),
-            pltpu.SemaphoreType.DMA((full + 1,)),
+            pltpu.SemaphoreType.DMA((4 if group % 4 == 0 else 1, full + 1)),
         ],
         compiler_params=pltpu.CompilerParams(vmem_limit_bytes=32 * MIB),
         name="unpack",
@@ -197,7 +208,7 @@
     for b in range(blk_dev):
         total = own_ref[b]
         for e in range(b * slots, (b + 1) * slots):
-            total += dot_nt(picked_ref[target_ref[e]], tiles_ref[e])
+            total += dot_nn(picked_ref[target_ref[e]], tiles_ref[e])
         out_ref[b] = total
 
 
@@ -217,6 +228,43 @@
     )(target, rounded, following, tiles, own)
 
 
+def mirror_kernel(tiles_ref, after_ref, out_ref):
+    for e in range(tiles_ref.shape[0]):
+        out_ref[e] = tiles_ref[e].T
+
+
+def mirrored(tiles, after):
+    return pl.pallas_call(
+        mirror_kernel,
+        out_shape=jax.ShapeDtypeStruct(tiles.shape, tiles.dtype),
+        in_specs=[VMEM_WHOLE, pl.BlockSpec(memory_space=pl.ANY)],
+        out_specs=VMEM_WHOLE,
+        compiler_params=pltpu.CompilerParams(vmem_limit_bytes=16 * MIB),
+        cost_estimate=pl.CostEstimate(flops=tiles.size * 400, bytes_accessed=4 * tiles.size, transcendentals=0),
+        name="mirror",
+    )(tiles, after)
+
+
+def update_kernel(direct_ref, arrive_ref, previous_ref, panel_ref, rounded_ref):
+    panel = 2.0 * (direct_ref[...] + arrive_ref[...].astype(jnp.float32)) - previous_ref[...]
+    panel_ref[...] = panel
+    rounded_ref[...] = panel.astype(jnp.bfloat16)
+
+
+def updated(direct, arrive, previous):
+    return pl.pallas_call(
+        update_kernel,
+        out_shape=(
+            jax.ShapeDtypeStruct(direct.shape, jnp.float32),
+            jax.ShapeDtypeStruct(direct.shape, jnp.bfloat16),
+        ),
+        in_specs=[VMEM_WHOLE] * 3,
+        out_specs=(VMEM_WHOLE, VMEM_WHOLE),
+        compiler_params=pltpu.CompilerParams(vmem_limit_bytes=16 * MIB),
+        name="update",
+    )(direct, arrive, previous)
+
+
 def gathered_tiles(edge_tiles, block_total, slots):
     group = lax.axis_size("gx")
     tiles, rows, orbs = edge_tiles.shape
@@ -235,18 +283,24 @@
     own_cols = lax.dynamic_slice_in_dim(col_blocks, domain * blk_dev, blk_dev, 0).reshape(-1)
     target = jnp.mod(own_cols - domain * blk_dev, block_total)
     tiles = gathered_tiles(edge_tiles, block_total, slots)
-
-    def operate(rounded):
+    mirror = None
+    previous, current = None, trial_panel
+    rounded = trial_panel.astype(jnp.bfloat16)
+    for k in range(DEGREE):
         following = passed_along(rounded, "gx", -1)
         own, send = turned_terms(target, rounded, tiles)
         arrive = passed_along(send, "gx", 1)
-        return direct_terms(target, rounded, following, tiles, own) + arrive.astype(jnp.float32)
-
-    previous = trial_panel
-    current = operate(trial_panel.astype(jnp.bfloat16))
-    for _ in range(DEGREE - 1):
-        following_panel = 2.0 * operate(current.astype(jnp.bfloat16)) - previous
-        previous, current = current, following_panel
+        if k == 0:
+            mirror = mirrored(tiles, send)
+        direct = direct_terms(target, rounded, following, mirror, own)
+        if k == 0:
+            total = direct + arrive.astype(jnp.float32)
+            rounded = total.astype(jnp.bfloat16)
+        elif k < DEGREE - 1:
+            total, rounded = updated(direct, arrive, previous)
+        else:
+            total = 2.0 * (direct + arrive.astype(jnp.float32)) - previous
+        previous, current = current, total
     return previous, current
 
 

time: 190 us -> 181 us (0.953)
  local copies, waits for them, and re-layouts: 5.34 us -> 0.19 us
  Pallas kernels: 29.5 us -> 27 us
    unnamed x8 -> x4, local copies, waits for them, and re-layouts: 5.16 us -> 0.01 us
    pallas_call x4, Pallas kernels: 9.23 us -> 6.33 us  [direct_terms(): pl.pallas_call(direct_kernel, out_shape=jax.ShapeDtypeStruct(rounded.shap...]
    pallas_call x0 -> x3, Pallas kernels: none -> 2.57 us  [the longest x1 1.69 us: mirrored(): pl.pallas_call(mirror_kernel, out_shape=jax.ShapeDtypeStruct(tiles.shape,...]
    pallas_call x1, Pallas kernels: 9.25 us -> 7.25 us  [pack(): pl.pallas_call(functools.partial(pack_kernel, batch), out_shape=jax.Shape...]
  transfers between devices with their start and end apart: 9 -> 9, of which waited for: 8 -> 8; matrix products, arithmetic and copies ran while one was open for 0% -> 0% of each run, Pallas kernels for 11% -> 10%
where the time goes in v3:
time: 181 us
  waiting for transfers between devices  137 us (76%)
  Pallas kernels  27 us (15%)
  starting transfers between devices  14.7 us (8%)
    all_to_all x1, waiting for transfers between devices, gathered_tiles(): lax.all_to_all(pack(edge_tiles), 'gx', split_axis=0, concat_axis=0, tiled...  96.4 us
    ppermute x8, waiting for transfers between devices, passed_along(): return lax.ppermute(value, axis, pairs)  41 us
    all_to_all x1, starting transfers between devices, gathered_tiles(): lax.all_to_all(pack(edge_tiles), 'gx', split_axis=0, concat_axis=0, tiled...  7.57 us
    pallas_call x1, Pallas kernels, pack(): pl.pallas_call(functools.partial(pack_kernel, batch), out_shape=jax.Shape...  7.25 us
    ppermute x8, starting transfers between devices, passed_along(): return lax.ppermute(value, axis, pairs)  7.16 us
    pallas_call x4, Pallas kernels, turned_terms(): pl.pallas_call(turned_kernel, out_shape=(jax.ShapeDtypeStruct(rounded.sha...  6.72 us
    pallas_call x4, Pallas kernels, direct_terms(): pl.pallas_call(direct_kernel, out_shape=jax.ShapeDtypeStruct(rounded.shap...  6.33 us
    pallas_call x1, Pallas kernels, unpack(): pl.pallas_call(functools.partial(unpack_kernel, orbs), out_shape=jax.Shap...  4.17 us
  transfers between devices with their start and end apart: 9, of which 8 were waited for; matrix products, arithmetic and copies ran while one was open for 0% of the time, Pallas kernels for 10%

profile of v3, /device:TPU:0, one launch (start us, length us, event | category | flops | bytes accessed | tf_op | source)
XLA Modules:
  0.0 181.2 jit_solution(11129682062667503877)
XLA Ops:
  0.6 7.3 %pack.1 = bf16[16,1352,128]{2,1,0:T(8,128)(2,1)} custom-call(bf16[52,64,832]{2,1,0:T(8,128)(2,1)} %bitcast.1), custom_call_target="tpu_custom_call" | custom-call | tf_op jit(solution)/shard_map/pack/pallas_call | solution.py:92
  7.9 7.6 %all-to-all-start = ((bf16[16,1352,128]{2,1,0:T(8,128)(2,1)}), bf16[16,1352,128]{2,1,0:T(8,128)(2,1)}, u32[]{:S(2)}, u32[]{:S(2)}) async-start(bf16[16,1352,128]{2,1,0:T(8,128)(2,1)} %pack.1), calls=%async_computation | async-start | bytes 11075584 | tf_op jit(solution)/shard_map/all_to_all | solution.py:273
  15.5 4.4 %collective-permute-start = (bf16[2,48,832]{2,1,0:T(8,128)(2,1)S(1)}, bf16[2,48,832]{2,1,0:T(8,128)(2,1)S(1)}, u32[]{:S(2)}, u32[]{:S(2)}) collective-permute-start(bf16[2,48,832]{2,1,0:T(8,128)(2,1)S(1)} %convert_element_type.12.rounded_ref), channel_id=1, source_target_pairs={{0,15},{1,0},{2,1},{3,2},{4,3},{5,4},{6,5},{7,6},{8,7},{9,8},{10,9... | collective-permute-start | bytes 479240 | tf_op jit(solution)/shard_map/ppermute | solution.py:22
  19.9 0.1 dynamic-slice_subtract_fusion
  20.0 0.1 copy.5
  20.1 0.1 sub.14
  20.2 96.4 %all-to-all-done.in_ref = bf16[16,1352,128]{2,1,0:T(8,128)(2,1)} async-done(((bf16[16,1352,128]{2,1,0:T(8,128)(2,1)}), bf16[16,1352,128]{2,1,0:T(8,128)(2,1)}, u32[]{:S(2)}, u32[]{:S(2)}) %all-to-all-start) | async-done | bytes 5537824 | tf_op jit(solution)/shard_map/all_to_all | solution.py:273
  116.6 4.2 %unpack.1.tiles_ref = bf16[4,832,832]{2,1,0:T(8,128)(2,1)S(1)} custom-call(bf16[16,1352,128]{2,1,0:T(8,128)(2,1)} %all-to-all-done.in_ref), custom_call_target="tpu_custom_call" | custom-call | tf_op jit(solution)/shard_map/unpack/pallas_call | solution.py:158
  120.8 1.7 turned.4
  122.5 0.8 collective-permute-start.1
  123.3 1.7 mirror.1.tiles_ref
  125.0 1.6 direct.4
  126.6 24.4 %collective-permute-done.1 = bf16[2,48,832]{2,1,0:T(8,128)(2,1)S(1)} collective-permute-done((bf16[2,48,832]{2,1,0:T(8,128)(2,1)S(1)}, bf16[2,48,832]{2,1,0:T(8,128)(2,1)S(1)}, u32[]{:S(2)}, u32[]{:S(2)}) %collective-permute-start.1) | collective-permute-done | bytes 159776 | tf_op jit(solution)/shard_map/ppermute | solution.py:22
  151.0 0.3 collective-permute-start.2
  151.3 1.7 turned.5
  153.0 0.5 collective-permute-start.3
  153.5 0.7 collective-permute-done.2.following_ref
  154.2 1.6 direct.5.direct_ref
  155.8 5.0 %collective-permute-done.3.arrive_ref = bf16[2,48,832]{2,1,0:T(8,128)(2,1)S(1)} collective-permute-done((bf16[2,48,832]{2,1,0:T(8,128)(2,1)S(1)}, bf16[2,48,832]{2,1,0:T(8,128)(2,1)S(1)}, u32[]{:S(2)}, u32[]{:S(2)}) %collective-permute-start.3) | collective-permute-done | bytes 159776 | tf_op jit(solution)/shard_map/ppermute | solution.py:22
  160.8 0.1 update.2
  161.0 1.7 turned.6
  162.7 0.5 collective-permute-start.5
  163.2 0.7 collective-permute-done.4.following_ref
  163.9 1.6 direct.6.direct_ref
  165.5 4.8 %collective-permute-done.5.arrive_ref = bf16[2,48,832]{2,1,0:T(8,128)(2,1)S(1)} collective-permute-done((bf16[2,48,832]{2,1,0:T(8,128)(2,1)S(1)}, bf16[2,48,832]{2,1,0:T(8,128)(2,1)S(1)}, u32[]{:S(2)}, u32[]{:S(2)}) %collective-permute-start.5) | collective-permute-done | bytes 159776 | tf_op jit(solution)/shard_map/ppermute | solution.py:22
  170.3 0.8 update.3
  171.1 1.7 turned.7
  172.8 0.6 collective-permute-start.7
  173.3 0.7 collective-permute-done.6.following_ref
  174.0 1.6 direct.7
  175.6 4.8 %collective-permute-done.7 = bf16[2,48,832]{2,1,0:T(8,128)(2,1)S(1)} collective-permute-done((bf16[2,48,832]{2,1,0:T(8,128)(2,1)S(1)}, bf16[2,48,832]{2,1,0:T(8,128)(2,1)S(1)}, u32[]{:S(2)}, u32[]{:S(2)}) %collective-permute-start.7) | collective-permute-done | bytes 159776 | tf_op jit(solution)/shard_map/ppermute | solution.py:22
  180.4 0.8 multiply_subtract_fusion
  (10 shorter events, 0.2 us)
Async XLA Ops:
  7.9 7.6 %copy-start = (f32[2,48,832]{2,1,0:T(8,128)S(1)}, f32[2,48,832]{2,1,0:T(8,128)}, u32[]{:S(2)}) copy-start(f32[2,48,832]{2,1,0:T(8,128)} %previous_ref.1) | copy-start | bytes 958468
  7.9 12.0 %copy-start.1 = (s32[32,2]{0,1:T(2,128)S(1)}, s32[32,2]{0,1:T(2,128)}, u32[]{:S(2)}) copy-start(s32[32,2]{0,1:T(2,128)} %param.5) | copy-start | bytes 772
  7.9 108.7 %all-to-all-start = ((bf16[16,1352,128]{2,1,0:T(8,128)(2,1)}), bf16[16,1352,128]{2,1,0:T(8,128)(2,1)}, u32[]{:S(2)}, u32[]{:S(2)}) async-start(bf16[16,1352,128]{2,1,0:T(8,128)(2,1)} %pack.1), calls=%async_computation | async-start | bytes 11075584 | tf_op jit(solution)/shard_map/all_to_all | solution.py:273
  15.5 109.4 %collective-permute-start = (bf16[2,48,832]{2,1,0:T(8,128)(2,1)S(1)}, bf16[2,48,832]{2,1,0:T(8,128)(2,1)S(1)}, u32[]{:S(2)}, u32[]{:S(2)}) collective-permute-start(bf16[2,48,832]{2,1,0:T(8,128)(2,1)S(1)} %convert_element_type.12.rounded_ref), channel_id=1, source_target_pairs={{0,15},{1,0},{2,1},{3,2},{4,3},{5,4},{6,5},{7,6},{8,7},{9,8},{10,9... | collective-permute-start | bytes 479240 | tf_op jit(solution)/shard_map/ppermute | solution.py:22
  122.5 28.5 %collective-permute-start.1 = (bf16[2,48,832]{2,1,0:T(8,128)(2,1)S(1)}, bf16[2,48,832]{2,1,0:T(8,128)(2,1)S(1)}, u32[]{:S(2)}, u32[]{:S(2)}) collective-permute-start(bf16[2,48,832]{2,1,0:T(8,128)(2,1)S(1)} %get-tuple-element.14.after_ref), channel_id=1, source_target_pairs={{0,1},{1,2},{2,3},{3,4},{4,5},{5,6},{6,7},{7,8},{8,9},{9,10},{10,1... | collective-permute-start | bytes 479240 | tf_op jit(solution)/shard_map/ppermute | solution.py:22
  151.0 3.2 %collective-permute-start.2 = (bf16[2,48,832]{2,1,0:T(8,128)(2,1)S(1)}, bf16[2,48,832]{2,1,0:T(8,128)(2,1)S(1)}, u32[]{:S(2)}, u32[]{:S(2)}) collective-permute-start(bf16[2,48,832]{2,1,0:T(8,128)(2,1)S(1)} %get-tuple-element.26.rounded_ref), channel_id=1, source_target_pairs={{0,15},{1,0},{2,1},{3,2},{4,3},{5,4},{6,5},{7,6},{8,7},{9,8},{10,9... | collective-permute-start | bytes 479240 | tf_op jit(solution)/shard_map/ppermute | solution.py:22
  153.0 7.9 %collective-permute-start.3 = (bf16[2,48,832]{2,1,0:T(8,128)(2,1)S(1)}, bf16[2,48,832]{2,1,0:T(8,128)(2,1)S(1)}, u32[]{:S(2)}, u32[]{:S(2)}) collective-permute-start(bf16[2,48,832]{2,1,0:T(8,128)(2,1)S(1)} %get-tuple-element.17), channel_id=1, source_target_pairs={{0,1},{1,2},{2,3},{3,4},{4,5},{5,6},{6,7},{7,8},{8,9},{9,10},{10,1... | collective-permute-start | bytes 479240 | tf_op jit(solution)/shard_map/ppermute | solution.py:22
  160.9 3.0 %collective-permute-start.4 = (bf16[2,48,832]{2,1,0:T(8,128)(2,1)S(1)}, bf16[2,48,832]{2,1,0:T(8,128)(2,1)S(1)}, u32[]{:S(2)}, u32[]{:S(2)}) collective-permute-start(bf16[2,48,832]{2,1,0:T(8,128)(2,1)S(1)} %get-tuple-element.18.rounded_ref), channel_id=1, source_target_pairs={{0,15},{1,0},{2,1},{3,2},{4,3},{5,4},{6,5},{7,6},{8,7},{9,8},{10,9... | collective-permute-start | bytes 479240 | tf_op jit(solution)/shard_map/ppermute | solution.py:22
  162.7 7.6 %collective-permute-start.5 = (bf16[2,48,832]{2,1,0:T(8,128)(2,1)S(1)}, bf16[2,48,832]{2,1,0:T(8,128)(2,1)S(1)}, u32[]{:S(2)}, u32[]{:S(2)}) collective-permute-start(bf16[2,48,832]{2,1,0:T(8,128)(2,1)S(1)} %get-tuple-element.20), channel_id=1, source_target_pairs={{0,1},{1,2},{2,3},{3,4},{4,5},{5,6},{6,7},{7,8},{8,9},{9,10},{10,1... | collective-permute-start | bytes 479240 | tf_op jit(solution)/shard_map/ppermute | solution.py:22
  171.1 2.9 %collective-permute-start.6 = (bf16[2,48,832]{2,1,0:T(8,128)(2,1)S(1)}, bf16[2,48,832]{2,1,0:T(8,128)(2,1)S(1)}, u32[]{:S(2)}, u32[]{:S(2)}) collective-permute-start(bf16[2,48,832]{2,1,0:T(8,128)(2,1)S(1)} %get-tuple-element.22.rounded_ref), channel_id=1, source_target_pairs={{0,15},{1,0},{2,1},{3,2},{4,3},{5,4},{6,5},{7,6},{8,7},{9,8},{10,9... | collective-permute-start | bytes 479240 | tf_op jit(solution)/shard_map/ppermute | solution.py:22
  172.8 7.6 %collective-permute-start.7 = (bf16[2,48,832]{2,1,0:T(8,128)(2,1)S(1)}, bf16[2,48,832]{2,1,0:T(8,128)(2,1)S(1)}, u32[]{:S(2)}, u32[]{:S(2)}) collective-permute-start(bf16[2,48,832]{2,1,0:T(8,128)(2,1)S(1)} %get-tuple-element.24), channel_id=1, source_target_pairs={{0,1},{1,2},{2,3},{3,4},{4,5},{5,6},{6,7},{7,8},{8,9},{9,10},{10,1... | collective-permute-start | bytes 479240 | tf_op jit(solution)/shard_map/ppermute | solution.py:22

commit v4 on v3

v4 whole, which is shorter than its diff:
```python
import functools

import jax
import jax.numpy as jnp
from jax import lax
from jax.experimental import pallas as pl
from jax.experimental.pallas import tpu as pltpu
from jax.sharding import PartitionSpec as P

DEGREE = 4
LANES = 128
QUAD = 4
MIB = 2**20
VMEM_WHOLE = pl.BlockSpec(memory_space=pltpu.VMEM)
HBM_WHOLE = pl.BlockSpec(memory_space=pltpu.HBM)
SMEM_WHOLE = pl.BlockSpec(memory_space=pltpu.SMEM)


def passed_along(value, axis, steps):
    count = lax.axis_size(axis)
    pairs = [(source, (source + steps) % count) for source in range(count)]
    return lax.ppermute(value, axis, pairs)


def dot_nn(a, b):
    return lax.dot_general(a, b, (((1,), (0,)), ((), ())), preferred_element_type=jnp.float32)


def dot_nt(a, b):
    return lax.dot_general(a, b, (((1,), (1,)), ((), ())), preferred_element_type=jnp.float32)


def selector(rows, columns, source_of_row):
    row = lax.broadcasted_iota(jnp.int32, (rows, columns), 0)
    column = lax.broadcasted_iota(jnp.int32, (rows, columns), 1)
    return (column == source_of_row(row)).astype(jnp.bfloat16)


def pack_kernel(left, bounds, x_ref, out_ref, x_buf, out_buf, tail_buf, in_sems, out_sems):
    rows, tiles, width = x_buf.shape
    group = tiles // QUAD
    unit = QUAD * QUAD
    steps = rows // QUAD
    full = width // LANES
    half = LANES // 2
    has_tail = width % LANES > 0
    length = steps * unit
    arrivals = []
    for stage, (start, stop) in enumerate(zip(bounds[:-1], bounds[1:])):
        part = pl.ds(start * QUAD, (stop - start) * QUAD)
        arrivals.append(
            pltpu.make_async_copy(x_ref.at[part, :, pl.ds(left, width)], x_buf.at[part], in_sems.at[stage])
        )
        arrivals[-1].start()
    order = selector(QUAD * tiles, QUAD * tiles, lambda o: ((o % unit) // QUAD) * tiles + (o // unit) * QUAD + o % QUAD)
    leaving = []

    def leave(first, count):
        part = pl.ds(first, count)
        copy = pltpu.make_async_copy(out_buf.at[:, part, :], out_ref.at[:, part, :], out_sems.at[len(leaving)])
        copy.start()
        leaving.append(copy)

    begun = 0
    for j in range(steps):
        if j in bounds:
            arrivals[bounds.index(j)].wait()
        data = x_buf[j * QUAD : (j + 1) * QUAD].reshape(QUAD * tiles, width)
        for at in range(0, full * LANES, 2 * LANES):
            wide = min(2 * LANES, full * LANES - at)
            part = dot_nn(order, data[:, at : at + wide]).astype(jnp.bfloat16)
            for k in range(0, wide, LANES):
                first = (at + k) // LANES * length + j * unit
                out_buf[:, first : first + unit, :] = part[:, k : k + LANES].reshape(group, unit, LANES)
        if has_tail:
            last = dot_nn(order, data[:, full * LANES :]).reshape(group, unit, half)
            both = jnp.concatenate([last[:, : unit // 2], last[:, unit // 2 :]], axis=2)
            tail_buf[:, j * unit // 2 : (j + 1) * unit // 2, :] = both
        if j + 1 in bounds:
            for k in range(full):
                leave(k * length + begun * unit, (j + 1 - begun) * unit)
            begun = j + 1
    if has_tail:
        out_buf[:, full * length :, :] = tail_buf[...].astype(jnp.bfloat16)
        leave(full * length, length // 2)
    for copy in leaving:
        copy.wait()


def pack(edge_tiles, left, width):
    tiles, rows, _ = edge_tiles.shape
    group = tiles // QUAD
    turned = jnp.transpose(edge_tiles, (1, 0, 2))
    flat = rows * QUAD * width // LANES
    steps = rows // QUAD
    bounds = tuple(sorted({0, -(-3 * steps // 8), -(-6 * steps // 8), steps}))
    stages = len(bounds) - 1
    return pl.pallas_call(
        functools.partial(pack_kernel, left, bounds),
        out_shape=jax.ShapeDtypeStruct((group, flat, LANES), jnp.bfloat16),
        in_specs=[HBM_WHOLE],
        out_specs=HBM_WHOLE,
        scratch_shapes=[
            pltpu.VMEM((rows, tiles, width), jnp.bfloat16),
            pltpu.VMEM((group, flat, LANES), jnp.bfloat16),
            pltpu.VMEM((group, rows * QUAD // 2, LANES), jnp.float32),
            pltpu.SemaphoreType.DMA((stages,)),
            pltpu.SemaphoreType.DMA((stages * (width // LANES) + 1,)),
        ],
        compiler_params=pltpu.CompilerParams(vmem_limit_bytes=58 * MIB),
        cost_estimate=pl.CostEstimate(
            flops=2 * rows * tiles * width * 4 * tiles, bytes_accessed=4 * rows * tiles * width, transcendentals=0
        ),
        name="pack",
    )(turned)


def unpack_kernel(rows, bounds, from_ref, out_ref, in_ref, sems):
    _, orbs, width = out_ref.shape
    full = width // LANES
    half = LANES // 2
    unit = QUAD * QUAD
    block = 4 * QUAD
    size = block * unit
    span = block * QUAD
    order = selector(size, size, lambda o: (o % span) // QUAD * unit + (o % QUAD) * QUAD + o // span)
    order_tail = selector(
        size, size // 2, lambda o: (o % span) // QUAD * (unit // 2) + (o % QUAD) % 2 * QUAD + o // span
    )
    early = lax.broadcasted_iota(jnp.int32, (size, half), 0) % QUAD < 2
    arrivals = []
    for stage, (start, stop) in enumerate(zip(bounds[:-1], bounds[1:])):
        part = pl.ds(start, stop - start)
        arrivals.append(pltpu.make_async_copy(from_ref.at[part], in_ref.at[part], sems.at[stage]))
        arrivals[-1].start()
    here = 0

    def lane_block(j, start, stop, scale):
        held = rows // scale
        pieces = []
        while start < stop:
            g, at = divmod(start, held)
            count = min(stop - start, held - at)
            pieces.append(in_ref[g, j * rows + at : j * rows + at + count, :])
            start += count
        return pieces[0] if len(pieces) == 1 else jnp.concatenate(pieces, axis=0)

    for i in range(orbs // span):
        while bounds[here] * rows < (i + 1) * size:
            arrivals[here].wait()
            here += 1
        for at in range(0, full, 2):
            wide = range(at, min(at + 2, full))
            data = jnp.concatenate([lane_block(j, i * size, (i + 1) * size, 1) for j in wide], axis=1)
            clean = dot_nn(order, data).astype(jnp.bfloat16)
            for e in range(QUAD):
                place = slice(at * LANES, (at + len(wide)) * LANES)
                out_ref[e, pl.ds(i * span, span), place] = clean[e * span : (e + 1) * span]
        if width % LANES:
            both = dot_nn(order_tail, lane_block(full, i * size // 2, (i + 1) * size // 2, 2))
            last = jnp.where(early, both[:, :half], both[:, half:]).astype(jnp.bfloat16)
            for e in range(QUAD):
                out_ref[e, pl.ds(i * span, span), full * LANES :] = last[e * span : (e + 1) * span]


def unpack(arrived, rows, orbs, width):
    group = arrived.shape[0]
    bounds = tuple(sorted({0, group // 2, group}))
    return pl.pallas_call(
        functools.partial(unpack_kernel, rows * QUAD, bounds),
        out_shape=jax.ShapeDtypeStruct((QUAD, orbs, width), jnp.bfloat16),
        in_specs=[HBM_WHOLE],
        out_specs=VMEM_WHOLE,
        scratch_shapes=[pltpu.VMEM(arrived.shape, arrived.dtype), pltpu.SemaphoreType.DMA((len(bounds) - 1,))],
        compiler_params=pltpu.CompilerParams(vmem_limit_bytes=20 * MIB),
        cost_estimate=pl.CostEstimate(
            flops=2 * QUAD * orbs * width * 256, bytes_accessed=4 * QUAD * orbs * width, transcendentals=0
        ),
        name="unpack",
    )(arrived)


def product_cost(parts, vecs):
    size = sum(part.size for part in parts)
    return pl.CostEstimate(flops=2 * size * vecs * 4, bytes_accessed=2 * size, transcendentals=0)


def turned_kernel(count, target_ref, rounded_ref, *refs):
    parts, early, (own_ref, send_ref, acc_ref) = refs[:count], refs[count:-3], refs[-3:]
    blk_dev = rounded_ref.shape[0]
    at = 0
    if early:
        at = early[0].shape[2]
        own_ref[:, :, :at] = early[0][...]
        send_ref[:, :, :at] = early[1][...]
    left = at
    acc_ref[...] = jnp.zeros_like(acc_ref)
    for part in parts:
        edges, _, width = part.shape
        for e in range(edges):
            acc_ref[target_ref[e], :, left : left + width] += dot_nn(rounded_ref[e * blk_dev // edges], part[e])
        left += width
    own_ref[:, :, at:] = acc_ref[:blk_dev, :, at:]
    send_ref[:, :, at:] = acc_ref[blk_dev:, :, at:].astype(jnp.bfloat16)


def turned_terms(target, rounded, parts, early=()):
    blk_dev, vecs, _ = rounded.shape
    shape = (blk_dev, vecs, sum(part.shape[2] for part in [*early[:1], *parts]))
    return pl.pallas_call(
        functools.partial(turned_kernel, len(parts)),
        out_shape=(jax.ShapeDtypeStruct(shape, jnp.float32), jax.ShapeDtypeStruct(shape, jnp.bfloat16)),
        in_specs=[SMEM_WHOLE] + [VMEM_WHOLE] * (1 + len(parts) + len(early)),
        out_specs=(VMEM_WHOLE, VMEM_WHOLE),
        scratch_shapes=[pltpu.VMEM((2 * blk_dev, *shape[1:]), jnp.float32)],
        compiler_params=pltpu.CompilerParams(vmem_limit_bytes=16 * MIB),
        cost_estimate=product_cost(parts, vecs),
        name="turned",
    )(target, rounded, *parts, *early)


def direct_kernel(target_ref, rounded_ref, following_ref, own_ref, *refs):
    mirrors, (out_ref, picked_ref) = refs[:-2], refs[-2:]
    blk_dev = rounded_ref.shape[0]
    edges = mirrors[0].shape[0]
    slots = edges // blk_dev
    picked_ref[:blk_dev] = rounded_ref[...]
    picked_ref[blk_dev:] = following_ref[...]
    for b in range(blk_dev):
        total = own_ref[b]
        for e in range(b * slots, (b + 1) * slots):
            left = 0
            for mirror in mirrors:
                width = mirror.shape[1]
                total += dot_nn(picked_ref[target_ref[e], :, left : left + width], mirror[e])
                left += width
        out_ref[b] = total


def direct_terms(target, rounded, following, own, mirrors):
    blk_dev, vecs, orbs = rounded.shape
    return pl.pallas_call(
        direct_kernel,
        out_shape=jax.ShapeDtypeStruct(rounded.shape, jnp.float32),
        in_specs=[SMEM_WHOLE] + [VMEM_WHOLE] * (3 + len(mirrors)),
        out_specs=VMEM_WHOLE,
        scratch_shapes=[pltpu.VMEM((2 * blk_dev, vecs, orbs), jnp.bfloat16)],
        compiler_params=pltpu.CompilerParams(vmem_limit_bytes=16 * MIB),
        cost_estimate=product_cost(mirrors, vecs),
        name="direct",
    )(target, rounded, following, own, *mirrors)


def mirror_kernel(tiles_ref, after_ref, out_ref):
    for e in range(tiles_ref.shape[0]):
        out_ref[e] = tiles_ref[e].T


def mirrored(tiles, after):
    edges, rows, width = tiles.shape
    return pl.pallas_call(
        mirror_kernel,
        out_shape=jax.ShapeDtypeStruct((edges, width, rows), tiles.dtype),
        in_specs=[VMEM_WHOLE, pl.BlockSpec(memory_space=pl.ANY)],
        out_specs=VMEM_WHOLE,
        compiler_params=pltpu.CompilerParams(vmem_limit_bytes=16 * MIB),
        cost_estimate=pl.CostEstimate(flops=tiles.size * 400, bytes_accessed=4 * tiles.size, transcendentals=0),
        name="mirror",
    )(tiles, after)


def rounded_kernel(direct_ref, arrive_ref, previous_ref, rounded_ref):
    panel = 2.0 * (direct_ref[...] + arrive_ref[...].astype(jnp.float32)) - previous_ref[...]
    rounded_ref[...] = panel.astype(jnp.bfloat16)


def rounded_update(direct, arrive, previous):
    return pl.pallas_call(
        rounded_kernel,
        out_shape=jax.ShapeDtypeStruct(direct.shape, jnp.bfloat16),
        in_specs=[VMEM_WHOLE] * 3,
        out_specs=VMEM_WHOLE,
        compiler_params=pltpu.CompilerParams(vmem_limit_bytes=16 * MIB),
        name="rounded",
    )(direct, arrive, previous)


def exchanged(tiles):
    return lax.all_to_all(tiles, "gx", split_axis=0, concat_axis=0, tiled=True)


def per_device(edge_tiles, trial_panel, col_blocks):
    blk_dev, _, orbs = trial_panel.shape
    tiles, rows, _ = edge_tiles.shape
    group = lax.axis_size("gx")
    block_total = blk_dev * group
    domain = lax.axis_index("gx")
    own_cols = lax.dynamic_slice_in_dim(col_blocks, domain * blk_dev, blk_dev, 0).reshape(-1)
    target = jnp.mod(own_cols - domain * blk_dev, block_total)
    rounded = trial_panel.astype(jnp.bfloat16)
    fits = tiles // group == QUAD and rows % QUAD == 0
    if fits and orbs % LANES == LANES // 2 and orbs % (4 * QUAD * QUAD) == 0:
        cuts = [(0, orbs)]
        parts = [unpack(exchanged(pack(edge_tiles, *cut)), rows, orbs, cut[1]) for cut in cuts]
    else:
        parts = [lax.all_to_all(edge_tiles, "gx", split_axis=0, concat_axis=1, tiled=True)]
    early = turned_terms(target, rounded, parts[:1]) if len(parts) > 1 else ()
    mirrors = [mirrored(part, early[1]) for part in parts[:-1]]

    previous, current = None, trial_panel
    for k in range(DEGREE):
        following = passed_along(rounded, "gx", -1)
        if k == 0:
            own, send = turned_terms(target, rounded, parts[len(parts) - 1 :], early)
            mirrors.append(mirrored(parts[-1], send))
        else:
            own, send = turned_terms(target, rounded, parts)
        arrive = passed_along(send, "gx", 1)
        direct = direct_terms(target, rounded, following, own, mirrors)
        if k == 0:
            total = direct + arrive.astype(jnp.float32)
            rounded = total.astype(jnp.bfloat16)
        else:
            if k == DEGREE - 2:
                rounded = rounded_update(direct, arrive, previous)
                direct, arrive, previous, rounded = lax.optimization_barrier((direct, arrive, previous, rounded))
            total = 2.0 * (direct + arrive.astype(jnp.float32)) - previous
            if k < DEGREE - 2:
                rounded = total.astype(jnp.bfloat16)
        previous, current = current, total
    return previous, current


def solution(mesh):
    return jax.shard_map(
        per_device,
        mesh=mesh,
        in_specs=(P("member", "gx", None), P(("member", "gx"), None, None), P()),
        out_specs=(P(("member", "gx"), None, None), P(("member", "gx"), None, None)),
        check_vma=False,
    )
```

time: 181 us -> 179 us (0.989)
  Pallas kernels: 27 us -> 24.1 us
    pallas_call x9 -> x8, Pallas kernels: 20.7 us -> 17.7 us  [the longest x4 6.64 us: turned_terms(): pl.pallas_call(functools.partial(turned_kernel, len(parts)), out_shape=(j...]
  transfers between devices with their start and end apart: 9 -> 9, of which waited for: 8 -> 8; matrix products, arithmetic and copies ran while one was open for 0% -> 1% of each run, Pallas kernels for 10% -> 9%
where the time goes in v4:
time: 179 us; the launch traced here: 178 us
  waiting for transfers between devices  137 us (77%)
  Pallas kernels  24.1 us (13%)
  starting transfers between devices  14.7 us (8%)
  other arithmetic  1.88 us (1%)
    all_to_all x1, waiting for transfers between devices, exchanged(): return lax.all_to_all(tiles, 'gx', split_axis=0, concat_axis=0, tiled=True)  96.4 us
    ppermute x8, waiting for transfers between devices, passed_along(): return lax.ppermute(value, axis, pairs)  40.3 us
    all_to_all x1, starting transfers between devices, exchanged(): return lax.all_to_all(tiles, 'gx', split_axis=0, concat_axis=0, tiled=True)  7.58 us
    ppermute x8, starting transfers between devices, passed_along(): return lax.ppermute(value, axis, pairs)  7.17 us
    pallas_call x4, Pallas kernels, turned_terms(): pl.pallas_call(functools.partial(turned_kernel, len(parts)), out_shape=(j...  6.64 us
    pallas_call x4, Pallas kernels, direct_terms(): pl.pallas_call(direct_kernel, out_shape=jax.ShapeDtypeStruct(rounded.shap...  6.36 us
    pallas_call x1, Pallas kernels, pack(): pl.pallas_call(functools.partial(pack_kernel, left, bounds), out_shape=ja...  5.51 us
    pallas_call x1, Pallas kernels, unpack(): pl.pallas_call(functools.partial(unpack_kernel, rows * QUAD, bounds), out...  3.8 us
  transfers between devices with their start and end apart: 9, of which 8 were waited for; matrix products, arithmetic and copies ran while one was open for 1% of the time, Pallas kernels for 9%

profile of v4, /device:TPU:0, one launch (start us, length us, event | category | flops | bytes accessed | tf_op | source)
XLA Modules:
  0.0 178.4 jit_solution(12794462150721784463)
XLA Ops:
  0.6 5.5 %pack.1 = bf16[16,1352,128]{2,1,0:T(8,128)(2,1)} custom-call(bf16[52,64,832]{2,1,0:T(8,128)(2,1)} %bitcast.1), custom_call_target="tpu_custom_call" | custom-call | flops 1417674752 | bytes 11075584 | tf_op jit(solution)/shard_map/pack/pallas_call | solution.py:98
  6.2 7.6 %all-to-all-start = ((bf16[16,1352,128]{2,1,0:T(8,128)(2,1)}), bf16[16,1352,128]{2,1,0:T(8,128)(2,1)}, u32[]{:S(2)}, u32[]{:S(2)}) async-start(bf16[16,1352,128]{2,1,0:T(8,128)(2,1)} %pack.1), calls=%async_computation | async-start | bytes 11075584 | tf_op jit(solution)/shard_map/all_to_all | solution.py:289
  13.8 4.4 %collective-permute-start = (bf16[2,48,832]{2,1,0:T(8,128)(2,1)S(1)}, bf16[2,48,832]{2,1,0:T(8,128)(2,1)S(1)}, u32[]{:S(2)}, u32[]{:S(2)}) collective-permute-start(bf16[2,48,832]{2,1,0:T(8,128)(2,1)S(1)} %convert_element_type.21.rounded_ref), channel_id=1, source_target_pairs={{0,15},{1,0},{2,1},{3,2},{4,3},{5,4},{6,5},{7,6},{8,7},{9,8},{10,9... | collective-permute-start | bytes 479240 | tf_op jit(solution)/shard_map/ppermute | solution.py:22
  18.2 0.1 dynamic-slice_subtract_fusion
  18.3 0.1 copy.5
  18.4 0.1 sub.20
  18.4 96.4 %all-to-all-done.from_ref = bf16[16,1352,128]{2,1,0:T(8,128)(2,1)} async-done(((bf16[16,1352,128]{2,1,0:T(8,128)(2,1)}), bf16[16,1352,128]{2,1,0:T(8,128)(2,1)}, u32[]{:S(2)}, u32[]{:S(2)}) %all-to-all-start) | async-done | bytes 5537824 | tf_op jit(solution)/shard_map/all_to_all | solution.py:289
  114.9 3.8 %unpack.1.refs_0_.tiles_ref = bf16[4,832,832]{2,1,0:T(8,128)(2,1)S(1)} custom-call(bf16[16,1352,128]{2,1,0:T(8,128)(2,1)} %all-to-all-done.from_ref), custom_call_target="tpu_custom_call" | custom-call | flops 1417674752 | bytes 11075584 | tf_op jit(solution)/shard_map/unpack/pallas_call | solution.py:169
  118.7 1.7 turned.4
  120.4 0.8 collective-permute-start.1
  121.2 1.7 mirror.1.refs_0_
  122.9 1.6 direct.4
  124.5 24.4 %collective-permute-done.1 = bf16[2,48,832]{2,1,0:T(8,128)(2,1)S(1)} collective-permute-done((bf16[2,48,832]{2,1,0:T(8,128)(2,1)S(1)}, bf16[2,48,832]{2,1,0:T(8,128)(2,1)S(1)}, u32[]{:S(2)}, u32[]{:S(2)}) %collective-permute-start.1) | collective-permute-done | bytes 159776 | tf_op jit(solution)/shard_map/ppermute | solution.py:22
  148.9 0.3 collective-permute-start.2
  149.2 1.7 turned.5
  150.9 0.3 collective-permute-start.3
  151.2 0.9 collective-permute-done.2.following_ref
  152.2 1.6 direct.5
  153.7 4.8 %collective-permute-done.3 = bf16[2,48,832]{2,1,0:T(8,128)(2,1)S(1)} collective-permute-done((bf16[2,48,832]{2,1,0:T(8,128)(2,1)S(1)}, bf16[2,48,832]{2,1,0:T(8,128)(2,1)S(1)}, u32[]{:S(2)}, u32[]{:S(2)}) %collective-permute-start.3) | collective-permute-done | bytes 159776 | tf_op jit(solution)/shard_map/ppermute | solution.py:22
  158.7 1.7 turned.6
  160.4 0.7 collective-permute-start.5
  161.1 0.5 collective-permute-done.4.following_ref
  161.6 1.6 direct.6.direct_ref
  163.2 4.9 %collective-permute-done.5.arrive_ref = bf16[2,48,832]{2,1,0:T(8,128)(2,1)S(1)} collective-permute-done((bf16[2,48,832]{2,1,0:T(8,128)(2,1)S(1)}, bf16[2,48,832]{2,1,0:T(8,128)(2,1)S(1)}, u32[]{:S(2)}, u32[]{:S(2)}) %collective-permute-start.5) | collective-permute-done | bytes 159776 | tf_op jit(solution)/shard_map/ppermute | solution.py:22
  168.1 0.1 rounded.1.rounded_ref
  168.2 1.7 turned.7
  169.9 0.5 collective-permute-start.7
  170.4 0.8 multiply_subtract_fusion.1
  171.2 1.6 collective-permute-done.6.following_ref
  172.9 1.6 direct.7
  174.5 3.1 %collective-permute-done.7 = bf16[2,48,832]{2,1,0:T(8,128)(2,1)S(1)} collective-permute-done((bf16[2,48,832]{2,1,0:T(8,128)(2,1)S(1)}, bf16[2,48,832]{2,1,0:T(8,128)(2,1)S(1)}, u32[]{:S(2)}, u32[]{:S(2)}) %collective-permute-start.7) | collective-permute-done | bytes 159776 | tf_op jit(solution)/shard_map/ppermute | solution.py:22
  177.5 0.8 multiply_subtract_fusion
  (11 shorter events, 0.3 us)
Async XLA Ops:
  6.1 7.6 %copy-start = (f32[2,48,832]{2,1,0:T(8,128)S(1)}, f32[2,48,832]{2,1,0:T(8,128)}, u32[]{:S(2)}) copy-start(f32[2,48,832]{2,1,0:T(8,128)} %param.4) | copy-start | bytes 958468
  6.2 12.0 %copy-start.1 = (s32[32,2]{0,1:T(2,128)S(1)}, s32[32,2]{0,1:T(2,128)}, u32[]{:S(2)}) copy-start(s32[32,2]{0,1:T(2,128)} %param.5) | copy-start | bytes 772
  6.2 108.7 %all-to-all-start = ((bf16[16,1352,128]{2,1,0:T(8,128)(2,1)}), bf16[16,1352,128]{2,1,0:T(8,128)(2,1)}, u32[]{:S(2)}, u32[]{:S(2)}) async-start(bf16[16,1352,128]{2,1,0:T(8,128)(2,1)} %pack.1), calls=%async_computation | async-start | bytes 11075584 | tf_op jit(solution)/shard_map/all_to_all | solution.py:289
  13.8 109.1 %collective-permute-start = (bf16[2,48,832]{2,1,0:T(8,128)(2,1)S(1)}, bf16[2,48,832]{2,1,0:T(8,128)(2,1)S(1)}, u32[]{:S(2)}, u32[]{:S(2)}) collective-permute-start(bf16[2,48,832]{2,1,0:T(8,128)(2,1)S(1)} %convert_element_type.21.rounded_ref), channel_id=1, source_target_pairs={{0,15},{1,0},{2,1},{3,2},{4,3},{5,4},{6,5},{7,6},{8,7},{9,8},{10,9... | collective-permute-start | bytes 479240 | tf_op jit(solution)/shard_map/ppermute | solution.py:22
  120.4 28.5 %collective-permute-start.1 = (bf16[2,48,832]{2,1,0:T(8,128)(2,1)S(1)}, bf16[2,48,832]{2,1,0:T(8,128)(2,1)S(1)}, u32[]{:S(2)}, u32[]{:S(2)}) collective-permute-start(bf16[2,48,832]{2,1,0:T(8,128)(2,1)S(1)} %get-tuple-element.15.after_ref), channel_id=1, source_target_pairs={{0,1},{1,2},{2,3},{3,4},{4,5},{5,6},{6,7},{7,8},{8,9},{9,10},{10,1... | collective-permute-start | bytes 479240 | tf_op jit(solution)/shard_map/ppermute | solution.py:22
  148.9 3.2 %collective-permute-start.2 = (bf16[2,48,832]{2,1,0:T(8,128)(2,1)S(1)}, bf16[2,48,832]{2,1,0:T(8,128)(2,1)S(1)}, u32[]{:S(2)}, u32[]{:S(2)}) collective-permute-start(bf16[2,48,832]{2,1,0:T(8,128)(2,1)S(1)} %get-tuple-element.26.rounded_ref), channel_id=1, source_target_pairs={{0,15},{1,0},{2,1},{3,2},{4,3},{5,4},{6,5},{7,6},{8,7},{9,8},{10,9... | collective-permute-start | bytes 479240 | tf_op jit(solution)/shard_map/ppermute | solution.py:22
  150.9 7.7 %collective-permute-start.3 = (bf16[2,48,832]{2,1,0:T(8,128)(2,1)S(1)}, bf16[2,48,832]{2,1,0:T(8,128)(2,1)S(1)}, u32[]{:S(2)}, u32[]{:S(2)}) collective-permute-start(bf16[2,48,832]{2,1,0:T(8,128)(2,1)S(1)} %get-tuple-element.17), channel_id=1, source_target_pairs={{0,1},{1,2},{2,3},{3,4},{4,5},{5,6},{6,7},{7,8},{8,9},{9,10},{10,1... | collective-permute-start | bytes 479240 | tf_op jit(solution)/shard_map/ppermute | solution.py:22
  158.6 3.0 %collective-permute-start.4 = (bf16[2,48,832]{2,1,0:T(8,128)(2,1)S(1)}, bf16[2,48,832]{2,1,0:T(8,128)(2,1)S(1)}, u32[]{:S(2)}, u32[]{:S(2)}) collective-permute-start(bf16[2,48,832]{2,1,0:T(8,128)(2,1)S(1)} %fusion.rounded_ref), channel_id=1, source_target_pairs={{0,15},{1,0},{2,1},{3,2},{4,3},{5,4},{6,5},{7,6},{8,7},{9,8},{10,9... | collective-permute-start | bytes 479240 | tf_op jit(solution)/shard_map/ppermute | solution.py:22
  160.4 7.8 %collective-permute-start.5 = (bf16[2,48,832]{2,1,0:T(8,128)(2,1)S(1)}, bf16[2,48,832]{2,1,0:T(8,128)(2,1)S(1)}, u32[]{:S(2)}, u32[]{:S(2)}) collective-permute-start(bf16[2,48,832]{2,1,0:T(8,128)(2,1)S(1)} %get-tuple-element.19), channel_id=1, source_target_pairs={{0,1},{1,2},{2,3},{3,4},{4,5},{5,6},{6,7},{7,8},{8,9},{9,10},{10,1... | collective-permute-start | bytes 479240 | tf_op jit(solution)/shard_map/ppermute | solution.py:22
  169.9 3.0 %collective-permute-start.6 = (bf16[2,48,832]{2,1,0:T(8,128)(2,1)S(1)}, bf16[2,48,832]{2,1,0:T(8,128)(2,1)S(1)}, u32[]{:S(2)}, u32[]{:S(2)}) collective-permute-start(bf16[2,48,832]{2,1,0:T(8,128)(2,1)S(1)} %rounded.1.rounded_ref), channel_id=1, source_target_pairs={{0,15},{1,0},{2,1},{3,2},{4,3},{5,4},{6,5},{7,6},{8,7},{9,8},{10,9... | collective-permute-start | bytes 479240 | tf_op jit(solution)/shard_map/ppermute | solution.py:22
  169.9 7.6 %collective-permute-start.7 = (bf16[2,48,832]{2,1,0:T(8,128)(2,1)S(1)}, bf16[2,48,832]{2,1,0:T(8,128)(2,1)S(1)}, u32[]{:S(2)}, u32[]{:S(2)}) collective-permute-start(bf16[2,48,832]{2,1,0:T(8,128)(2,1)S(1)} %get-tuple-element.25), channel_id=1, source_target_pairs={{0,1},{1,2},{2,3},{3,4},{4,5},{5,6},{6,7},{7,8},{8,9},{9,10},{10,1... | collective-permute-start | bytes 479240 | tf_op jit(solution)/shard_map/ppermute | solution.py:22

commit v5 on v4

--- a/solution.py
+++ b/solution.py
@@ -13,7 +13,7 @@
 MIB = 2**20
 VMEM_WHOLE = pl.BlockSpec(memory_space=pltpu.VMEM)
 HBM_WHOLE = pl.BlockSpec(memory_space=pltpu.HBM)
-SMEM_WHOLE = pl.BlockSpec(memory_space=pltpu.SMEM)
+SUBLANES = 8
 
 
 def passed_along(value, axis, steps):
@@ -187,6 +187,7 @@
 
 def turned_kernel(count, target_ref, rounded_ref, *refs):
     parts, early, (own_ref, send_ref, acc_ref) = refs[:count], refs[count:-3], refs[-3:]
+    targets = [target_ref[...][e, 0] for e in range(parts[0].shape[0])]
     blk_dev = rounded_ref.shape[0]
     at = 0
     if early:
@@ -198,7 +199,7 @@
     for part in parts:
         edges, _, width = part.shape
         for e in range(edges):
-            acc_ref[target_ref[e], :, left : left + width] += dot_nn(rounded_ref[e * blk_dev // edges], part[e])
+            acc_ref[targets[e], :, left : left + width] += dot_nn(rounded_ref[e * blk_dev // edges], part[e])
         left += width
     own_ref[:, :, at:] = acc_ref[:blk_dev, :, at:]
     send_ref[:, :, at:] = acc_ref[blk_dev:, :, at:].astype(jnp.bfloat16)
@@ -210,7 +211,7 @@
     return pl.pallas_call(
         functools.partial(turned_kernel, len(parts)),
         out_shape=(jax.ShapeDtypeStruct(shape, jnp.float32), jax.ShapeDtypeStruct(shape, jnp.bfloat16)),
-        in_specs=[SMEM_WHOLE] + [VMEM_WHOLE] * (1 + len(parts) + len(early)),
+        in_specs=[VMEM_WHOLE] + [VMEM_WHOLE] * (1 + len(parts) + len(early)),
         out_specs=(VMEM_WHOLE, VMEM_WHOLE),
         scratch_shapes=[pltpu.VMEM((2 * blk_dev, *shape[1:]), jnp.float32)],
         compiler_params=pltpu.CompilerParams(vmem_limit_bytes=16 * MIB),
@@ -221,6 +222,7 @@
 
 def direct_kernel(target_ref, rounded_ref, following_ref, own_ref, *refs):
     mirrors, (out_ref, picked_ref) = refs[:-2], refs[-2:]
+    targets = [target_ref[...][e, 0] for e in range(mirrors[0].shape[0])]
     blk_dev = rounded_ref.shape[0]
     edges = mirrors[0].shape[0]
     slots = edges // blk_dev
@@ -232,7 +234,7 @@
             left = 0
             for mirror in mirrors:
                 width = mirror.shape[1]
-                total += dot_nn(picked_ref[target_ref[e], :, left : left + width], mirror[e])
+                total += dot_nn(picked_ref[targets[e], :, left : left + width], mirror[e])
                 left += width
         out_ref[b] = total
 
@@ -242,7 +244,7 @@
     return pl.pallas_call(
         direct_kernel,
         out_shape=jax.ShapeDtypeStruct(rounded.shape, jnp.float32),
-        in_specs=[SMEM_WHOLE] + [VMEM_WHOLE] * (3 + len(mirrors)),
+        in_specs=[VMEM_WHOLE] + [VMEM_WHOLE] * (3 + len(mirrors)),
         out_specs=VMEM_WHOLE,
         scratch_shapes=[pltpu.VMEM((2 * blk_dev, vecs, orbs), jnp.bfloat16)],
         compiler_params=pltpu.CompilerParams(vmem_limit_bytes=16 * MIB),
@@ -297,6 +299,8 @@
     domain = lax.axis_index("gx")
     own_cols = lax.dynamic_slice_in_dim(col_blocks, domain * blk_dev, blk_dev, 0).reshape(-1)
     target = jnp.mod(own_cols - domain * blk_dev, block_total)
+    padded = jnp.pad(target, (0, -target.size % SUBLANES))
+    target = jnp.broadcast_to(padded[:, None], (padded.size, LANES))
     rounded = trial_panel.astype(jnp.bfloat16)
     fits = tiles // group == QUAD and rows % QUAD == 0
     if fits and orbs % LANES == LANES // 2 and orbs % (4 * QUAD * QUAD) == 0:

time: 179 us -> 176 us (0.983)
  Pallas kernels: 24.1 us -> 20 us
  waiting for transfers between devices: 137 us -> 139 us
    pallas_call x4, Pallas kernels: 6.36 us -> 4.25 us  [direct_terms(): pl.pallas_call(direct_kernel, out_shape=jax.ShapeDtypeStruct(rounded.shap...]
    pallas_call x4, Pallas kernels: 6.64 us -> 4.71 us  [turned_terms(): pl.pallas_call(functools.partial(turned_kernel, len(parts)), out_shape=(j...]
    ppermute x8, waiting for transfers between devices: 40.3 us -> 42.1 us  [passed_along(): return lax.ppermute(value, axis, pairs)]
  transfers between devices with their start and end apart: 9 -> 9, of which waited for: 8 -> 8; matrix products, arithmetic and copies ran while one was open for 1% -> 1% of each run, Pallas kernels for 9% -> 8%
where the time goes in v5:
time: 176 us
  waiting for transfers between devices  139 us (79%)
  Pallas kernels  20 us (11%)
  starting transfers between devices  14.7 us (8%)
  other arithmetic  1.87 us (1%)
    all_to_all x1, waiting for transfers between devices, exchanged(): return lax.all_to_all(tiles, 'gx', split_axis=0, concat_axis=0, tiled=True)  96.4 us
    ppermute x8, waiting for transfers between devices, passed_along(): return lax.ppermute(value, axis, pairs)  42.1 us
    all_to_all x1, starting transfers between devices, exchanged(): return lax.all_to_all(tiles, 'gx', split_axis=0, concat_axis=0, tiled=True)  7.58 us
    ppermute x8, starting transfers between devices, passed_along(): return lax.ppermute(value, axis, pairs)  7.15 us
    pallas_call x1, Pallas kernels, pack(): pl.pallas_call(functools.partial(pack_kernel, left, bounds), out_shape=ja...  5.51 us
    pallas_call x4, Pallas kernels, turned_terms(): pl.pallas_call(functools.partial(turned_kernel, len(parts)), out_shape=(j...  4.71 us
    pallas_call x4, Pallas kernels, direct_terms(): pl.pallas_call(direct_kernel, out_shape=jax.ShapeDtypeStruct(rounded.shap...  4.25 us
    pallas_call x1, Pallas kernels, unpack(): pl.pallas_call(functools.partial(unpack_kernel, rows * QUAD, bounds), out...  3.8 us
  transfers between devices with their start and end apart: 9, of which 8 were waited for; matrix products, arithmetic and copies ran while one was open for 1% of the time, Pallas kernels for 8%

profile of v5, /device:TPU:0, one launch (start us, length us, event | category | flops | bytes accessed | tf_op | source)
XLA Modules:
  0.0 176.2 jit_solution(15042151705637476737)
XLA Ops:
  0.6 5.5 %pack.1 = bf16[16,1352,128]{2,1,0:T(8,128)(2,1)} custom-call(bf16[52,64,832]{2,1,0:T(8,128)(2,1)} %bitcast.1), custom_call_target="tpu_custom_call" | custom-call | flops 1417674752 | bytes 11075584 | tf_op jit(solution)/shard_map/pack/pallas_call | solution.py:98
  6.2 7.6 %all-to-all-start = ((bf16[16,1352,128]{2,1,0:T(8,128)(2,1)}), bf16[16,1352,128]{2,1,0:T(8,128)(2,1)}, u32[]{:S(2)}, u32[]{:S(2)}) async-start(bf16[16,1352,128]{2,1,0:T(8,128)(2,1)} %pack.1), calls=%async_computation | async-start | bytes 11075584 | tf_op jit(solution)/shard_map/all_to_all | solution.py:291
  13.8 4.4 %collective-permute-start = (bf16[2,48,832]{2,1,0:T(8,128)(2,1)S(1)}, bf16[2,48,832]{2,1,0:T(8,128)(2,1)S(1)}, u32[]{:S(2)}, u32[]{:S(2)}) collective-permute-start(bf16[2,48,832]{2,1,0:T(8,128)(2,1)S(1)} %convert_element_type.21.rounded_ref), channel_id=1, source_target_pairs={{0,15},{1,0},{2,1},{3,2},{4,3},{5,4},{6,5},{7,6},{8,7},{9,8},{10,9... | collective-permute-start | bytes 479240 | tf_op jit(solution)/shard_map/ppermute | solution.py:22
  18.2 0.1 dynamic-slice_subtract_fusion
  18.3 0.1 copy.5
  18.4 0.1 sub.20
  18.5 96.4 %all-to-all-done.from_ref = bf16[16,1352,128]{2,1,0:T(8,128)(2,1)} async-done(((bf16[16,1352,128]{2,1,0:T(8,128)(2,1)}), bf16[16,1352,128]{2,1,0:T(8,128)(2,1)}, u32[]{:S(2)}, u32[]{:S(2)}) %all-to-all-start) | async-done | bytes 5537824 | tf_op jit(solution)/shard_map/all_to_all | solution.py:291
  114.9 3.8 %unpack.1.refs_0_.tiles_ref = bf16[4,832,832]{2,1,0:T(8,128)(2,1)S(1)} custom-call(bf16[16,1352,128]{2,1,0:T(8,128)(2,1)} %all-to-all-done.from_ref), custom_call_target="tpu_custom_call" | custom-call | flops 1417674752 | bytes 11075584 | tf_op jit(solution)/shard_map/unpack/pallas_call | solution.py:169
  118.7 0.1 broadcast_in_dim.2.target_ref
  118.8 1.2 turned.4
  119.9 0.8 collective-permute-start.1
  120.8 1.7 mirror.1.refs_0_
  122.5 1.1 direct.4
  123.5 24.9 %collective-permute-done.1 = bf16[2,48,832]{2,1,0:T(8,128)(2,1)S(1)} collective-permute-done((bf16[2,48,832]{2,1,0:T(8,128)(2,1)S(1)}, bf16[2,48,832]{2,1,0:T(8,128)(2,1)S(1)}, u32[]{:S(2)}, u32[]{:S(2)}) %collective-permute-start.1) | collective-permute-done | bytes 159776 | tf_op jit(solution)/shard_map/ppermute | solution.py:22
  148.6 1.2 turned.5
  149.7 0.5 collective-permute-start.3
  150.3 1.2 collective-permute-done.2.following_ref
  151.5 1.1 direct.5
  152.5 4.8 %collective-permute-done.3 = bf16[2,48,832]{2,1,0:T(8,128)(2,1)S(1)} collective-permute-done((bf16[2,48,832]{2,1,0:T(8,128)(2,1)S(1)}, bf16[2,48,832]{2,1,0:T(8,128)(2,1)S(1)}, u32[]{:S(2)}, u32[]{:S(2)}) %collective-permute-start.3) | collective-permute-done | bytes 159776 | tf_op jit(solution)/shard_map/ppermute | solution.py:22
  157.5 1.2 turned.6
  158.7 0.7 collective-permute-start.5
  159.4 1.0 collective-permute-done.4.following_ref
  160.4 1.1 direct.6.direct_ref
  161.5 5.0 %collective-permute-done.5.arrive_ref = bf16[2,48,832]{2,1,0:T(8,128)(2,1)S(1)} collective-permute-done((bf16[2,48,832]{2,1,0:T(8,128)(2,1)S(1)}, bf16[2,48,832]{2,1,0:T(8,128)(2,1)S(1)}, u32[]{:S(2)}, u32[]{:S(2)}) %collective-permute-start.5) | collective-permute-done | bytes 159776 | tf_op jit(solution)/shard_map/ppermute | solution.py:22
  166.5 0.1 rounded.1.rounded_ref
  166.5 1.2 turned.7
  167.8 0.5 collective-permute-start.7
  168.3 0.8 multiply_subtract_fusion.1
  169.1 1.6 collective-permute-done.6.following_ref
  170.7 1.1 direct.7
  171.8 3.6 %collective-permute-done.7 = bf16[2,48,832]{2,1,0:T(8,128)(2,1)S(1)} collective-permute-done((bf16[2,48,832]{2,1,0:T(8,128)(2,1)S(1)}, bf16[2,48,832]{2,1,0:T(8,128)(2,1)S(1)}, u32[]{:S(2)}, u32[]{:S(2)}) %collective-permute-start.7) | collective-permute-done | bytes 159776 | tf_op jit(solution)/shard_map/ppermute | solution.py:22
  175.4 0.9 multiply_subtract_fusion
  (13 shorter events, 0.3 us)
Async XLA Ops:
  6.1 7.6 %copy-start = (f32[2,48,832]{2,1,0:T(8,128)S(1)}, f32[2,48,832]{2,1,0:T(8,128)}, u32[]{:S(2)}) copy-start(f32[2,48,832]{2,1,0:T(8,128)} %param.4) | copy-start | bytes 958468
  6.2 12.0 %copy-start.1 = (s32[32,2]{0,1:T(2,128)S(1)}, s32[32,2]{0,1:T(2,128)}, u32[]{:S(2)}) copy-start(s32[32,2]{0,1:T(2,128)} %param.5) | copy-start | bytes 772
  6.2 108.7 %all-to-all-start = ((bf16[16,1352,128]{2,1,0:T(8,128)(2,1)}), bf16[16,1352,128]{2,1,0:T(8,128)(2,1)}, u32[]{:S(2)}, u32[]{:S(2)}) async-start(bf16[16,1352,128]{2,1,0:T(8,128)(2,1)} %pack.1), calls=%async_computation | async-start | bytes 11075584 | tf_op jit(solution)/shard_map/all_to_all | solution.py:291
  13.8 108.7 %collective-permute-start = (bf16[2,48,832]{2,1,0:T(8,128)(2,1)S(1)}, bf16[2,48,832]{2,1,0:T(8,128)(2,1)S(1)}, u32[]{:S(2)}, u32[]{:S(2)}) collective-permute-start(bf16[2,48,832]{2,1,0:T(8,128)(2,1)S(1)} %convert_element_type.21.rounded_ref), channel_id=1, source_target_pairs={{0,15},{1,0},{2,1},{3,2},{4,3},{5,4},{6,5},{7,6},{8,7},{9,8},{10,9... | collective-permute-start | bytes 479240 | tf_op jit(solution)/shard_map/ppermute | solution.py:22
  119.9 28.5 %collective-permute-start.1 = (bf16[2,48,832]{2,1,0:T(8,128)(2,1)S(1)}, bf16[2,48,832]{2,1,0:T(8,128)(2,1)S(1)}, u32[]{:S(2)}, u32[]{:S(2)}) collective-permute-start(bf16[2,48,832]{2,1,0:T(8,128)(2,1)S(1)} %get-tuple-element.15.after_ref), channel_id=1, source_target_pairs={{0,1},{1,2},{2,3},{3,4},{4,5},{5,6},{6,7},{7,8},{8,9},{9,10},{10,1... | collective-permute-start | bytes 479240 | tf_op jit(solution)/shard_map/ppermute | solution.py:22
  148.5 3.0 %collective-permute-start.2 = (bf16[2,48,832]{2,1,0:T(8,128)(2,1)S(1)}, bf16[2,48,832]{2,1,0:T(8,128)(2,1)S(1)}, u32[]{:S(2)}, u32[]{:S(2)}) collective-permute-start(bf16[2,48,832]{2,1,0:T(8,128)(2,1)S(1)} %get-tuple-element.26.rounded_ref), channel_id=1, source_target_pairs={{0,15},{1,0},{2,1},{3,2},{4,3},{5,4},{6,5},{7,6},{8,7},{9,8},{10,9... | collective-permute-start | bytes 479240 | tf_op jit(solution)/shard_map/ppermute | solution.py:22
  149.7 7.6 %collective-permute-start.3 = (bf16[2,48,832]{2,1,0:T(8,128)(2,1)S(1)}, bf16[2,48,832]{2,1,0:T(8,128)(2,1)S(1)}, u32[]{:S(2)}, u32[]{:S(2)}) collective-permute-start(bf16[2,48,832]{2,1,0:T(8,128)(2,1)S(1)} %get-tuple-element.17), channel_id=1, source_target_pairs={{0,1},{1,2},{2,3},{3,4},{4,5},{5,6},{6,7},{7,8},{8,9},{9,10},{10,1... | collective-permute-start | bytes 479240 | tf_op jit(solution)/shard_map/ppermute | solution.py:22
  157.4 3.0 %collective-permute-start.4 = (bf16[2,48,832]{2,1,0:T(8,128)(2,1)S(1)}, bf16[2,48,832]{2,1,0:T(8,128)(2,1)S(1)}, u32[]{:S(2)}, u32[]{:S(2)}) collective-permute-start(bf16[2,48,832]{2,1,0:T(8,128)(2,1)S(1)} %fusion.rounded_ref), channel_id=1, source_target_pairs={{0,15},{1,0},{2,1},{3,2},{4,3},{5,4},{6,5},{7,6},{8,7},{9,8},{10,9... | collective-permute-start | bytes 479240 | tf_op jit(solution)/shard_map/ppermute | solution.py:22
  158.7 7.8 %collective-permute-start.5 = (bf16[2,48,832]{2,1,0:T(8,128)(2,1)S(1)}, bf16[2,48,832]{2,1,0:T(8,128)(2,1)S(1)}, u32[]{:S(2)}, u32[]{:S(2)}) collective-permute-start(bf16[2,48,832]{2,1,0:T(8,128)(2,1)S(1)} %get-tuple-element.19), channel_id=1, source_target_pairs={{0,1},{1,2},{2,3},{3,4},{4,5},{5,6},{6,7},{7,8},{8,9},{9,10},{10,1... | collective-permute-start | bytes 479240 | tf_op jit(solution)/shard_map/ppermute | solution.py:22
  167.7 3.0 %collective-permute-start.6 = (bf16[2,48,832]{2,1,0:T(8,128)(2,1)S(1)}, bf16[2,48,832]{2,1,0:T(8,128)(2,1)S(1)}, u32[]{:S(2)}, u32[]{:S(2)}) collective-permute-start(bf16[2,48,832]{2,1,0:T(8,128)(2,1)S(1)} %rounded.1.rounded_ref), channel_id=1, source_target_pairs={{0,15},{1,0},{2,1},{3,2},{4,3},{5,4},{6,5},{7,6},{8,7},{9,8},{10,9... | collective-permute-start | bytes 479240 | tf_op jit(solution)/shard_map/ppermute | solution.py:22
  167.8 7.6 %collective-permute-start.7 = (bf16[2,48,832]{2,1,0:T(8,128)(2,1)S(1)}, bf16[2,48,832]{2,1,0:T(8,128)(2,1)S(1)}, u32[]{:S(2)}, u32[]{:S(2)}) collective-permute-start(bf16[2,48,832]{2,1,0:T(8,128)(2,1)S(1)} %get-tuple-element.25), channel_id=1, source_target_pairs={{0,1},{1,2},{2,3},{3,4},{4,5},{5,6},{6,7},{7,8},{8,9},{9,10},{10,1... | collective-permute-start | bytes 479240 | tf_op jit(solution)/shard_map/ppermute | solution.py:22

commit v6 on v5

--- a/solution.py
+++ b/solution.py
@@ -115,7 +115,7 @@
     )(turned)
 
 
-def unpack_kernel(rows, bounds, from_ref, out_ref, in_ref, sems):
+def unpack_kernel(rows, in_ref, out_ref):
     _, orbs, width = out_ref.shape
     full = width // LANES
     half = LANES // 2
@@ -128,12 +128,6 @@
         size, size // 2, lambda o: (o % span) // QUAD * (unit // 2) + (o % QUAD) % 2 * QUAD + o // span
     )
     early = lax.broadcasted_iota(jnp.int32, (size, half), 0) % QUAD < 2
-    arrivals = []
-    for stage, (start, stop) in enumerate(zip(bounds[:-1], bounds[1:])):
-        part = pl.ds(start, stop - start)
-        arrivals.append(pltpu.make_async_copy(from_ref.at[part], in_ref.at[part], sems.at[stage]))
-        arrivals[-1].start()
-    here = 0
 
     def lane_block(j, start, stop, scale):
         held = rows // scale
@@ -146,9 +140,6 @@
         return pieces[0] if len(pieces) == 1 else jnp.concatenate(pieces, axis=0)
 
     for i in range(orbs // span):
-        while bounds[here] * rows < (i + 1) * size:
-            arrivals[here].wait()
-            here += 1
         for at in range(0, full, 2):
             wide = range(at, min(at + 2, full))
             data = jnp.concatenate([lane_block(j, i * size, (i + 1) * size, 1) for j in wide], axis=1)
@@ -164,15 +155,12 @@
 
 
 def unpack(arrived, rows, orbs, width):
-    group = arrived.shape[0]
-    bounds = tuple(sorted({0, group // 2, group}))
-    return pl.pallas_call(
-        functools.partial(unpack_kernel, rows * QUAD, bounds),
+    return pl.pallas_call(
+        functools.partial(unpack_kernel, rows * QUAD),
         out_shape=jax.ShapeDtypeStruct((QUAD, orbs, width), jnp.bfloat16),
-        in_specs=[HBM_WHOLE],
+        in_specs=[VMEM_WHOLE],
         out_specs=VMEM_WHOLE,
-        scratch_shapes=[pltpu.VMEM(arrived.shape, arrived.dtype), pltpu.SemaphoreType.DMA((len(bounds) - 1,))],
-        compiler_params=pltpu.CompilerParams(vmem_limit_bytes=20 * MIB),
+        compiler_params=pltpu.CompilerParams(vmem_limit_bytes=16 * MIB),
         cost_estimate=pl.CostEstimate(
             flops=2 * QUAD * orbs * width * 256, bytes_accessed=4 * QUAD * orbs * width, transcendentals=0
         ),
@@ -180,77 +168,146 @@
     )(arrived)
 
 
-def product_cost(parts, vecs):
-    size = sum(part.size for part in parts)
-    return pl.CostEstimate(flops=2 * size * vecs * 4, bytes_accessed=2 * size, transcendentals=0)
-
-
-def turned_kernel(count, target_ref, rounded_ref, *refs):
-    parts, early, (own_ref, send_ref, acc_ref) = refs[:count], refs[count:-3], refs[-3:]
-    targets = [target_ref[...][e, 0] for e in range(parts[0].shape[0])]
+def product_cost(tiles, vecs):
+    return pl.CostEstimate(flops=8 * tiles.size * vecs, bytes_accessed=2 * tiles.size, transcendentals=0)
+
+
+def spread_panels(rounded, rows, bounds):
+    blk_dev, vecs, orbs = rounded.shape
+    repeated = jnp.repeat(rounded, QUAD // blk_dev, axis=0).reshape(QUAD * vecs, orbs)
+
+    def spread(first, count, unit, offset):
+        row = jnp.arange(count)[None, :]
+        source = first + row // unit * QUAD + offset + row % unit // QUAD
+        place = (jnp.arange(orbs)[:, None] == source).astype(jnp.bfloat16)
+        mine = jnp.arange(QUAD * vecs)[:, None] // vecs == row % QUAD
+        wide = jnp.dot(repeated, place, preferred_element_type=jnp.float32)
+        return jnp.where(mine, wide, 0.0).astype(jnp.bfloat16)
+
+    panels = []
+    for start, stop in zip(bounds[:-1], bounds[1:]):
+        first, count = start * rows, (stop - start) * rows * QUAD
+        panels.append(spread(first, count, QUAD * QUAD, 0))
+        panels.append(spread(first, count // 2, QUAD * QUAD // 2, 0))
+        panels.append(spread(first, count // 2, QUAD * QUAD // 2, QUAD // 2))
+    return panels
+
+
+def first_turned_kernel(rows, bounds, target_ref, from_ref, *refs):
+    panels, (own_ref, send_ref, packed_ref, acc_ref, spread_ref, sems) = refs[:-6], refs[-6:]
+    targets = [target_ref[...][e, 0] for e in range(QUAD)]
+    blk_dev, vecs, orbs = own_ref.shape
+    full = orbs // LANES
+    half = LANES // 2
+    arrivals = []
+    for stage, (start, stop) in enumerate(zip(bounds[:-1], bounds[1:])):
+        part = pl.ds(start, stop - start)
+        arrivals.append(pltpu.make_async_copy(from_ref.at[part], packed_ref.at[part], sems.at[stage]))
+        arrivals[-1].start()
+    for stage, (start, stop) in enumerate(zip(bounds[:-1], bounds[1:])):
+        arrivals[stage].wait()
+        whole, early, late = (panel[...] for panel in panels[3 * stage : 3 * stage + 3])
+
+        def add(place, part, stage=stage):
+            if stage == 0:
+                acc_ref[:, place] = part
+            else:
+                acc_ref[:, place] += part
+
+        for at in range(0, full, 2):
+            wide = range(at, min(at + 2, full))
+            data = [packed_ref[start:stop, j * rows : (j + 1) * rows, :].reshape(-1, LANES) for j in wide]
+            add(slice(at * LANES, (at + len(wide)) * LANES), dot_nn(whole, jnp.concatenate(data, axis=1)))
+        tail = jnp.concatenate([packed_ref[g, full * rows :, :] for g in range(start, stop)], axis=0)
+        add(slice(full * LANES, orbs), dot_nn(early, tail)[:, :half] + dot_nn(late, tail)[:, half:])
+    spread_ref[...] = jnp.zeros_like(spread_ref)
+    for e in range(QUAD):
+        spread_ref[targets[e]] += acc_ref[e * vecs : (e + 1) * vecs]
+    own_ref[...] = spread_ref[:blk_dev]
+    send_ref[...] = spread_ref[blk_dev:].astype(jnp.bfloat16)
+
+
+def first_turned(target, rounded, arrived, rows):
+    blk_dev, vecs, orbs = rounded.shape
+    group = arrived.shape[0]
+    bounds = (0, group // 2, group)
+    panels = spread_panels(rounded, rows, bounds)
+    return pl.pallas_call(
+        functools.partial(first_turned_kernel, rows * QUAD, bounds),
+        out_shape=(
+            jax.ShapeDtypeStruct(rounded.shape, jnp.float32),
+            jax.ShapeDtypeStruct(rounded.shape, jnp.bfloat16),
+            jax.ShapeDtypeStruct(arrived.shape, arrived.dtype),
+        ),
+        in_specs=[VMEM_WHOLE, HBM_WHOLE] + [VMEM_WHOLE] * len(panels),
+        out_specs=(VMEM_WHOLE,) * 3,
+        scratch_shapes=[
+            pltpu.VMEM((QUAD * vecs, orbs), jnp.float32),
+            pltpu.VMEM((2 * blk_dev, vecs, orbs), jnp.float32),
+            pltpu.SemaphoreType.DMA((len(bounds) - 1,)),
+        ],
+        compiler_params=pltpu.CompilerParams(vmem_limit_bytes=20 * MIB),
+        cost_estimate=pl.CostEstimate(
+            flops=8 * arrived.size * vecs, bytes_accessed=2 * arrived.size, transcendentals=0
+        ),
+        name="first_turned",
+    )(target, arrived, *panels)
+
+
+def turned_kernel(target_ref, rounded_ref, tiles_ref, own_ref, send_ref, acc_ref):
+    targets = [target_ref[...][e, 0] for e in range(tiles_ref.shape[0])]
     blk_dev = rounded_ref.shape[0]
-    at = 0
-    if early:
-        at = early[0].shape[2]
-        own_ref[:, :, :at] = early[0][...]
-        send_ref[:, :, :at] = early[1][...]
-    left = at
+    edges = tiles_ref.shape[0]
     acc_ref[...] = jnp.zeros_like(acc_ref)
-    for part in parts:
-        edges, _, width = part.shape
-        for e in range(edges):
-            acc_ref[targets[e], :, left : left + width] += dot_nn(rounded_ref[e * blk_dev // edges], part[e])
-        left += width
-    own_ref[:, :, at:] = acc_ref[:blk_dev, :, at:]
-    send_ref[:, :, at:] = acc_ref[blk_dev:, :, at:].astype(jnp.bfloat16)
-
-
-def turned_terms(target, rounded, parts, early=()):
-    blk_dev, vecs, _ = rounded.shape
-    shape = (blk_dev, vecs, sum(part.shape[2] for part in [*early[:1], *parts]))
-    return pl.pallas_call(
-        functools.partial(turned_kernel, len(parts)),
-        out_shape=(jax.ShapeDtypeStruct(shape, jnp.float32), jax.ShapeDtypeStruct(shape, jnp.bfloat16)),
-        in_specs=[VMEM_WHOLE] + [VMEM_WHOLE] * (1 + len(parts) + len(early)),
+    for e in range(edges):
+        acc_ref[targets[e]] += dot_nn(rounded_ref[e * blk_dev // edges], tiles_ref[e])
+    own_ref[...] = acc_ref[:blk_dev]
+    send_ref[...] = acc_ref[blk_dev:].astype(jnp.bfloat16)
+
+
+def turned_terms(target, rounded, tiles):
+    blk_dev, vecs, orbs = rounded.shape
+    return pl.pallas_call(
+        turned_kernel,
+        out_shape=(
+            jax.ShapeDtypeStruct(rounded.shape, jnp.float32),
+            jax.ShapeDtypeStruct(rounded.shape, jnp.bfloat16),
+        ),
+        in_specs=[VMEM_WHOLE] * 3,
         out_specs=(VMEM_WHOLE, VMEM_WHOLE),
-        scratch_shapes=[pltpu.VMEM((2 * blk_dev, *shape[1:]), jnp.float32)],
-        compiler_params=pltpu.CompilerParams(vmem_limit_bytes=16 * MIB),
-        cost_estimate=product_cost(parts, vecs),
+        scratch_shapes=[pltpu.VMEM((2 * blk_dev, vecs, orbs), jnp.float32)],
+        compiler_params=pltpu.CompilerParams(vmem_limit_bytes=16 * MIB),
+        cost_estimate=product_cost(tiles, vecs),
         name="turned",
-    )(target, rounded, *parts, *early)
-
-
-def direct_kernel(target_ref, rounded_ref, following_ref, own_ref, *refs):
-    mirrors, (out_ref, picked_ref) = refs[:-2], refs[-2:]
-    targets = [target_ref[...][e, 0] for e in range(mirrors[0].shape[0])]
+    )(target, rounded, tiles)
+
+
+def direct_kernel(product, target_ref, rounded_ref, following_ref, own_ref, tiles_ref, out_ref, picked_ref):
+    targets = [target_ref[...][e, 0] for e in range(tiles_ref.shape[0])]
     blk_dev = rounded_ref.shape[0]
-    edges = mirrors[0].shape[0]
+    edges = tiles_ref.shape[0]
     slots = edges // blk_dev
     picked_ref[:blk_dev] = rounded_ref[...]
     picked_ref[blk_dev:] = following_ref[...]
     for b in range(blk_dev):
         total = own_ref[b]
         for e in range(b * slots, (b + 1) * slots):
-            left = 0
-            for mirror in mirrors:
-                width = mirror.shape[1]
-                total += dot_nn(picked_ref[targets[e], :, left : left + width], mirror[e])
-                left += width
+            total += product(picked_ref[targets[e]], tiles_ref[e])
         out_ref[b] = total
 
 
-def direct_terms(target, rounded, following, own, mirrors):
+def direct_terms(target, rounded, following, own, tiles, product):
     blk_dev, vecs, orbs = rounded.shape
     return pl.pallas_call(
-        direct_kernel,
+        functools.partial(direct_kernel, product),
         out_shape=jax.ShapeDtypeStruct(rounded.shape, jnp.float32),
-        in_specs=[VMEM_WHOLE] + [VMEM_WHOLE] * (3 + len(mirrors)),
+        in_specs=[VMEM_WHOLE] + [VMEM_WHOLE] * 4,
         out_specs=VMEM_WHOLE,
         scratch_shapes=[pltpu.VMEM((2 * blk_dev, vecs, orbs), jnp.bfloat16)],
         compiler_params=pltpu.CompilerParams(vmem_limit_bytes=16 * MIB),
-        cost_estimate=product_cost(mirrors, vecs),
+        cost_estimate=product_cost(tiles, vecs),
         name="direct",
-    )(target, rounded, following, own, *mirrors)
+    )(target, rounded, following, own, tiles)
 
 
 def mirror_kernel(tiles_ref, after_ref, out_ref):
@@ -284,6 +341,28 @@
         out_specs=VMEM_WHOLE,
         compiler_params=pltpu.CompilerParams(vmem_limit_bytes=16 * MIB),
         name="rounded",
+    )(direct, arrive, previous)
+
+
+def final_kernel(direct_ref, arrive_ref, previous_ref, out_ref, panel_ref, sems):
+    copies = []
+    for b in range(panel_ref.shape[0]):
+        panel_ref[b] = 2.0 * (direct_ref[b] + arrive_ref[b].astype(jnp.float32)) - previous_ref[b]
+        copies.append(pltpu.make_async_copy(panel_ref.at[b], out_ref.at[b], sems.at[b]))
+        copies[-1].start()
+    for copy in copies:
+        copy.wait()
+
+
+def final_update(direct, arrive, previous):
+    return pl.pallas_call(
+        final_kernel,
+        out_shape=jax.ShapeDtypeStruct(direct.shape, jnp.float32),
+        in_specs=[VMEM_WHOLE] * 3,
+        out_specs=HBM_WHOLE,
+        scratch_shapes=[pltpu.VMEM(direct.shape, jnp.float32), pltpu.SemaphoreType.DMA(direct.shape[:1])],
+        compiler_params=pltpu.CompilerParams(vmem_limit_bytes=16 * MIB),
+        name="final",
     )(direct, arrive, previous)
 
 
@@ -302,35 +381,34 @@
     padded = jnp.pad(target, (0, -target.size % SUBLANES))
     target = jnp.broadcast_to(padded[:, None], (padded.size, LANES))
     rounded = trial_panel.astype(jnp.bfloat16)
-    fits = tiles // group == QUAD and rows % QUAD == 0
+    fits = tiles // group == QUAD and QUAD % blk_dev == 0 and rows % QUAD == 0 and group % 8 == 0
+    following = passed_along(rounded, "gx", -1)
     if fits and orbs % LANES == LANES // 2 and orbs % (4 * QUAD * QUAD) == 0:
-        cuts = [(0, orbs)]
-        parts = [unpack(exchanged(pack(edge_tiles, *cut)), rows, orbs, cut[1]) for cut in cuts]
+        own, send, packed = first_turned(target, rounded, exchanged(pack(edge_tiles, 0, orbs)), rows)
+        arrive = passed_along(send, "gx", 1)
+        owned = unpack(packed, rows, orbs, orbs)
     else:
-        parts = [lax.all_to_all(edge_tiles, "gx", split_axis=0, concat_axis=1, tiled=True)]
-    early = turned_terms(target, rounded, parts[:1]) if len(parts) > 1 else ()
-    mirrors = [mirrored(part, early[1]) for part in parts[:-1]]
-
-    previous, current = None, trial_panel
-    for k in range(DEGREE):
+        owned = lax.all_to_all(edge_tiles, "gx", split_axis=0, concat_axis=1, tiled=True)
+        own, send = turned_terms(target, rounded, owned)
+        arrive = passed_along(send, "gx", 1)
+    direct = direct_terms(target, rounded, following, own, owned, dot_nt)
+    mirror = mirrored(owned, direct)
+    previous, current = trial_panel, direct + arrive.astype(jnp.float32)
+    rounded = current.astype(jnp.bfloat16)
+    for k in range(1, DEGREE):
         following = passed_along(rounded, "gx", -1)
-        if k == 0:
-            own, send = turned_terms(target, rounded, parts[len(parts) - 1 :], early)
-            mirrors.append(mirrored(parts[-1], send))
+        own, send = turned_terms(target, rounded, owned)
+        arrive = passed_along(send, "gx", 1)
+        direct = direct_terms(target, rounded, following, own, mirror, dot_nn)
+        if k == DEGREE - 2:
+            rounded = rounded_update(direct, arrive, previous)
+            direct, arrive, previous, rounded = lax.optimization_barrier((direct, arrive, previous, rounded))
+        if k < DEGREE - 1:
+            total = 2.0 * (direct + arrive.astype(jnp.float32)) - previous
         else:
-            own, send = turned_terms(target, rounded, parts)
-        arrive = passed_along(send, "gx", 1)
-        direct = direct_terms(target, rounded, following, own, mirrors)
-        if k == 0:
-            total = direct + arrive.astype(jnp.float32)
+            total = final_update(direct, arrive, previous)
+        if k < DEGREE - 2:
             rounded = total.astype(jnp.bfloat16)
-        else:
-            if k == DEGREE - 2:
-                rounded = rounded_update(direct, arrive, previous)
-                direct, arrive, previous, rounded = lax.optimization_barrier((direct, arrive, previous, rounded))
-            total = 2.0 * (direct + arrive.astype(jnp.float32)) - previous
-            if k < DEGREE - 2:
-                rounded = total.astype(jnp.bfloat16)
         previous, current = current, total
     return previous, current
 

time: 176 us -> 176 us (level)
  waiting for transfers between devices: 139 us -> 131 us
  matrix products: 0 us -> 5.58 us
  Pallas kernels: 20 us -> 22.3 us
    all_to_all x1, waiting for transfers between devices: 96.4 us -> 90.7 us  [exchanged(): return lax.all_to_all(tiles, 'gx', split_axis=0, concat_axis=0, tiled=True)]
    dot_general x0 -> x6, matrix products: none -> 5.58 us  [spread(): wide = jnp.dot(repeated, place, preferred_element_type=jnp.float32)]
    pallas_call x9 -> x10, Pallas kernels: 12.8 us -> 15 us  [the longest x4 5.03 us: direct_terms(): pl.pallas_call(functools.partial(direct_kernel, product), out_shape=jax.S...]
    ppermute x8, waiting for transfers between devices: 42.1 us -> 40 us  [passed_along(): return lax.ppermute(value, axis, pairs)]
  transfers between devices with their start and end apart: 9 -> 9, of which waited for: 8 -> 7; matrix products, arithmetic and copies ran while one was open for 1% -> 4% of each run, Pallas kernels for 8% -> 8%
where the time goes in v6:
time: 176 us
  waiting for transfers between devices  131 us (74%)
  Pallas kernels  22.3 us (13%)
  starting transfers between devices  14.9 us (8%)
  matrix products  5.58 us (3%)
    all_to_all x1, waiting for transfers between devices, exchanged(): return lax.all_to_all(tiles, 'gx', split_axis=0, concat_axis=0, tiled=True)  90.7 us
    ppermute x8, waiting for transfers between devices, passed_along(): return lax.ppermute(value, axis, pairs)  40 us
    all_to_all x1, starting transfers between devices, exchanged(): return lax.all_to_all(tiles, 'gx', split_axis=0, concat_axis=0, tiled=True)  7.58 us
    ppermute x8, starting transfers between devices, passed_along(): return lax.ppermute(value, axis, pairs)  7.3 us
    dot_general x6, matrix products, spread(): wide = jnp.dot(repeated, place, preferred_element_type=jnp.float32)  5.58 us
    pallas_call x1, Pallas kernels, pack(): pl.pallas_call(functools.partial(pack_kernel, left, bounds), out_shape=ja...  5.54 us
    pallas_call x4, Pallas kernels, direct_terms(): pl.pallas_call(functools.partial(direct_kernel, product), out_shape=jax.S...  5.03 us
    pallas_call x1, Pallas kernels, first_turned(): pl.pallas_call(functools.partial(first_turned_kernel, rows * QUAD, bounds...  3.86 us
  transfers between devices with their start and end apart: 9, of which 7 were waited for; matrix products, arithmetic and copies ran while one was open for 4% of the time, Pallas kernels for 8%

profile of v6, /device:TPU:0, one launch (start us, length us, event | category | flops | bytes accessed | tf_op | source)
XLA Modules:
  0.0 175.9 jit_solution(18150838518420033154)
XLA Ops:
  0.6 5.5 %pack.1 = bf16[16,1352,128]{2,1,0:T(8,128)(2,1)} custom-call(bf16[52,64,832]{2,1,0:T(8,128)(2,1)} %bitcast.44), custom_call_target="tpu_custom_call" | custom-call | flops 1417674752 | bytes 11075584 | tf_op jit(solution)/shard_map/pack/pallas_call | solution.py:98
  6.2 7.6 %all-to-all-start = ((bf16[16,1352,128]{2,1,0:T(8,128)(2,1)}), bf16[16,1352,128]{2,1,0:T(8,128)(2,1)}, u32[]{:S(2)}, u32[]{:S(2)}) async-start(bf16[16,1352,128]{2,1,0:T(8,128)(2,1)} %pack.1), calls=%async_computation | async-start | bytes 11075584 | tf_op jit(solution)/shard_map/all_to_all | solution.py:370
  13.8 4.4 %collective-permute-start = (bf16[2,48,832]{2,1,0:T(8,128)(2,1)S(1)}, bf16[2,48,832]{2,1,0:T(8,128)(2,1)S(1)}, u32[]{:S(2)}, u32[]{:S(2)}) collective-permute-start(bf16[2,48,832]{2,1,0:T(8,128)(2,1)S(1)} %convert_element_type.42.rounded_ref), channel_id=1, source_target_pairs={{0,15},{1,0},{2,1},{3,2},{4,3},{5,4},{6,5},{7,6},{8,7},{9,8},{10,9... | collective-permute-start | bytes 479240 | tf_op jit(solution)/shard_map/ppermute | solution.py:22
  18.6 0.7 fusion.26.refs_1_
  19.4 0.7 fusion.27.refs_2_
  20.1 0.7 fusion.28.refs_4_
  20.9 0.7 fusion.29.refs_5_
  21.6 1.3 fusion.12.refs_0_
  22.9 1.3 fusion.13.refs_3_
  24.3 90.7 %all-to-all-done.from_ref = bf16[16,1352,128]{2,1,0:T(8,128)(2,1)} async-done(((bf16[16,1352,128]{2,1,0:T(8,128)(2,1)}), bf16[16,1352,128]{2,1,0:T(8,128)(2,1)}, u32[]{:S(2)}, u32[]{:S(2)}) %all-to-all-start) | async-done | bytes 5537824 | tf_op jit(solution)/shard_map/all_to_all | solution.py:370
  115.0 3.9 %first_turned.1 = (f32[2,48,832]{2,1,0:T(8,128)S(1)}, bf16[2,48,832]{2,1,0:T(8,128)(2,1)S(1)}, bf16[16,1352,128]{2,1,0:T(8,128)(2,1)S(1)}) custom-call(s32[8,128]{1,0:T(8,128)S(1)} %broadcast_in_dim.16.target_ref, bf16[16,1352,128]{2,1,0:T(8,128)(2,1)} %all-to-all-done.from_ref, bf16[192,1664]{1,0:T(8,128)(2,1)S(1)} %fusion.12.refs_0_, ...), custom_call_target="tpu_custom_call" | custom-call | flops 1063256064 | bytes 5537792 | tf_op jit(solution)/shard_map/first_turned/pallas_call | solution.py:235
  118.8 1.0 collective-permute-start.1
  119.9 1.8 %unpack.1.tiles_ref = bf16[4,832,832]{2,1,0:T(8,128)(2,1)S(1)} custom-call(bf16[16,1352,128]{2,1,0:T(8,128)(2,1)S(1)} %get-tuple-element.16.in_ref), custom_call_target="tpu_custom_call" | custom-call | flops 1417674752 | bytes 11075584 | tf_op jit(solution)/shard_map/unpack/pallas_call | solution.py:158
  121.7 1.8 %direct.4.after_ref = f32[2,48,832]{2,1,0:T(8,128)S(1)} custom-call(s32[8,128]{1,0:T(8,128)S(1)} %broadcast_in_dim.16.target_ref, bf16[2,48,832]{2,1,0:T(8,128)(2,1)S(1)} %convert_element_type.42.rounded_ref, bf16[2,48,832]{2,1,0:T(8,128)(2,1)S(1)} %collective-permute-done.following_ref, f32[2,48,832]{2,1,0:T(8,128)S(1)} %get-tuple-element.15.own_ref, ...), custom_call_target="tpu_custom_call" | custom-call | flops 1063256064 | bytes 5537792 | tf_op jit(solution)/shard_map/direct/pallas_call | solution.py:301
  123.5 24.0 %collective-permute-done.1 = bf16[2,48,832]{2,1,0:T(8,128)(2,1)S(1)} collective-permute-done((bf16[2,48,832]{2,1,0:T(8,128)(2,1)S(1)}, bf16[2,48,832]{2,1,0:T(8,128)(2,1)S(1)}, u32[]{:S(2)}, u32[]{:S(2)}) %collective-permute-start.1) | collective-permute-done | bytes 159776 | tf_op jit(solution)/shard_map/ppermute | solution.py:22
  147.6 0.7 collective-permute-start.2
  148.3 1.2 turned.3
  149.5 1.7 mirror.1.tiles_ref
  151.2 1.1 direct.5
  152.3 4.8 %collective-permute-done.3 = bf16[2,48,832]{2,1,0:T(8,128)(2,1)S(1)} collective-permute-done((bf16[2,48,832]{2,1,0:T(8,128)(2,1)S(1)}, bf16[2,48,832]{2,1,0:T(8,128)(2,1)S(1)}, u32[]{:S(2)}, u32[]{:S(2)}) %collective-permute-start.3) | collective-permute-done | bytes 159776 | tf_op jit(solution)/shard_map/ppermute | solution.py:22
  157.3 1.2 turned.4
  158.5 0.5 collective-permute-start.5
  159.0 1.2 collective-permute-done.4.following_ref
  160.2 1.1 direct.6.direct_ref
  161.3 4.8 %collective-permute-done.5.arrive_ref = bf16[2,48,832]{2,1,0:T(8,128)(2,1)S(1)} collective-permute-done((bf16[2,48,832]{2,1,0:T(8,128)(2,1)S(1)}, bf16[2,48,832]{2,1,0:T(8,128)(2,1)S(1)}, u32[]{:S(2)}, u32[]{:S(2)}) %collective-permute-start.5) | collective-permute-done | bytes 159776 | tf_op jit(solution)/shard_map/ppermute | solution.py:22
  166.1 1.2 turned.5
  167.4 0.5 collective-permute-start.7
  167.9 0.8 multiply_subtract_fusion
  168.7 1.6 collective-permute-done.6.following_ref
  170.3 1.1 direct.7.direct_ref
  171.4 3.6 %collective-permute-done.7.arrive_ref = bf16[2,48,832]{2,1,0:T(8,128)(2,1)S(1)} collective-permute-done((bf16[2,48,832]{2,1,0:T(8,128)(2,1)S(1)}, bf16[2,48,832]{2,1,0:T(8,128)(2,1)S(1)}, u32[]{:S(2)}, u32[]{:S(2)}) %collective-permute-start.7) | collective-permute-done | bytes 159776 | tf_op jit(solution)/shard_map/ppermute | solution.py:22
  175.0 0.8 final.1
  (27 shorter events, 0.8 us)
Async XLA Ops:
  6.2 7.6 %copy-start = (f32[2,48,832]{2,1,0:T(8,128)S(1)}, f32[2,48,832]{2,1,0:T(8,128)}, u32[]{:S(2)}) copy-start(f32[2,48,832]{2,1,0:T(8,128)} %param.4) | copy-start | bytes 958468
  6.2 12.0 %copy-start.1 = (s32[32,2]{0,1:T(2,128)S(1)}, s32[32,2]{0,1:T(2,128)}, u32[]{:S(2)}) copy-start(s32[32,2]{0,1:T(2,128)} %param.5) | copy-start | bytes 772
  6.2 108.7 %all-to-all-start = ((bf16[16,1352,128]{2,1,0:T(8,128)(2,1)}), bf16[16,1352,128]{2,1,0:T(8,128)(2,1)}, u32[]{:S(2)}, u32[]{:S(2)}) async-start(bf16[16,1352,128]{2,1,0:T(8,128)(2,1)} %pack.1), calls=%async_computation | async-start | bytes 11075584 | tf_op jit(solution)/shard_map/all_to_all | solution.py:370
  13.8 107.9 %collective-permute-start = (bf16[2,48,832]{2,1,0:T(8,128)(2,1)S(1)}, bf16[2,48,832]{2,1,0:T(8,128)(2,1)S(1)}, u32[]{:S(2)}, u32[]{:S(2)}) collective-permute-start(bf16[2,48,832]{2,1,0:T(8,128)(2,1)S(1)} %convert_element_type.42.rounded_ref), channel_id=1, source_target_pairs={{0,15},{1,0},{2,1},{3,2},{4,3},{5,4},{6,5},{7,6},{8,7},{9,8},{10,9... | collective-permute-start | bytes 479240 | tf_op jit(solution)/shard_map/ppermute | solution.py:22
  118.8 28.7 %collective-permute-start.1 = (bf16[2,48,832]{2,1,0:T(8,128)(2,1)S(1)}, bf16[2,48,832]{2,1,0:T(8,128)(2,1)S(1)}, u32[]{:S(2)}, u32[]{:S(2)}) collective-permute-start(bf16[2,48,832]{2,1,0:T(8,128)(2,1)S(1)} %get-tuple-element.17), channel_id=1, source_target_pairs={{0,1},{1,2},{2,3},{3,4},{4,5},{5,6},{6,7},{7,8},{8,9},{9,10},{10,1... | collective-permute-start | bytes 479240 | tf_op jit(solution)/shard_map/ppermute | solution.py:22
  147.6 3.6 %collective-permute-start.2 = (bf16[2,48,832]{2,1,0:T(8,128)(2,1)S(1)}, bf16[2,48,832]{2,1,0:T(8,128)(2,1)S(1)}, u32[]{:S(2)}, u32[]{:S(2)}) collective-permute-start(bf16[2,48,832]{2,1,0:T(8,128)(2,1)S(1)} %get-tuple-element.30.rounded_ref), channel_id=1, source_target_pairs={{0,15},{1,0},{2,1},{3,2},{4,3},{5,4},{6,5},{7,6},{8,7},{9,8},{10,9... | collective-permute-start | bytes 479240 | tf_op jit(solution)/shard_map/ppermute | solution.py:22
  149.5 7.7 %collective-permute-start.3 = (bf16[2,48,832]{2,1,0:T(8,128)(2,1)S(1)}, bf16[2,48,832]{2,1,0:T(8,128)(2,1)S(1)}, u32[]{:S(2)}, u32[]{:S(2)}) collective-permute-start(bf16[2,48,832]{2,1,0:T(8,128)(2,1)S(1)} %get-tuple-element.19), channel_id=1, source_target_pairs={{0,1},{1,2},{2,3},{3,4},{4,5},{5,6},{6,7},{7,8},{8,9},{9,10},{10,1... | collective-permute-start | bytes 479240 | tf_op jit(solution)/shard_map/ppermute | solution.py:22
  157.2 3.0 %collective-permute-start.4 = (bf16[2,48,832]{2,1,0:T(8,128)(2,1)S(1)}, bf16[2,48,832]{2,1,0:T(8,128)(2,1)S(1)}, u32[]{:S(2)}, u32[]{:S(2)}) collective-permute-start(bf16[2,48,832]{2,1,0:T(8,128)(2,1)S(1)} %get-tuple-element.28.rounded_ref), channel_id=1, source_target_pairs={{0,15},{1,0},{2,1},{3,2},{4,3},{5,4},{6,5},{7,6},{8,7},{9,8},{10,9... | collective-permute-start | bytes 479240 | tf_op jit(solution)/shard_map/ppermute | solution.py:22
  158.5 7.6 %collective-permute-start.5 = (bf16[2,48,832]{2,1,0:T(8,128)(2,1)S(1)}, bf16[2,48,832]{2,1,0:T(8,128)(2,1)S(1)}, u32[]{:S(2)}, u32[]{:S(2)}) collective-permute-start(bf16[2,48,832]{2,1,0:T(8,128)(2,1)S(1)} %get-tuple-element.21), channel_id=1, source_target_pairs={{0,1},{1,2},{2,3},{3,4},{4,5},{5,6},{6,7},{7,8},{8,9},{9,10},{10,1... | collective-permute-start | bytes 479240 | tf_op jit(solution)/shard_map/ppermute | solution.py:22
  167.3 3.0 %collective-permute-start.6 = (bf16[2,48,832]{2,1,0:T(8,128)(2,1)S(1)}, bf16[2,48,832]{2,1,0:T(8,128)(2,1)S(1)}, u32[]{:S(2)}, u32[]{:S(2)}) collective-permute-start(bf16[2,48,832]{2,1,0:T(8,128)(2,1)S(1)} %rounded.1.rounded_ref), channel_id=1, source_target_pairs={{0,15},{1,0},{2,1},{3,2},{4,3},{5,4},{6,5},{7,6},{8,7},{9,8},{10,9... | collective-permute-start | bytes 479240 | tf_op jit(solution)/shard_map/ppermute | solution.py:22
  167.4 7.6 %collective-permute-start.7 = (bf16[2,48,832]{2,1,0:T(8,128)(2,1)S(1)}, bf16[2,48,832]{2,1,0:T(8,128)(2,1)S(1)}, u32[]{:S(2)}, u32[]{:S(2)}) collective-permute-start(bf16[2,48,832]{2,1,0:T(8,128)(2,1)S(1)} %get-tuple-element.27), channel_id=1, source_target_pairs={{0,1},{1,2},{2,3},{3,4},{4,5},{5,6},{6,7},{7,8},{8,9},{9,10},{10,1... | collective-permute-start | bytes 479240 | tf_op jit(solution)/shard_map/ppermute | solution.py:22

commit v7 on v6

--- a/solution.py
+++ b/solution.py
@@ -34,6 +34,30 @@
     row = lax.broadcasted_iota(jnp.int32, (rows, columns), 0)
     column = lax.broadcasted_iota(jnp.int32, (rows, columns), 1)
     return (column == source_of_row(row)).astype(jnp.bfloat16)
+
+
+def dense_rows(blk_dev, vecs, orbs):
+    return blk_dev * vecs * orbs // LANES
+
+
+def store_dense(ref, panels):
+    vecs, orbs = panels[0].shape
+    full = orbs // LANES
+    for c, panel in enumerate(panels):
+        for j in range(full):
+            first = (j * len(panels) + c) * vecs
+            ref[first : first + vecs, :] = panel[:, j * LANES : (j + 1) * LANES].astype(ref.dtype)
+    ends = jnp.concatenate([panel[:, full * LANES :] for panel in panels], axis=1)
+    ref[full * len(panels) * vecs :, :] = ends.astype(ref.dtype)
+
+
+def load_dense(ref, c, shape):
+    blk_dev, vecs, orbs = shape
+    full = orbs // LANES
+    blocks = [ref[(j * blk_dev + c) * vecs : (j * blk_dev + c + 1) * vecs, :].astype(jnp.float32) for j in range(full)]
+    width = orbs % LANES
+    ends = ref[full * blk_dev * vecs :, :].astype(jnp.float32)
+    return jnp.concatenate([*blocks, ends[:, c * width : (c + 1) * width]], axis=1)
 
 
 def pack_kernel(left, bounds, x_ref, out_ref, x_buf, out_buf, tail_buf, in_sems, out_sems):
@@ -224,7 +248,7 @@
     for e in range(QUAD):
         spread_ref[targets[e]] += acc_ref[e * vecs : (e + 1) * vecs]
     own_ref[...] = spread_ref[:blk_dev]
-    send_ref[...] = spread_ref[blk_dev:].astype(jnp.bfloat16)
+    store_dense(send_ref, [spread_ref[blk_dev + c] for c in range(blk_dev)])
 
 
 def first_turned(target, rounded, arrived, rows):
@@ -236,7 +260,7 @@
         functools.partial(first_turned_kernel, rows * QUAD, bounds),
         out_shape=(
             jax.ShapeDtypeStruct(rounded.shape, jnp.float32),
-            jax.ShapeDtypeStruct(rounded.shape, jnp.bfloat16),
+            jax.ShapeDtypeStruct((dense_rows(*rounded.shape), LANES), jnp.bfloat16),
             jax.ShapeDtypeStruct(arrived.shape, arrived.dtype),
         ),
         in_specs=[VMEM_WHOLE, HBM_WHOLE] + [VMEM_WHOLE] * len(panels),
@@ -262,7 +286,7 @@
     for e in range(edges):
         acc_ref[targets[e]] += dot_nn(rounded_ref[e * blk_dev // edges], tiles_ref[e])
     own_ref[...] = acc_ref[:blk_dev]
-    send_ref[...] = acc_ref[blk_dev:].astype(jnp.bfloat16)
+    store_dense(send_ref, [acc_ref[blk_dev + c] for c in range(blk_dev)])
 
 
 def turned_terms(target, rounded, tiles):
@@ -271,7 +295,7 @@
         turned_kernel,
         out_shape=(
             jax.ShapeDtypeStruct(rounded.shape, jnp.float32),
-            jax.ShapeDtypeStruct(rounded.shape, jnp.bfloat16),
+            jax.ShapeDtypeStruct((dense_rows(*rounded.shape), LANES), jnp.bfloat16),
         ),
         in_specs=[VMEM_WHOLE] * 3,
         out_specs=(VMEM_WHOLE, VMEM_WHOLE),
@@ -288,7 +312,8 @@
     edges = tiles_ref.shape[0]
     slots = edges // blk_dev
     picked_ref[:blk_dev] = rounded_ref[...]
-    picked_ref[blk_dev:] = following_ref[...]
+    for c in range(blk_dev):
+        picked_ref[blk_dev + c] = load_dense(following_ref, c, rounded_ref.shape).astype(jnp.bfloat16)
     for b in range(blk_dev):
         total = own_ref[b]
         for e in range(b * slots, (b + 1) * slots):
@@ -328,26 +353,45 @@
     )(tiles, after)
 
 
-def rounded_kernel(direct_ref, arrive_ref, previous_ref, rounded_ref):
-    panel = 2.0 * (direct_ref[...] + arrive_ref[...].astype(jnp.float32)) - previous_ref[...]
-    rounded_ref[...] = panel.astype(jnp.bfloat16)
-
-
-def rounded_update(direct, arrive, previous):
-    return pl.pallas_call(
-        rounded_kernel,
-        out_shape=jax.ShapeDtypeStruct(direct.shape, jnp.bfloat16),
-        in_specs=[VMEM_WHOLE] * 3,
-        out_specs=VMEM_WHOLE,
-        compiler_params=pltpu.CompilerParams(vmem_limit_bytes=16 * MIB),
-        name="rounded",
-    )(direct, arrive, previous)
+def update_kernel(extra, total_out, first_ref, *refs):
+    arrive, previous, outs = refs[: min(extra, 1)], refs[min(extra, 1) : extra], refs[extra:]
+    shape = first_ref.shape
+    panels = []
+    for c in range(shape[0]):
+        panel = first_ref[c]
+        if arrive:
+            panel = panel + load_dense(arrive[0], c, shape)
+        if previous:
+            panel = 2.0 * panel - previous[0][c]
+        panels.append(panel)
+        if total_out:
+            outs[0][c] = panel
+        if outs[total_out:]:
+            outs[total_out][c] = panel.astype(jnp.bfloat16)
+    if outs[total_out:]:
+        store_dense(outs[total_out + 1], panels)
+
+
+def updated(first, *rest, total=True, rounded=True):
+    shapes = [jax.ShapeDtypeStruct(first.shape, jnp.float32)] if total else []
+    if rounded:
+        shapes.append(jax.ShapeDtypeStruct(first.shape, jnp.bfloat16))
+        shapes.append(jax.ShapeDtypeStruct((dense_rows(*first.shape), LANES), jnp.bfloat16))
+    return pl.pallas_call(
+        functools.partial(update_kernel, len(rest), int(total)),
+        out_shape=shapes,
+        in_specs=[VMEM_WHOLE] * (1 + len(rest)),
+        out_specs=[VMEM_WHOLE] * len(shapes),
+        compiler_params=pltpu.CompilerParams(vmem_limit_bytes=16 * MIB),
+        name="update",
+    )(first, *rest)
 
 
 def final_kernel(direct_ref, arrive_ref, previous_ref, out_ref, panel_ref, sems):
     copies = []
     for b in range(panel_ref.shape[0]):
-        panel_ref[b] = 2.0 * (direct_ref[b] + arrive_ref[b].astype(jnp.float32)) - previous_ref[b]
+        arrived = load_dense(arrive_ref, b, direct_ref.shape)
+        panel_ref[b] = 2.0 * (direct_ref[b] + arrived) - previous_ref[b]
         copies.append(pltpu.make_async_copy(panel_ref.at[b], out_ref.at[b], sems.at[b]))
         copies[-1].start()
     for copy in copies:
@@ -380,9 +424,9 @@
     target = jnp.mod(own_cols - domain * blk_dev, block_total)
     padded = jnp.pad(target, (0, -target.size % SUBLANES))
     target = jnp.broadcast_to(padded[:, None], (padded.size, LANES))
-    rounded = trial_panel.astype(jnp.bfloat16)
+    rounded, dense = updated(trial_panel, total=False)
     fits = tiles // group == QUAD and QUAD % blk_dev == 0 and rows % QUAD == 0 and group % 8 == 0
-    following = passed_along(rounded, "gx", -1)
+    following = passed_along(dense, "gx", -1)
     if fits and orbs % LANES == LANES // 2 and orbs % (4 * QUAD * QUAD) == 0:
         own, send, packed = first_turned(target, rounded, exchanged(pack(edge_tiles, 0, orbs)), rows)
         arrive = passed_along(send, "gx", 1)
@@ -393,22 +437,23 @@
         arrive = passed_along(send, "gx", 1)
     direct = direct_terms(target, rounded, following, own, owned, dot_nt)
     mirror = mirrored(owned, direct)
-    previous, current = trial_panel, direct + arrive.astype(jnp.float32)
-    rounded = current.astype(jnp.bfloat16)
+    previous = trial_panel
+    current, rounded, dense = updated(direct, arrive)
     for k in range(1, DEGREE):
-        following = passed_along(rounded, "gx", -1)
+        following = passed_along(dense, "gx", -1)
         own, send = turned_terms(target, rounded, owned)
         arrive = passed_along(send, "gx", 1)
         direct = direct_terms(target, rounded, following, own, mirror, dot_nn)
-        if k == DEGREE - 2:
-            rounded = rounded_update(direct, arrive, previous)
-            direct, arrive, previous, rounded = lax.optimization_barrier((direct, arrive, previous, rounded))
-        if k < DEGREE - 1:
-            total = 2.0 * (direct + arrive.astype(jnp.float32)) - previous
+        if k == DEGREE - 1:
+            total = final_update(direct, arrive, previous)
+        elif k == DEGREE - 2:
+            rounded, dense = updated(direct, arrive, previous, total=False)
+            direct, arrive, previous, rounded, dense = lax.optimization_barrier(
+                (direct, arrive, previous, rounded, dense)
+            )
+            (total,) = updated(direct, arrive, previous, rounded=False)
         else:
-            total = final_update(direct, arrive, previous)
-        if k < DEGREE - 2:
-            rounded = total.astype(jnp.bfloat16)
+            total, rounded, dense = updated(direct, arrive, previous)
         previous, current = current, total
     return previous, current
 

time: 176 us -> 176 us (level)
  transfers between devices with their start and end apart: 9 -> 9, of which waited for: 7 -> 7; matrix products, arithmetic and copies ran while one was open for 4% -> 3% of each run, Pallas kernels for 8% -> 10%
where the time goes in v7:
time: 176 us
  waiting for transfers between devices  130 us (74%)
  Pallas kernels  23.8 us (14%)
  starting transfers between devices  14.7 us (8%)
  matrix products  5.58 us (3%)
    all_to_all x1, waiting for transfers between devices, exchanged(): return lax.all_to_all(tiles, 'gx', split_axis=0, concat_axis=0, tiled=True)  90.6 us
    ppermute x8, waiting for transfers between devices, passed_along(): return lax.ppermute(value, axis, pairs)  39.4 us
    all_to_all x1, starting transfers between devices, exchanged(): return lax.all_to_all(tiles, 'gx', split_axis=0, concat_axis=0, tiled=True)  7.58 us
    ppermute x8, starting transfers between devices, passed_along(): return lax.ppermute(value, axis, pairs)  7.17 us
    dot_general x6, matrix products, spread(): wide = jnp.dot(repeated, place, preferred_element_type=jnp.float32)  5.58 us
    pallas_call x1, Pallas kernels, pack(): pl.pallas_call(functools.partial(pack_kernel, left, bounds), out_shape=ja...  5.48 us
    pallas_call x4, Pallas kernels, direct_terms(): pl.pallas_call(functools.partial(direct_kernel, product), out_shape=jax.S...  5.08 us
    pallas_call x1, Pallas kernels, first_turned(): pl.pallas_call(functools.partial(first_turned_kernel, rows * QUAD, bounds...  3.88 us
  transfers between devices with their start and end apart: 9, of which 7 were waited for; matrix products, arithmetic and copies ran while one was open for 3% of the time, Pallas kernels for 10%

profile of v7, /device:TPU:0, one launch (start us, length us, event | category | flops | bytes accessed | tf_op | source)
XLA Modules:
  0.0 175.6 jit_solution(1357497203951914911)
XLA Ops:
  0.6 5.5 %pack.1 = bf16[16,1352,128]{2,1,0:T(8,128)(2,1)} custom-call(bf16[52,64,832]{2,1,0:T(8,128)(2,1)} %bitcast.44), custom_call_target="tpu_custom_call" | custom-call | flops 1417674752 | bytes 11075584 | tf_op jit(solution)/shard_map/pack/pallas_call | solution.py:122
  6.1 7.6 %all-to-all-start = ((bf16[16,1352,128]{2,1,0:T(8,128)(2,1)}), bf16[16,1352,128]{2,1,0:T(8,128)(2,1)}, u32[]{:S(2)}, u32[]{:S(2)}) async-start(bf16[16,1352,128]{2,1,0:T(8,128)(2,1)} %pack.1), calls=%async_computation | async-start | bytes 11075584 | tf_op jit(solution)/shard_map/all_to_all | solution.py:414
  13.8 4.3 %collective-permute-start = (bf16[624,128]{1,0:T(8,128)(2,1)S(1)}, bf16[624,128]{1,0:T(8,128)(2,1)S(1)}, u32[]{:S(2)}, u32[]{:S(2)}) collective-permute-start(bf16[624,128]{1,0:T(8,128)(2,1)S(1)} %get-tuple-element.27), channel_id=1, source_target_pairs={{0,15},{1,0},{2,1},{3,2},{4,3},{5,4},{6,5},{7,6},{8,7},{9,8},{10,9... | collective-permute-start | bytes 479240 | tf_op jit(solution)/shard_map/ppermute | solution.py:22
  18.6 0.7 fusion.29.refs_5_
  19.3 0.7 fusion.28.refs_4_
  20.1 0.7 fusion.27.refs_2_
  20.8 0.7 fusion.26.refs_1_
  21.6 1.3 fusion.13.refs_3_
  22.9 1.3 fusion.12.refs_0_
  24.2 90.6 %all-to-all-done.from_ref = bf16[16,1352,128]{2,1,0:T(8,128)(2,1)} async-done(((bf16[16,1352,128]{2,1,0:T(8,128)(2,1)}), bf16[16,1352,128]{2,1,0:T(8,128)(2,1)}, u32[]{:S(2)}, u32[]{:S(2)}) %all-to-all-start) | async-done | bytes 5537824 | tf_op jit(solution)/shard_map/all_to_all | solution.py:414
  114.9 3.9 %first_turned.1 = (f32[2,48,832]{2,1,0:T(8,128)S(1)}, bf16[624,128]{1,0:T(8,128)(2,1)S(1)}, bf16[16,1352,128]{2,1,0:T(8,128)(2,1)S(1)}) custom-call(s32[8,128]{1,0:T(8,128)S(1)} %broadcast_in_dim.16.target_ref, bf16[16,1352,128]{2,1,0:T(8,128)(2,1)} %all-to-all-done.from_ref, bf16[192,1664]{1,0:T(8,128)(2,1)S(1)} %fusion.12.refs_0_, ...), custom_call_target="tpu_custom_call" | custom-call | flops 1063256064 | bytes 5537792 | tf_op jit(solution)/shard_map/first_turned/pallas_call | solution.py:259
  118.8 1.0 collective-permute-start.1
  119.8 1.8 %unpack.1.tiles_ref = bf16[4,832,832]{2,1,0:T(8,128)(2,1)S(1)} custom-call(bf16[16,1352,128]{2,1,0:T(8,128)(2,1)S(1)} %get-tuple-element.29.in_ref), custom_call_target="tpu_custom_call" | custom-call | flops 1417674752 | bytes 11075584 | tf_op jit(solution)/shard_map/unpack/pallas_call | solution.py:182
  121.6 1.8 %direct.4.first_ref.after_ref = f32[2,48,832]{2,1,0:T(8,128)S(1)} custom-call(s32[8,128]{1,0:T(8,128)S(1)} %broadcast_in_dim.16.target_ref, bf16[2,48,832]{2,1,0:T(8,128)(2,1)S(1)} %get-tuple-element.26.rounded_ref, bf16[624,128]{1,0:T(8,128)(2,1)S(1)} %collective-permute-done.following_ref, f32[2,48,832]{2,1,0:T(8,128)S(1)} %get-tuple-element.28.own_ref, ...), custom_call_target="tpu_custom_call" | custom-call | flops 1063256064 | bytes 5537792 | tf_op jit(solution)/shard_map/direct/pallas_call | solution.py:326
  123.5 23.8 %collective-permute-done.1.refs_0_ = bf16[624,128]{1,0:T(8,128)(2,1)S(1)} collective-permute-done((bf16[624,128]{1,0:T(8,128)(2,1)S(1)}, bf16[624,128]{1,0:T(8,128)(2,1)S(1)}, u32[]{:S(2)}, u32[]{:S(2)}) %collective-permute-start.1) | collective-permute-done | bytes 159776 | tf_op jit(solution)/shard_map/ppermute | solution.py:22
  147.4 0.7 collective-permute-start.2
  148.1 1.3 turned.3
  149.4 1.7 mirror.1.tiles_ref
  151.1 1.1 direct.5.first_ref
  152.2 4.7 %collective-permute-done.3.refs_0_ = bf16[624,128]{1,0:T(8,128)(2,1)S(1)} collective-permute-done((bf16[624,128]{1,0:T(8,128)(2,1)S(1)}, bf16[624,128]{1,0:T(8,128)(2,1)S(1)}, u32[]{:S(2)}, u32[]{:S(2)}) %collective-permute-start.3) | collective-permute-done | bytes 159776 | tf_op jit(solution)/shard_map/ppermute | solution.py:22
  157.1 1.3 turned.4
  158.3 0.5 collective-permute-start.5
  158.8 1.0 collective-permute-done.4.following_ref
  159.9 1.1 direct.6.first_ref
  161.0 4.8 %collective-permute-done.5.refs_0_ = bf16[624,128]{1,0:T(8,128)(2,1)S(1)} collective-permute-done((bf16[624,128]{1,0:T(8,128)(2,1)S(1)}, bf16[624,128]{1,0:T(8,128)(2,1)S(1)}, u32[]{:S(2)}, u32[]{:S(2)}) %collective-permute-start.5) | collective-permute-done | bytes 159776 | tf_op jit(solution)/shard_map/ppermute | solution.py:22
  166.0 1.3 turned.5
  167.2 0.5 collective-permute-start.7
  167.7 0.8 update.9
  168.6 0.2 collective-permute-done.6.following_ref
  168.8 1.1 direct.7.direct_ref
  169.9 4.8 %collective-permute-done.7.arrive_ref = bf16[624,128]{1,0:T(8,128)(2,1)S(1)} collective-permute-done((bf16[624,128]{1,0:T(8,128)(2,1)S(1)}, bf16[624,128]{1,0:T(8,128)(2,1)S(1)}, u32[]{:S(2)}, u32[]{:S(2)}) %collective-permute-start.7) | collective-permute-done | bytes 159776 | tf_op jit(solution)/shard_map/ppermute | solution.py:22
  174.7 0.8 final.1
  (27 shorter events, 1.1 us)
Async XLA Ops:
  6.1 7.6 %copy-start = (f32[2,48,832]{2,1,0:T(8,128)S(1)}, f32[2,48,832]{2,1,0:T(8,128)}, u32[]{:S(2)}) copy-start(f32[2,48,832]{2,1,0:T(8,128)} %refs_1_.1) | copy-start | bytes 958468
  6.1 12.0 %copy-start.1 = (s32[32,2]{0,1:T(2,128)S(1)}, s32[32,2]{0,1:T(2,128)}, u32[]{:S(2)}) copy-start(s32[32,2]{0,1:T(2,128)} %param.5) | copy-start | bytes 772
  6.1 108.7 %all-to-all-start = ((bf16[16,1352,128]{2,1,0:T(8,128)(2,1)}), bf16[16,1352,128]{2,1,0:T(8,128)(2,1)}, u32[]{:S(2)}, u32[]{:S(2)}) async-start(bf16[16,1352,128]{2,1,0:T(8,128)(2,1)} %pack.1), calls=%async_computation | async-start | bytes 11075584 | tf_op jit(solution)/shard_map/all_to_all | solution.py:414
  13.8 107.8 %collective-permute-start = (bf16[624,128]{1,0:T(8,128)(2,1)S(1)}, bf16[624,128]{1,0:T(8,128)(2,1)S(1)}, u32[]{:S(2)}, u32[]{:S(2)}) collective-permute-start(bf16[624,128]{1,0:T(8,128)(2,1)S(1)} %get-tuple-element.27), channel_id=1, source_target_pairs={{0,15},{1,0},{2,1},{3,2},{4,3},{5,4},{6,5},{7,6},{8,7},{9,8},{10,9... | collective-permute-start | bytes 479240 | tf_op jit(solution)/shard_map/ppermute | solution.py:22
  118.8 28.4 %collective-permute-start.1 = (bf16[624,128]{1,0:T(8,128)(2,1)S(1)}, bf16[624,128]{1,0:T(8,128)(2,1)S(1)}, u32[]{:S(2)}, u32[]{:S(2)}) collective-permute-start(bf16[624,128]{1,0:T(8,128)(2,1)S(1)} %get-tuple-element.30), channel_id=1, source_target_pairs={{0,1},{1,2},{2,3},{3,4},{4,5},{5,6},{6,7},{7,8},{8,9},{9,10},{10,1... | collective-permute-start | bytes 479240 | tf_op jit(solution)/shard_map/ppermute | solution.py:22
  147.4 3.7 %collective-permute-start.2 = (bf16[624,128]{1,0:T(8,128)(2,1)S(1)}, bf16[624,128]{1,0:T(8,128)(2,1)S(1)}, u32[]{:S(2)}, u32[]{:S(2)}) collective-permute-start(bf16[624,128]{1,0:T(8,128)(2,1)S(1)} %get-tuple-element.32), channel_id=1, source_target_pairs={{0,15},{1,0},{2,1},{3,2},{4,3},{5,4},{6,5},{7,6},{8,7},{9,8},{10,9... | collective-permute-start | bytes 479240 | tf_op jit(solution)/shard_map/ppermute | solution.py:22
  149.4 7.5 %collective-permute-start.3 = (bf16[624,128]{1,0:T(8,128)(2,1)S(1)}, bf16[624,128]{1,0:T(8,128)(2,1)S(1)}, u32[]{:S(2)}, u32[]{:S(2)}) collective-permute-start(bf16[624,128]{1,0:T(8,128)(2,1)S(1)} %get-tuple-element.34), channel_id=1, source_target_pairs={{0,1},{1,2},{2,3},{3,4},{4,5},{5,6},{6,7},{7,8},{8,9},{9,10},{10,1... | collective-permute-start | bytes 479240 | tf_op jit(solution)/shard_map/ppermute | solution.py:22
  157.0 2.9 %collective-permute-start.4 = (bf16[624,128]{1,0:T(8,128)(2,1)S(1)}, bf16[624,128]{1,0:T(8,128)(2,1)S(1)}, u32[]{:S(2)}, u32[]{:S(2)}) collective-permute-start(bf16[624,128]{1,0:T(8,128)(2,1)S(1)} %get-tuple-element.36), channel_id=1, source_target_pairs={{0,15},{1,0},{2,1},{3,2},{4,3},{5,4},{6,5},{7,6},{8,7},{9,8},{10,9... | collective-permute-start | bytes 479240 | tf_op jit(solution)/shard_map/ppermute | solution.py:22
  158.3 7.5 %collective-permute-start.5 = (bf16[624,128]{1,0:T(8,128)(2,1)S(1)}, bf16[624,128]{1,0:T(8,128)(2,1)S(1)}, u32[]{:S(2)}, u32[]{:S(2)}) collective-permute-start(bf16[624,128]{1,0:T(8,128)(2,1)S(1)} %get-tuple-element.38), channel_id=1, source_target_pairs={{0,1},{1,2},{2,3},{3,4},{4,5},{5,6},{6,7},{7,8},{8,9},{9,10},{10,1... | collective-permute-start | bytes 479240 | tf_op jit(solution)/shard_map/ppermute | solution.py:22
  166.0 2.8 %collective-permute-start.6 = (bf16[624,128]{1,0:T(8,128)(2,1)S(1)}, bf16[624,128]{1,0:T(8,128)(2,1)S(1)}, u32[]{:S(2)}, u32[]{:S(2)}) collective-permute-start(bf16[624,128]{1,0:T(8,128)(2,1)S(1)} %get-tuple-element.46), channel_id=1, source_target_pairs={{0,15},{1,0},{2,1},{3,2},{4,3},{5,4},{6,5},{7,6},{8,7},{9,8},{10,9... | collective-permute-start | bytes 479240 | tf_op jit(solution)/shard_map/ppermute | solution.py:22
  167.2 7.4 %collective-permute-start.7 = (bf16[624,128]{1,0:T(8,128)(2,1)S(1)}, bf16[624,128]{1,0:T(8,128)(2,1)S(1)}, u32[]{:S(2)}, u32[]{:S(2)}) collective-permute-start(bf16[624,128]{1,0:T(8,128)(2,1)S(1)} %get-tuple-element.48), channel_id=1, source_target_pairs={{0,1},{1,2},{2,3},{3,4},{4,5},{5,6},{6,7},{7,8},{8,9},{9,10},{10,1... | collective-permute-start | bytes 479240 | tf_op jit(solution)/shard_map/ppermute | solution.py:22
